TPU v7x, 32 devices: a whole 2x2x4 slice. The times are simulated.
32 devices in a mesh: ens: 2 (over x), gx: 16 (over z, y, core).
Axes of the slice: x: 2, y: 2, z: 4, core: 2. Of those that a mesh axis runs over, the one named last changes fastest.
Arguments:
- rhs_pressure: float32 [256, 128, 128], P(('ens', 'gx')), parts along dimension 0, may hold values from -6 to 6
- rhs_saturation: float32 [256, 128, 128], P(('ens', 'gx')), parts along dimension 0, may hold values from -6 to 6
- trans_x: float32 [256, 128, 128], P(('ens', 'gx')), parts along dimension 0, may hold values from 0.05 to 2
- trans_y: float32 [256, 128, 128], P(('ens', 'gx')), parts along dimension 0, may hold values from 0.05 to 2
- trans_z: float32 [256, 128, 128], P(('ens', 'gx')), parts along dimension 0, may hold values from 0.05 to 2
- coupling: float32 [256, 128, 128], P(('ens', 'gx')), parts along dimension 0, may hold values from -4 to 4
- upwind: float32 [256, 128, 128], P(('ens', 'gx')), parts along dimension 0, may hold values from -5 to 5
- storage: float32 [256, 128, 128], P(('ens', 'gx')), parts along dimension 0, may hold values from 0.3 to 3
- cross: float32 [256, 128, 128], P(('ens', 'gx')), parts along dimension 0, may hold values from -4 to 4
- accel: float32 [256, 128, 128], P(('ens', 'gx')), parts along dimension 0, may hold values from 1.15 to 3
- perf_cell: int32 [8192], P(('ens', 'gx')), parts along dimension 0, may hold values from 0 to 131071, as said below
- perf_well: int32 [8192], P(('ens', 'gx')), parts along dimension 0, may hold values from 0 to 511, as said below
- perf_index: float32 [8192], P(('ens', 'gx')), parts along dimension 0, may hold values from 0.1 to 2
- well_rhs: float32 [1024], P('ens'), parts along dimension 0, may hold values from -6 to 6
- well_slot: int32 [1024], P('ens'), parts along dimension 0, may hold values from 0 to 511, each once
Outputs:
- adj_pressure: float32 [256, 128, 128], P(('ens', 'gx')), parts along dimension 0
- adj_saturation: float32 [256, 128, 128], P(('ens', 'gx')), parts along dimension 0
- control_grad: float32 [1024], P(('ens', 'gx')), parts along dimension 0
There are 2 independent parts, one for each index of `ens`. A program takes and returns all parts, laid end to end along the dimension named above; each array names one. Nothing has to cross between parts.
Inputs may be any that keep to these rules, and one draw needn't show every extreme that they name: `perf_cell`: flat index within the brick: x within the brick times 128 * 128, plus y * 128, plus z. Each device's perforations come in 32 groups of 8 consecutive entries, one well's path each: consecutive cells along z at one (x, y), or cells along x through the brick's planes. `perf_well`: group g of device j belongs to well j * 32 + g, or, for wells that run along x across a brick face, to well (j - 1) * 32 + g; a well has perforations on at most two neighbouring devices, and some wells have none. `well_slot`: each slot once; slots j * 32 to (j + 1) * 32 - 1 belong to device j of gx.
All inputs are finite; a program needn't handle non-finite values.
Results may differ from a plain program's by a relative error of at most 0.00002.
Values sent between devices are 32-bit elements; how exact they have to be, the bound alone decides.
No kernel may reach another device: no remote copies, remote signals or barrier semaphores. Data moves between devices by JAX's collectives and lax.ppermute only.
A program may use at most 64 MiB of HBM per device.

v0:
```python
import functools

import jax
import jax.numpy as jnp
from jax import lax
from jax.experimental import pallas as pl
from jax.experimental.pallas import tpu as pltpu
from jax.sharding import PartitionSpec as P

SWEEPS = 6
SUB = 8
LANES = 128
F32 = jnp.float32


def vmem(rows):
    return pltpu.VMEM((rows, LANES), F32)


def placed(array, space):
    return array if space is pltpu.SMEM else pltpu.with_memory_space_constraint(array, space)


def spec(space):
    return pl.BlockSpec(memory_space=space)


def iota(shape, dim):
    return lax.broadcasted_iota(jnp.int32, shape, dim)


def lane_sum(block):
    return jnp.sum(block, axis=1, keepdims=True)


def spread(column, groups):
    return jnp.broadcast_to(column, (groups, LANES))


def row_of(column, groups):
    mine = iota((groups, LANES), 0) == iota((groups, LANES), 1)
    return jnp.sum(jnp.where(mine, column, 0.0), axis=0, keepdims=True)


def column_of(row, groups):
    mine = iota((groups, LANES), 0) == iota((groups, LANES), 1)
    return spread(lane_sum(jnp.where(mine, jnp.broadcast_to(row, (groups, LANES)), 0.0)), groups)


def well_block(part_own, part_before, groups):
    sub = iota((SUB, LANES), 0)
    own = jnp.broadcast_to(row_of(part_own, groups), (SUB, LANES))
    before = jnp.broadcast_to(row_of(part_before, groups), (SUB, LANES))
    return jnp.where(sub == 0, own, jnp.where(sub == 1, before, 0.0))


def group_rows(ref, groups, run):
    per_row = LANES // run
    return jnp.concatenate(
        [jnp.broadcast_to(ref[i : i + 1, :], (per_row, LANES)) for i in range(groups // per_row)], axis=0
    )


def first_kernel(sizes, tx_hbm, well_ref, index_ref, send_ref, wells_ref, sem):
    ny, groups, run = sizes.ny, sizes.groups, sizes.run
    copy = pltpu.make_async_copy(
        tx_hbm.at[pl.ds((sizes.planes - 1) * ny, ny)], send_ref.at[pl.ds(0, ny)], sem
    )
    copy.start()
    place = lax.axis_index("gx")
    shape = (groups, LANES)
    per_row = LANES // run
    local = iota(shape, 0) % per_row
    lane = iota(shape, 1)
    weights = jnp.where(lane // run == local, group_rows(index_ref, groups, run), 0.0)
    total = lane_sum(weights)
    first = jnp.where(lane == local * run, group_rows(well_ref, groups, run).astype(F32), 0.0)
    well = lane_sum(first)
    before = well < (place * groups).astype(F32)
    before = spread(jnp.where(before, 1.0, 0.0), groups)
    total = spread(total, groups)
    wells_ref[0:groups, :] = before
    wells_ref[groups : 2 * groups, :] = total
    send_ref[ny : ny + SUB, :] = well_block(total * (1.0 - before), total * before, groups)
    copy.wait()


def setup_kernel(
    sizes,
    cell_ref,
    index_ref,
    tx_hbm,
    ty_hbm,
    tz_hbm,
    accel_hbm,
    coupling_hbm,
    upwind_hbm,
    storage_hbm,
    rhs_p_hbm,
    rhs_s_hbm,
    cross_hbm,
    tx_ref,
    ty_ref,
    tyl_ref,
    tz_ref,
    tzl_ref,
    rp_ref,
    ip_ref,
    cc_ref,
    rs_ref,
    uu_ref,
    xx_ref,
    extra_ref,
    weight_ref,
    raw_ty,
    raw_storage,
    cwi_ref,
    sems,
):
    ny, planes, groups, run = sizes.ny, sizes.planes, sizes.groups, sizes.run
    rows = planes * ny
    moves = [
        (tx_hbm, tx_ref),
        (ty_hbm, raw_ty.at[pl.ds(SUB, rows)]),
        (tz_hbm, tz_ref),
        (accel_hbm, ip_ref),
        (coupling_hbm, cc_ref),
        (upwind_hbm, uu_ref),
        (storage_hbm, raw_storage),
        (rhs_p_hbm, rp_ref),
        (rhs_s_hbm, rs_ref),
        (cross_hbm, xx_ref),
    ]
    copies = [pltpu.make_async_copy(src, dst, sems.at[i]) for i, (src, dst) in enumerate(moves)]
    for copy in copies:
        copy.start()

    last = lax.axis_index("gx") == lax.axis_size("gx") - 1
    keep_last = jnp.where(last, 0.0, 1.0)
    zero = jnp.zeros((SUB, LANES), F32)

    @pl.loop(0, rows // SUB, unroll=8)
    def _(i):
        cwi_ref[pl.ds(pl.multiple_of(i * SUB, SUB), SUB), :] = zero

    spot = iota((SUB, LANES), 0) * LANES + iota((SUB, LANES), 1)
    for g in range(groups):
        weight = zero
        for k in range(g * run, (g + 1) * run):
            cell = cell_ref[k]
            at = (cell // (ny * LANES)) * LANES + cell % LANES
            weight = weight + jnp.where(spot == at, index_ref[k], 0.0)
        weight_ref[g * SUB : (g + 1) * SUB, :] = weight
        slab = pl.ds((cell_ref[g * run] // LANES) % ny, planes, ny)
        cwi_ref[slab, :] = cwi_ref[slab, :] + weight

    for copy in copies:
        copy.wait()

    lane = iota((SUB, LANES), 1)
    sub = iota((SUB, LANES), 0)

    @pl.loop(0, ny // SUB)
    def _(r):
        y0 = pl.multiple_of(r * SUB, SUB)
        ypos = sub + y0
        txl = None
        for x in range(planes):
            at = pl.ds(y0 + x * ny, SUB)
            tx = tx_ref[at, :]
            if x == planes - 1:
                tx = tx * keep_last
                tx_ref[at, :] = tx
            ty = jnp.where(ypos == ny - 1, 0.0, raw_ty[pl.ds(y0 + (x * ny + SUB), SUB), :])
            tyl = jnp.where(ypos == 0, 0.0, raw_ty[pl.ds(y0 + (x * ny + SUB - 1), SUB), :])
            tz = jnp.where(lane == LANES - 1, 0.0, tz_ref[at, :])
            tzl = pltpu.roll(tz, 1, 1)
            ty_ref[at, :] = ty
            tyl_ref[at, :] = tyl
            tz_ref[at, :] = tz
            tzl_ref[at, :] = tzl
            tsum = tx + ty + tyl + tz + tzl
            if x > 0:
                tsum = tsum + txl
            accel = ip_ref[at, :]
            coupling = cc_ref[at, :]
            upwind = uu_ref[at, :]
            to_p = accel * (1.0 + jnp.abs(coupling))
            to_s = accel * jnp.abs(upwind)
            dp = to_p * tsum + accel * cwi_ref[at, :]
            ds = to_s * tsum + raw_storage[at, :]
            if x == 0:
                here = pl.ds(y0, SUB)
                extra_ref[here, :] = to_p
                extra_ref[pl.ds(y0 + ny, SUB), :] = to_s
                extra_ref[pl.ds(y0 + 2 * ny, SUB), :] = ds
                ip_ref[at, :] = dp
            else:
                ip = 1.0 / dp
                is_ = 1.0 / ds
                ip_ref[at, :] = ip
                cc_ref[at, :] = coupling * ip
                rp_ref[at, :] = rp_ref[at, :] * ip
                rs_ref[at, :] = rs_ref[at, :] * is_
                uu_ref[at, :] = upwind * is_
                xx_ref[at, :] = xx_ref[at, :] * is_
            txl = tx


def add_wells(sizes, cell_ref, mu_ref, wp_ref, ws_ref, p_ref, s_ref):
    for g in range(sizes.groups):
        slab = pl.ds((cell_ref[g * sizes.run] // LANES) % sizes.ny + SUB, sizes.planes, sizes.ny)
        at = pl.ds(g * SUB, SUB)
        mu = mu_ref[g : g + 1, :]
        p_ref[slab, :] = p_ref[slab, :] + mu * wp_ref[at, :]
        s_ref[slab, :] = s_ref[slab, :] - mu * ws_ref[at, :]


def path_sums(sizes, cell_ref, weight_ref, p_ref, parts_ref):
    for g in range(sizes.groups):
        slab = pl.ds((cell_ref[g * sizes.run] // LANES) % sizes.ny + SUB, sizes.planes, sizes.ny)
        parts_ref[g : g + 1, :] = jnp.sum(
            p_ref[slab, :] * weight_ref[g * SUB : (g + 1) * SUB, :], axis=0, keepdims=True
        )
    return spread(lane_sum(parts_ref[...]), sizes.groups)


def pack(sizes, even, p_ref, s_ref, send_e, send_o, wells):
    ny = sizes.ny
    top = (sizes.planes - 1) * ny
    from_e = pl.multiple_of(jnp.where(even, top, 0) + SUB, SUB)
    from_o = pl.multiple_of(jnp.where(even, 0, top) + SUB, SUB)
    for r in range(0, ny, SUB):
        for send, start in ((send_e, from_e), (send_o, from_o)):
            send[r : r + SUB, :] = p_ref[pl.ds(start + r, SUB), :]
            send[ny + r : ny + r + SUB, :] = s_ref[pl.ds(start + r, SUB), :]
    send_e[2 * ny : 2 * ny + SUB, :] = wells
    send_o[2 * ny : 2 * ny + SUB, :] = wells


def own_lanes(ref, place, groups):
    shape = (groups, LANES)
    start = place * groups
    row = jnp.broadcast_to(ref[pl.ds(start // LANES, 1), :].astype(F32), shape)
    mine = iota(shape, 1) == iota(shape, 0) + start % LANES
    return spread(lane_sum(jnp.where(mine, row, 0.0)), groups)


BEFORE, RHS_OWN, INV_OWN, SUM_OWN, RHS, INV, SLOT_OWN, SLOT_BEFORE, TABLE = range(9)


def start_kernel(
    sizes,
    cell_ref,
    from_e,
    from_o,
    wells_ref,
    rhs_ref,
    slot_ref,
    rp_ref,
    ip_ref,
    cc_ref,
    rs_ref,
    uu_ref,
    xx_ref,
    extra_ref,
    weight_ref,
    p_ref,
    s_ref,
    edge_ref,
    wp_ref,
    ws_ref,
    table_ref,
    parts_out,
    send_e,
    send_o,
    mu_ref,
    parts_ref,
):
    ny, planes, groups = sizes.ny, sizes.planes, sizes.groups
    rows = planes * ny
    place = lax.axis_index("gx")
    even = place % 2 == 0

    tile_e, tile_o = from_e[ny : ny + SUB, :], from_o[ny : ny + SUB, :]
    low = jnp.where(even, tile_o, tile_e)
    high = jnp.where(even, tile_e, tile_o)
    before = wells_ref[0:groups, :]
    mine = wells_ref[groups : 2 * groups, :]
    is_before = before > 0.5
    sum_own = mine * (1.0 - before) + column_of(high[1:2, :], groups)
    sum_before = mine * before + column_of(low[0:1, :], groups)
    rhs_own = own_lanes(rhs_ref, place, groups)
    rhs_before = own_lanes(rhs_ref, jnp.maximum(place - 1, 0), groups)
    inv_own = 1.0 / (1.5 * sum_own + 0.5)
    inv_before = 1.0 / (1.5 * sum_before + 0.5)
    rhs = jnp.where(is_before, rhs_before, rhs_own)
    inv = jnp.where(is_before, inv_before, inv_own)
    entries = {
        BEFORE: before,
        RHS_OWN: rhs_own,
        INV_OWN: inv_own,
        SUM_OWN: sum_own,
        RHS: rhs,
        INV: inv,
        SLOT_OWN: own_lanes(slot_ref, place, groups),
        SLOT_BEFORE: own_lanes(slot_ref, jnp.maximum(place - 1, 0), groups),
    }
    for i, entry in entries.items():
        table_ref[i * groups : (i + 1) * groups, :] = entry
    mu_ref[...] = rhs * inv

    @pl.loop(0, ny // SUB)
    def _(r):
        y0 = pl.multiple_of(r * SUB, SUB)
        at = pl.ds(y0, SUB)
        txl = jnp.where(even, from_o[at, :], from_e[at, :])
        ip = 1.0 / (ip_ref[at, :] + extra_ref[at, :] * txl)
        is_ = 1.0 / (extra_ref[pl.ds(y0 + 2 * ny, SUB), :] + extra_ref[pl.ds(y0 + ny, SUB), :] * txl)
        rp, rs, xx = rp_ref[at, :] * ip, rs_ref[at, :] * is_, xx_ref[at, :] * is_
        plane = [txl, ip, cc_ref[at, :] * ip, rp, rs, uu_ref[at, :] * is_, xx]
        for i, value in enumerate(plane):
            edge_ref[pl.ds(y0 + i * ny, SUB), :] = value
        p_ref[pl.ds(y0 + SUB, SUB), :] = rp
        s_ref[pl.ds(y0 + SUB, SUB), :] = rs - xx * rp
        for x in range(1, planes):
            at = pl.ds(y0 + x * ny, SUB)
            to = pl.ds(y0 + (x * ny + SUB), SUB)
            rp = rp_ref[at, :]
            p_ref[to, :] = rp
            s_ref[to, :] = rs_ref[at, :] - xx_ref[at, :] * rp

    clear_ends(rows, p_ref, s_ref)
    sub = iota((SUB, LANES), 0)
    for g in range(groups):
        y = (cell_ref[g * sizes.run] // LANES) % ny
        at = pl.ds(g * SUB, SUB)
        slab = pl.ds(y, planes, ny)
        ip = jnp.where(sub == 0, edge_ref[pl.ds(y + ny, 1), :], ip_ref[slab, :])
        xx = jnp.where(sub == 0, edge_ref[pl.ds(y + 6 * ny, 1), :], xx_ref[slab, :])
        wp = weight_ref[at, :] * ip
        wp_ref[at, :] = wp
        ws_ref[at, :] = wp * xx
    add_wells(sizes, cell_ref, mu_ref, wp_ref, ws_ref, p_ref, s_ref)
    total = path_sums(sizes, cell_ref, weight_ref, p_ref, parts_ref)
    part_own, part_before = total * (1.0 - before), total * before
    parts_out[0:groups, :] = part_own
    parts_out[groups : 2 * groups, :] = part_before
    pack(sizes, even, p_ref, s_ref, send_e, send_o, well_block(part_own, part_before, groups))


def clear_ends(rows, *refs):
    zero = jnp.zeros((SUB, LANES), F32)
    for ref in refs:
        ref[0:SUB, :] = zero
        ref[rows + SUB : rows + 2 * SUB, :] = zero


def sweep_kernel(
    sizes,
    final,
    cell_ref,
    from_e,
    from_o,
    p_old,
    s_old,
    parts_in,
    tx_ref,
    ty_ref,
    tyl_ref,
    tz_ref,
    tzl_ref,
    rp_ref,
    ip_ref,
    cc_ref,
    rs_ref,
    uu_ref,
    xx_ref,
    edge_ref,
    weight_ref,
    wp_ref,
    ws_ref,
    table_ref,
    p_ref,
    s_ref,
    *rest,
):
    ny, planes, groups = sizes.ny, sizes.planes, sizes.groups
    rows = planes * ny
    if final:
        grads_ref, mu_ref, parts_ref = rest
    else:
        parts_out, send_e, send_o, mu_ref, parts_ref = rest
    place = lax.axis_index("gx")
    even = place % 2 == 0

    def table(i):
        return table_ref[i * groups : (i + 1) * groups, :]

    tile_e, tile_o = from_e[2 * ny : 2 * ny + SUB, :], from_o[2 * ny : 2 * ny + SUB, :]
    low = jnp.where(even, tile_o, tile_e)
    high = jnp.where(even, tile_e, tile_o)
    before = table(BEFORE)
    total_own = parts_in[0:groups, :] + column_of(high[1:2, :], groups)
    total_before = parts_in[groups : 2 * groups, :] + column_of(low[0:1, :], groups)
    mu_ref[...] = (table(RHS) + jnp.where(before > 0.5, total_before, total_own)) * table(INV)

    @pl.loop(0, ny // SUB)
    def _(r):
        y0 = pl.multiple_of(r * SUB, SUB)
        at = pl.ds(y0, SUB)
        at_s = pl.ds(y0 + ny, SUB)
        p_e, p_o, s_e, s_o = from_e[at, :], from_o[at, :], from_e[at_s, :], from_o[at_s, :]
        ps = [jnp.where(even, p_o, p_e)]
        ss = [jnp.where(even, s_o, s_e)]
        for x in range(planes):
            here = pl.ds(y0 + (x * ny + SUB), SUB)
            ps.append(p_old[here, :])
            ss.append(s_old[here, :])
        ps.append(jnp.where(even, p_e, p_o))
        ss.append(jnp.where(even, s_e, s_o))

        def edge(i):
            return edge_ref[pl.ds(y0 + i * ny, SUB), :]

        txl = edge(0)
        for x in range(planes):
            at = pl.ds(y0 + x * ny, SUB)
            up = pl.ds(y0 + (x * ny + SUB + 1), SUB)
            down = pl.ds(y0 + (x * ny + SUB - 1), SUB)
            tx, ty, tyl, tz, tzl = tx_ref[at, :], ty_ref[at, :], tyl_ref[at, :], tz_ref[at, :], tzl_ref[at, :]

            def neighbours(fields, old):
                mid = fields[x + 1]
                total = tx * fields[x + 2] + txl * fields[x]
                total = total + (ty * old[up, :] + tyl * old[down, :])
                return total + (tz * pltpu.roll(mid, LANES - 1, 1) + tzl * pltpu.roll(mid, 1, 1))

            sum_p = neighbours(ps, p_old)
            sum_s = neighbours(ss, s_old)
            if x == 0:
                ip, cc, rp, rs, uu, xx = [edge(i) for i in range(1, 7)]
            else:
                ip, cc, rp, rs, uu, xx = [ref[at, :] for ref in (ip_ref, cc_ref, rp_ref, rs_ref, uu_ref, xx_ref)]
            p = rp + ip * sum_p + cc * sum_s
            to = pl.ds(y0 + (x * ny + SUB), SUB)
            p_ref[to, :] = p
            s_ref[to, :] = rs + uu * sum_s - xx * p
            txl = tx

    add_wells(sizes, cell_ref, mu_ref, wp_ref, ws_ref, p_ref, s_ref)
    total = path_sums(sizes, cell_ref, weight_ref, p_ref, parts_ref)
    part_own, part_before = total * (1.0 - before), total * before
    clear_ends(rows, p_ref, s_ref)
    if not final:
        parts_out[0:groups, :] = part_own
        parts_out[groups : 2 * groups, :] = part_before
        pack(sizes, even, p_ref, s_ref, send_e, send_o, well_block(part_own, part_before, groups))
        return
    mu_own = (table(RHS_OWN) + total_own) * table(INV_OWN)
    grad_own = mu_own * table(SUM_OWN) - part_own
    grad_before = -part_before
    lane = iota((groups, LANES), 1)
    slot_own, slot_before = table(SLOT_OWN), table(SLOT_BEFORE)
    inside = lane < groups
    for d in range(sizes.devices):
        want = (lane + d * groups).astype(F32)
        own = jnp.where(inside & (slot_own == want), grad_own, 0.0)
        other = jnp.where(inside & (slot_before == want), grad_before, 0.0)
        row = jnp.sum(own + other, axis=0, keepdims=True)
        grads_ref[d * SUB : (d + 1) * SUB, :] = jnp.where(
            iota((SUB, LANES), 0) == 0, jnp.broadcast_to(row, (SUB, LANES)), 0.0
        )


class Sizes:
    def __init__(self, planes, ny, groups, run, devices):
        self.planes, self.ny, self.groups, self.run, self.devices = planes, ny, groups, run, devices


def body(
    rhs_pressure,
    rhs_saturation,
    trans_x,
    trans_y,
    trans_z,
    coupling,
    upwind,
    storage,
    cross,
    accel,
    perf_cell,
    perf_well,
    perf_index,
    well_rhs,
    well_slot,
):
    planes, ny, nz = trans_x.shape
    devices = lax.axis_size("gx")
    groups = well_rhs.shape[0] // devices
    run = perf_cell.shape[0] // groups
    sizes = Sizes(planes, ny, groups, run, devices)
    rows = planes * ny
    padded = rows + 2 * SUB
    SMEM, VMEM, HBM = pltpu.SMEM, pltpu.VMEM, pltpu.HBM

    def flat(array):
        return array.reshape(rows, nz)

    def lines(array):
        return array.reshape(-1, LANES)

    def call(kernel, args, spaces, outs, scratch, name, micros):
        return pl.pallas_call(
            functools.partial(kernel),
            in_specs=[spec(space) for space in spaces],
            out_specs=[spec(VMEM)] * len(outs),
            out_shape=outs,
            scratch_shapes=scratch,
            compiler_params=pltpu.CompilerParams(vmem_limit_bytes=16 * 1024 * 1024),
            cost_estimate=pl.CostEstimate(flops=int(micros * 4e6), bytes_accessed=int(micros * 3e6), transcendentals=0),
            name=name,
        )(*[placed(a, space) for a, space in zip(args, spaces)])

    pairs_e = [(i, i ^ 1) for i in range(devices) if i ^ 1 < devices]
    pairs_o = []
    for i in range(1, devices - 1, 2):
        pairs_o += [(i, i + 1), (i + 1, i)]

    def exchange(send_e, send_o):
        return lax.ppermute(send_e, "gx", pairs_e), lax.ppermute(send_o, "gx", pairs_o)

    tx = flat(trans_x)
    send, wells = call(
        functools.partial(first_kernel, sizes),
        [tx, lines(perf_well), lines(perf_index)],
        [HBM, VMEM, VMEM],
        [vmem(ny + SUB), vmem(2 * groups)],
        [pltpu.SemaphoreType.DMA],
        "first",
        1,
    )
    from_e, from_o = exchange(send, send)
    big = [tx] + [
        flat(a)
        for a in (trans_y, trans_z, accel, coupling, upwind, storage, rhs_pressure, rhs_saturation, cross)
    ]
    made = call(
        functools.partial(setup_kernel, sizes),
        [perf_cell, perf_index] + big,
        [SMEM, SMEM] + [HBM] * len(big),
        [vmem(rows)] * 11 + [vmem(3 * ny), vmem(groups * SUB)],
        [VMEM((padded, LANES), F32), VMEM((rows, LANES), F32), VMEM((rows, LANES), F32), pltpu.SemaphoreType.DMA((10,))],
        "setup",
        4,
    )
    coefficients, (extra, weight) = list(made[:11]), made[11:]
    scratch = [VMEM((groups, LANES), F32), VMEM((groups, LANES), F32)]
    fields = [vmem(padded), vmem(padded)]
    sends = [vmem(2 * groups), vmem(2 * ny + SUB), vmem(2 * ny + SUB)]
    p, s, edge, wp, ws, table, parts, send_e, send_o = call(
        functools.partial(start_kernel, sizes),
        [perf_cell, from_e, from_o, wells, lines(well_rhs), lines(well_slot)] + coefficients[5:] + [extra, weight],
        [SMEM] + [VMEM] * 13,
        fields + [vmem(7 * ny), vmem(groups * SUB), vmem(groups * SUB), vmem(TABLE * groups)] + sends,
        scratch,
        "start",
        1,
    )
    for sweep in range(1, SWEEPS):
        final = sweep == SWEEPS - 1
        from_e, from_o = exchange(send_e, send_o)
        args = [perf_cell, from_e, from_o, p, s, parts] + coefficients + [edge, weight, wp, ws, table]
        p, s, *rest = call(
            functools.partial(sweep_kernel, sizes, final),
            args,
            [SMEM] + [VMEM] * (len(args) - 1),
            fields + ([vmem(devices * SUB)] if final else sends),
            scratch,
            "sweep",
            1,
        )
        if not final:
            parts, send_e, send_o = rest
    grads = lax.all_to_all(rest[0].reshape(devices, SUB, LANES), "gx", 0, 0)
    control = jnp.sum(grads, axis=(0, 1))[:groups]
    shape = trans_x.shape
    return p[SUB : SUB + rows].reshape(shape), s[SUB : SUB + rows].reshape(shape), control


def solution(mesh):
    grid = P(("ens", "gx"), None, None)
    line = P(("ens", "gx"))
    return jax.shard_map(
        body,
        mesh=mesh,
        in_specs=(grid,) * 10 + (line,) * 3 + (P("ens"), P("ens")),
        out_specs=(grid, grid, line),
        check_vma=False,
    )
```

profile of v0, /device:TPU:0, one launch (start us, length us, event | category | flops | bytes accessed | tf_op | source)
XLA Modules:
  0.0 84.5 jit_solution(12646827144793184226)
XLA Ops:
  0.6 0.0 copy-start.4
  0.6 0.0 copy-start.1
  0.7 0.7 copy-done.4
  1.3 0.0 copy-done.1
  1.3 0.8 %first.1 = (f32[136,128]{1,0:T(8,128)S(1)}, f32[64,128]{1,0:T(8,128)S(1)}) custom-call(f32[1024,128]{1,0:T(8,128)} %bitcast.22, s32[2,128]{1,0:T(2,128)S(1)} %bitcast.21, f32[2,128]{1,0:T(2,128)S(1)} %bitcast.18), custom_call_target="tpu_custom_call" | custom-call | flops 4000000 | bytes 3000000 | tf_op jit(solution)/shard_map/first/pallas_call | solution.py:514
  2.2 0.7 collective-permute-start.1
  2.9 4.4 %collective-permute-start = (f32[136,128]{1,0:T(8,128)S(1)}, f32[136,128]{1,0:T(8,128)S(1)}, u32[]{:S(2)}, u32[]{:S(2)}) collective-permute-start(f32[136,128]{1,0:T(8,128)S(1)} %get-tuple-element.50), channel_id=1, source_target_pairs={{0,1},{1,0},{2,3},{3,2},{4,5},{5,4},{6,7},{7,6},{8,9},{9,8},{10,11... | collective-permute-start | bytes 208904 | tf_op jit(solution)/shard_map/ppermute | solution.py:531
  7.2 0.0 copy-start
  7.2 0.7 copy-done
  7.9 4.8 %setup.1 = (f32[1024,128]{1,0:T(8,128)S(1)}, f32[1024,128]{1,0:T(8,128)S(1)}, f32[1024,128]{1,0:T(8,128)S(1)}, f32[1024,128]{1,0:T(8,128)S(1)}, f32[1024,128]{1,...) custom-call(s32[256]{0:T(256)S(1)} %copy-done, ...), custom_call_target="tpu_custom_call" | custom-call | flops 16000000 | bytes 12000000 | tf_op jit(solution)/shard_map/setup/pallas_call | solution.py:514
  12.7 0.0 collective-permute-done.1.from_o
  12.8 0.0 collective-permute-done.from_e
  12.8 0.0 copy-start.3
  12.8 0.0 copy-start.2
  12.8 0.7 copy-done.3
  13.4 0.0 copy-done.2
  13.5 2.2 %start.1 = (f32[1040,128]{1,0:T(8,128)S(1)}, f32[1040,128]{1,0:T(8,128)S(1)}, f32[896,128]{1,0:T(8,128)S(1)}, f32[256,128]{1,0:T(8,128)S(1)}, f32[256,128]{1,0:T...) custom-call(s32[256]{0:T(256)S(1)} %copy-done, ...), custom_call_target="tpu_custom_call" | custom-call | flops 4000000 | bytes 3000000 | tf_op jit(solution)/shard_map/start/pallas_call | solution.py:514
  15.6 0.1 collective-permute-start.2
  15.7 0.7 collective-permute-start.3
  16.4 0.7 collective-permute-done.2.from_e
  17.0 0.0 collective-permute-done.3.from_o
  17.1 3.3 %sweep.5 = (f32[1040,128]{1,0:T(8,128)S(1)}, f32[1040,128]{1,0:T(8,128)S(1)}, f32[64,128]{1,0:T(8,128)S(1)}, f32[264,128]{1,0:T(8,128)S(1)}, f32[264,128]{1,0:T(8,128)S(1)}) custom-call(s32[256]{0:T(256)S(1)} %copy-done, f32[264,128]{1,0:T(8,128)S(1)} %collective-permute-done.2.from_e, f32[264,128]{1,0:T(8,128)S(1)} %collective-permute-done.3.from_o, ...), custom_call_target="tpu_custom_call" | custom-call | flops 4000000 | bytes 3000000 | tf_op jit(solution)/shard_map/sweep/pallas_call | solution.py:514
  20.3 5.5 %collective-permute-start.4 = (f32[264,128]{1,0:T(8,128)S(1)}, f32[264,128]{1,0:T(8,128)S(1)}, u32[]{:S(2)}, u32[]{:S(2)}) collective-permute-start(f32[264,128]{1,0:T(8,128)S(1)} %get-tuple-element.74), channel_id=1, source_target_pairs={{0,1},{1,0},{2,3},{3,2},{4,5},{5,4},{6,7},{7,6},{8,9},{9,8},{10,11... | collective-permute-start | bytes 405512 | tf_op jit(solution)/shard_map/ppermute | solution.py:531
  25.9 0.7 collective-permute-start.5
  26.5 0.3 collective-permute-done.4.from_e
  26.9 0.0 collective-permute-done.5.from_o
  26.9 3.2 %sweep.6 = (f32[1040,128]{1,0:T(8,128)S(1)}, f32[1040,128]{1,0:T(8,128)S(1)}, f32[64,128]{1,0:T(8,128)S(1)}, f32[264,128]{1,0:T(8,128)S(1)}, f32[264,128]{1,0:T(8,128)S(1)}) custom-call(s32[256]{0:T(256)S(1)} %copy-done, f32[264,128]{1,0:T(8,128)S(1)} %collective-permute-done.4.from_e, f32[264,128]{1,0:T(8,128)S(1)} %collective-permute-done.5.from_o, ...), custom_call_target="tpu_custom_call" | custom-call | flops 4000000 | bytes 3000000 | tf_op jit(solution)/shard_map/sweep/pallas_call | solution.py:514
  30.1 6.9 %collective-permute-start.6 = (f32[264,128]{1,0:T(8,128)S(1)}, f32[264,128]{1,0:T(8,128)S(1)}, u32[]{:S(2)}, u32[]{:S(2)}) collective-permute-start(f32[264,128]{1,0:T(8,128)S(1)} %get-tuple-element.79), channel_id=1, source_target_pairs={{0,1},{1,0},{2,3},{3,2},{4,5},{5,4},{6,7},{7,6},{8,9},{9,8},{10,11... | collective-permute-start | bytes 405512 | tf_op jit(solution)/shard_map/ppermute | solution.py:531
  37.0 0.7 collective-permute-start.7
  37.7 0.3 collective-permute-done.6.from_e
  38.0 0.0 collective-permute-done.7.from_o
  38.0 3.3 %sweep.7 = (f32[1040,128]{1,0:T(8,128)S(1)}, f32[1040,128]{1,0:T(8,128)S(1)}, f32[64,128]{1,0:T(8,128)S(1)}, f32[264,128]{1,0:T(8,128)S(1)}, f32[264,128]{1,0:T(8,128)S(1)}) custom-call(s32[256]{0:T(256)S(1)} %copy-done, f32[264,128]{1,0:T(8,128)S(1)} %collective-permute-done.6.from_e, f32[264,128]{1,0:T(8,128)S(1)} %collective-permute-done.7.from_o, ...), custom_call_target="tpu_custom_call" | custom-call | flops 4000000 | bytes 3000000 | tf_op jit(solution)/shard_map/sweep/pallas_call | solution.py:514
  41.3 6.2 %collective-permute-start.8 = (f32[264,128]{1,0:T(8,128)S(1)}, f32[264,128]{1,0:T(8,128)S(1)}, u32[]{:S(2)}, u32[]{:S(2)}) collective-permute-start(f32[264,128]{1,0:T(8,128)S(1)} %get-tuple-element.84), channel_id=1, source_target_pairs={{0,1},{1,0},{2,3},{3,2},{4,5},{5,4},{6,7},{7,6},{8,9},{9,8},{10,11... | collective-permute-start | bytes 405512 | tf_op jit(solution)/shard_map/ppermute | solution.py:531
  47.5 0.7 collective-permute-start.9
  48.1 0.3 collective-permute-done.8.from_e
  48.5 0.0 collective-permute-done.9.from_o
  48.5 3.3 %sweep.8 = (f32[1040,128]{1,0:T(8,128)S(1)}, f32[1040,128]{1,0:T(8,128)S(1)}, f32[64,128]{1,0:T(8,128)S(1)}, f32[264,128]{1,0:T(8,128)S(1)}, f32[264,128]{1,0:T(8,128)S(1)}) custom-call(s32[256]{0:T(256)S(1)} %copy-done, f32[264,128]{1,0:T(8,128)S(1)} %collective-permute-done.8.from_e, f32[264,128]{1,0:T(8,128)S(1)} %collective-permute-done.9.from_o, ...), custom_call_target="tpu_custom_call" | custom-call | flops 4000000 | bytes 3000000 | tf_op jit(solution)/shard_map/sweep/pallas_call | solution.py:514
  51.8 7.5 %collective-permute-start.10 = (f32[264,128]{1,0:T(8,128)S(1)}, f32[264,128]{1,0:T(8,128)S(1)}, u32[]{:S(2)}, u32[]{:S(2)}) collective-permute-start(f32[264,128]{1,0:T(8,128)S(1)} %get-tuple-element.89), channel_id=1, source_target_pairs={{0,1},{1,0},{2,3},{3,2},{4,5},{5,4},{6,7},{7,6},{8,9},{9,8},{10,11... | collective-permute-start | bytes 405512 | tf_op jit(solution)/shard_map/ppermute | solution.py:531
  59.2 0.7 collective-permute-start.11
  59.9 0.3 collective-permute-done.10.from_e
  60.2 0.0 collective-permute-done.11.from_o
  60.2 3.9 %sweep.9 = (f32[1040,128]{1,0:T(8,128)S(1)}, f32[1040,128]{1,0:T(8,128)S(1)}, f32[128,128]{1,0:T(8,128)}) custom-call(s32[256]{0:T(256)S(1)} %copy-done, f32[264,128]{1,0:T(8,128)S(1)} %collective-permute-done.10.from_e, f32[264,128]{1,0:T(8,128)S(1)} %collective-permute-done.11.from_o, f32[1040,128]{1,0:T(8,128)S(1)} %get-tuple-element.91.p_old, ...), custom_call_target="tpu_custom_call" | custom-call | flops 4000000 | bytes 3000000 | tf_op jit(solution)/shard_map/sweep/pallas_call | solution.py:514
  64.1 12.9 %all-to-all-start = ((f32[16,8,128]{2,1,0:T(8,128)}), f32[16,8,128]{2,1,0:T(8,128)S(1)}, u32[]{:S(2)}, u32[]{:S(2)}) async-start(f32[16,8,128]{2,1,0:T(8,128)} %bitcast.16), calls=%async_computation | async-start | bytes 131072 | tf_op jit(solution)/shard_map/all_to_all | solution.py:585
  77.1 0.8 slice.9
  77.9 0.8 slice.10
  78.7 5.2 %all-to-all-done = f32[16,8,128]{2,1,0:T(8,128)S(1)} async-done(((f32[16,8,128]{2,1,0:T(8,128)}), f32[16,8,128]{2,1,0:T(8,128)S(1)}, u32[]{:S(2)}, u32[]{:S(2)}) %all-to-all-start) | async-done | bytes 65568 | tf_op jit(solution)/shard_map/all_to_all | solution.py:585
  84.0 0.5 reduce_sum.9
Async XLA Ops:
  0.6 0.7 copy-start.4
  0.6 0.7 copy-start.1
  2.2 10.6 %collective-permute-start.1 = (f32[136,128]{1,0:T(8,128)S(1)}, f32[136,128]{1,0:T(8,128)S(1)}, u32[]{:S(2)}, u32[]{:S(2)}) collective-permute-start(f32[136,128]{1,0:T(8,128)S(1)} %get-tuple-element.50), channel_id=1, source_target_pairs={{1,2},{2,1},{3,4},{4,3},{5,6},{6,5},{7,8},{8,7},{9,10},{10,9},{11,... | collective-permute-start | bytes 208904 | tf_op jit(solution)/shard_map/ppermute | solution.py:531
  2.9 9.9 %collective-permute-start = (f32[136,128]{1,0:T(8,128)S(1)}, f32[136,128]{1,0:T(8,128)S(1)}, u32[]{:S(2)}, u32[]{:S(2)}) collective-permute-start(f32[136,128]{1,0:T(8,128)S(1)} %get-tuple-element.50), channel_id=1, source_target_pairs={{0,1},{1,0},{2,3},{3,2},{4,5},{5,4},{6,7},{7,6},{8,9},{9,8},{10,11... | collective-permute-start | bytes 208904 | tf_op jit(solution)/shard_map/ppermute | solution.py:531
  7.2 0.7 copy-start
  12.8 0.7 copy-start.3
  12.8 0.7 copy-start.2
  15.6 1.4 %collective-permute-start.2 = (f32[264,128]{1,0:T(8,128)S(1)}, f32[264,128]{1,0:T(8,128)S(1)}, u32[]{:S(2)}, u32[]{:S(2)}) collective-permute-start(f32[264,128]{1,0:T(8,128)S(1)} %get-tuple-element.60), channel_id=1, source_target_pairs={{0,1},{1,0},{2,3},{3,2},{4,5},{5,4},{6,7},{7,6},{8,9},{9,8},{10,11... | collective-permute-start | bytes 405512 | tf_op jit(solution)/shard_map/ppermute | solution.py:531
  15.7 1.3 %collective-permute-start.3 = (f32[264,128]{1,0:T(8,128)S(1)}, f32[264,128]{1,0:T(8,128)S(1)}, u32[]{:S(2)}, u32[]{:S(2)}) collective-permute-start(f32[264,128]{1,0:T(8,128)S(1)} %get-tuple-element.61), channel_id=1, source_target_pairs={{1,2},{2,1},{3,4},{4,3},{5,6},{6,5},{7,8},{8,7},{9,10},{10,9},{11,... | collective-permute-start | bytes 405512 | tf_op jit(solution)/shard_map/ppermute | solution.py:531
  20.3 6.5 %collective-permute-start.4 = (f32[264,128]{1,0:T(8,128)S(1)}, f32[264,128]{1,0:T(8,128)S(1)}, u32[]{:S(2)}, u32[]{:S(2)}) collective-permute-start(f32[264,128]{1,0:T(8,128)S(1)} %get-tuple-element.74), channel_id=1, source_target_pairs={{0,1},{1,0},{2,3},{3,2},{4,5},{5,4},{6,7},{7,6},{8,9},{9,8},{10,11... | collective-permute-start | bytes 405512 | tf_op jit(solution)/shard_map/ppermute | solution.py:531
  25.9 1.0 %collective-permute-start.5 = (f32[264,128]{1,0:T(8,128)S(1)}, f32[264,128]{1,0:T(8,128)S(1)}, u32[]{:S(2)}, u32[]{:S(2)}) collective-permute-start(f32[264,128]{1,0:T(8,128)S(1)} %get-tuple-element.75), channel_id=1, source_target_pairs={{1,2},{2,1},{3,4},{4,3},{5,6},{6,5},{7,8},{8,7},{9,10},{10,9},{11,... | collective-permute-start | bytes 405512 | tf_op jit(solution)/shard_map/ppermute | solution.py:531
  30.1 7.9 %collective-permute-start.6 = (f32[264,128]{1,0:T(8,128)S(1)}, f32[264,128]{1,0:T(8,128)S(1)}, u32[]{:S(2)}, u32[]{:S(2)}) collective-permute-start(f32[264,128]{1,0:T(8,128)S(1)} %get-tuple-element.79), channel_id=1, source_target_pairs={{0,1},{1,0},{2,3},{3,2},{4,5},{5,4},{6,7},{7,6},{8,9},{9,8},{10,11... | collective-permute-start | bytes 405512 | tf_op jit(solution)/shard_map/ppermute | solution.py:531
  37.0 1.0 %collective-permute-start.7 = (f32[264,128]{1,0:T(8,128)S(1)}, f32[264,128]{1,0:T(8,128)S(1)}, u32[]{:S(2)}, u32[]{:S(2)}) collective-permute-start(f32[264,128]{1,0:T(8,128)S(1)} %get-tuple-element.80), channel_id=1, source_target_pairs={{1,2},{2,1},{3,4},{4,3},{5,6},{6,5},{7,8},{8,7},{9,10},{10,9},{11,... | collective-permute-start | bytes 405512 | tf_op jit(solution)/shard_map/ppermute | solution.py:531
  41.3 7.2 %collective-permute-start.8 = (f32[264,128]{1,0:T(8,128)S(1)}, f32[264,128]{1,0:T(8,128)S(1)}, u32[]{:S(2)}, u32[]{:S(2)}) collective-permute-start(f32[264,128]{1,0:T(8,128)S(1)} %get-tuple-element.84), channel_id=1, source_target_pairs={{0,1},{1,0},{2,3},{3,2},{4,5},{5,4},{6,7},{7,6},{8,9},{9,8},{10,11... | collective-permute-start | bytes 405512 | tf_op jit(solution)/shard_map/ppermute | solution.py:531
  47.5 1.0 %collective-permute-start.9 = (f32[264,128]{1,0:T(8,128)S(1)}, f32[264,128]{1,0:T(8,128)S(1)}, u32[]{:S(2)}, u32[]{:S(2)}) collective-permute-start(f32[264,128]{1,0:T(8,128)S(1)} %get-tuple-element.85), channel_id=1, source_target_pairs={{1,2},{2,1},{3,4},{4,3},{5,6},{6,5},{7,8},{8,7},{9,10},{10,9},{11,... | collective-permute-start | bytes 405512 | tf_op jit(solution)/shard_map/ppermute | solution.py:531
  51.8 8.5 %collective-permute-start.10 = (f32[264,128]{1,0:T(8,128)S(1)}, f32[264,128]{1,0:T(8,128)S(1)}, u32[]{:S(2)}, u32[]{:S(2)}) collective-permute-start(f32[264,128]{1,0:T(8,128)S(1)} %get-tuple-element.89), channel_id=1, source_target_pairs={{0,1},{1,0},{2,3},{3,2},{4,5},{5,4},{6,7},{7,6},{8,9},{9,8},{10,11... | collective-permute-start | bytes 405512 | tf_op jit(solution)/shard_map/ppermute | solution.py:531
  59.2 1.0 %collective-permute-start.11 = (f32[264,128]{1,0:T(8,128)S(1)}, f32[264,128]{1,0:T(8,128)S(1)}, u32[]{:S(2)}, u32[]{:S(2)}) collective-permute-start(f32[264,128]{1,0:T(8,128)S(1)} %get-tuple-element.90), channel_id=1, source_target_pairs={{1,2},{2,1},{3,4},{4,3},{5,6},{6,5},{7,8},{8,7},{9,10},{10,9},{11,... | collective-permute-start | bytes 405512 | tf_op jit(solution)/shard_map/ppermute | solution.py:531
  64.1 19.9 %all-to-all-start = ((f32[16,8,128]{2,1,0:T(8,128)}), f32[16,8,128]{2,1,0:T(8,128)S(1)}, u32[]{:S(2)}, u32[]{:S(2)}) async-start(f32[16,8,128]{2,1,0:T(8,128)} %bitcast.16), calls=%async_computation | async-start | bytes 131072 | tf_op jit(solution)/shard_map/all_to_all | solution.py:585
where the time goes:
time: 84.9 us; the launch traced here: 84.5 us
  starting transfers between devices  47.4 us (56%)
  Pallas kernels  24.8 us (29%)
  waiting for transfers between devices  7.23 us (9%)
  local copies, waits for them, and re-layouts  3.7 us (4%)
    ppermute x6, starting transfers between devices, exchange(): lax.ppermute(send_e, 'gx', pairs_e)  30.5 us
    pallas_call x8, Pallas kernels, call(): pl.pallas_call(functools.partial(kernel), in_specs=[spec(space) for space...  24.8 us
    all_to_all x1, starting transfers between devices, body(): grads = lax.all_to_all(rest[0].reshape(devices, SUB, LANES), 'gx', 0, 0)  12.9 us
    all_to_all x1, waiting for transfers between devices, body(): grads = lax.all_to_all(rest[0].reshape(devices, SUB, LANES), 'gx', 0, 0)  5.24 us
    ppermute x6, starting transfers between devices, exchange(): lax.ppermute(send_o, 'gx', pairs_o)  3.96 us
    unnamed x10, local copies, waits for them, and re-layouts  2.04 us
    ppermute x6, waiting for transfers between devices, exchange(): lax.ppermute(send_e, 'gx', pairs_e)  1.97 us
  transfers between devices with their start and end apart: 13, of which 6 were waited for; matrix products, arithmetic and copies ran while one was open for 2% of the time, Pallas kernels for 6%

commit v1 on v0

v1 whole, which is shorter than its diff:
```python
import functools

import jax
import jax.numpy as jnp
from jax import lax
from jax.experimental import pallas as pl
from jax.experimental.pallas import tpu as pltpu
from jax.sharding import PartitionSpec as P

SWEEPS = 6
SUB = 8
LANES = 128
F32 = jnp.float32


def vmem(rows):
    return pltpu.VMEM((rows, LANES), F32)


def placed(array, space):
    return array if space is pltpu.SMEM else pltpu.with_memory_space_constraint(array, space)


def spec(space):
    return pl.BlockSpec(memory_space=space)


def iota(shape, dim):
    return lax.broadcasted_iota(jnp.int32, shape, dim)


def lane_sum(block):
    return jnp.sum(block, axis=1, keepdims=True)


def spread(column, groups):
    return jnp.broadcast_to(column, (groups, LANES))


def row_of(column, groups):
    mine = iota((groups, LANES), 0) == iota((groups, LANES), 1)
    return jnp.sum(jnp.where(mine, column, 0.0), axis=0, keepdims=True)


def column_of(row, groups):
    mine = iota((groups, LANES), 0) == iota((groups, LANES), 1)
    return spread(lane_sum(jnp.where(mine, jnp.broadcast_to(row, (groups, LANES)), 0.0)), groups)


def well_block(part_own, part_before, groups):
    sub = iota((SUB, LANES), 0)
    own = jnp.broadcast_to(row_of(part_own, groups), (SUB, LANES))
    before = jnp.broadcast_to(row_of(part_before, groups), (SUB, LANES))
    return jnp.where(sub == 0, own, jnp.where(sub == 1, before, 0.0))


def group_rows(ref, groups, run):
    per_row = LANES // run
    return jnp.concatenate(
        [jnp.broadcast_to(ref[i : i + 1, :], (per_row, LANES)) for i in range(groups // per_row)], axis=0
    )


def first_kernel(sizes, tx_hbm, well_hbm, index_hbm, send_ref, wells_ref, well_ref, index_ref, sems):
    ny, groups, run = sizes.ny, sizes.groups, sizes.run
    plane = pltpu.make_async_copy(
        tx_hbm.at[pl.ds((sizes.planes - 1) * ny, ny)], send_ref.at[pl.ds(0, ny)], sems.at[0]
    )
    get_well = pltpu.make_async_copy(well_hbm, well_ref, sems.at[1])
    get_index = pltpu.make_async_copy(index_hbm, index_ref, sems.at[2])
    for copy in (get_well, get_index, plane):
        copy.start()
    place = lax.axis_index("gx")
    shape = (groups, LANES)
    per_row = LANES // run
    local = iota(shape, 0) % per_row
    lane = iota(shape, 1)
    get_well.wait()
    get_index.wait()
    weights = jnp.where(lane // run == local, group_rows(index_ref, groups, run), 0.0)
    total = lane_sum(weights)
    first = jnp.where(lane == local * run, group_rows(well_ref, groups, run).astype(F32), 0.0)
    well = lane_sum(first)
    before = well < (place * groups).astype(F32)
    before = spread(jnp.where(before, 1.0, 0.0), groups)
    total = spread(total, groups)
    wells_ref[0:groups, :] = before
    wells_ref[groups : 2 * groups, :] = total
    send_ref[ny : ny + SUB, :] = well_block(total * (1.0 - before), total * before, groups)
    plane.wait()


def setup_kernel(
    sizes,
    cell_ref,
    index_hbm,
    tx_hbm,
    ty_hbm,
    tz_hbm,
    accel_hbm,
    coupling_hbm,
    upwind_hbm,
    storage_hbm,
    rhs_p_hbm,
    rhs_s_hbm,
    cross_hbm,
    tx_ref,
    ty_ref,
    tyl_ref,
    tz_ref,
    tzl_ref,
    rp_ref,
    ip_ref,
    cc_ref,
    rs_ref,
    uu_ref,
    xx_ref,
    extra_ref,
    weight_ref,
    raw_ty,
    raw_storage,
    cwi_ref,
    index_ref,
    sems,
    index_sem,
):
    ny, planes, groups, run = sizes.ny, sizes.planes, sizes.groups, sizes.run
    rows = planes * ny
    moves = [
        (tx_hbm, tx_ref),
        (ty_hbm, raw_ty.at[pl.ds(SUB, rows)]),
        (tz_hbm, tz_ref),
        (accel_hbm, ip_ref),
        (coupling_hbm, cc_ref),
        (upwind_hbm, uu_ref),
        (storage_hbm, raw_storage),
        (rhs_p_hbm, rp_ref),
        (rhs_s_hbm, rs_ref),
        (cross_hbm, xx_ref),
    ]
    copies = [pltpu.make_async_copy(src, dst, sems.at[i]) for i, (src, dst) in enumerate(moves)]
    fetch = pltpu.make_async_copy(index_hbm, index_ref, index_sem)
    fetch.start()
    for copy in copies:
        copy.start()

    last = lax.axis_index("gx") == lax.axis_size("gx") - 1
    keep_last = jnp.where(last, 0.0, 1.0)
    zero = jnp.zeros((SUB, LANES), F32)

    @pl.loop(0, rows // SUB, unroll=8)
    def _(i):
        cwi_ref[pl.ds(pl.multiple_of(i * SUB, SUB), SUB), :] = zero

    fetch.wait()
    spot = iota((SUB, LANES), 0) * LANES + iota((SUB, LANES), 1)
    for g in range(groups):
        weight = zero
        for k in range(g * run, (g + 1) * run):
            cell = cell_ref[k]
            at = (cell // (ny * LANES)) * LANES + cell % LANES
            weight = weight + jnp.where(spot == at, index_ref[k], 0.0)
        weight_ref[g * SUB : (g + 1) * SUB, :] = weight
        slab = pl.ds((cell_ref[g * run] // LANES) % ny, planes, ny)
        cwi_ref[slab, :] = cwi_ref[slab, :] + weight

    for copy in copies:
        copy.wait()

    lane = iota((SUB, LANES), 1)
    sub = iota((SUB, LANES), 0)

    @pl.loop(0, ny // SUB)
    def _(r):
        y0 = pl.multiple_of(r * SUB, SUB)
        ypos = sub + y0
        txl = None
        for x in range(planes):
            at = pl.ds(y0 + x * ny, SUB)
            tx = tx_ref[at, :]
            if x == planes - 1:
                tx = tx * keep_last
                tx_ref[at, :] = tx
            ty = jnp.where(ypos == ny - 1, 0.0, raw_ty[pl.ds(y0 + (x * ny + SUB), SUB), :])
            tyl = jnp.where(ypos == 0, 0.0, raw_ty[pl.ds(y0 + (x * ny + SUB - 1), SUB), :])
            tz = jnp.where(lane == LANES - 1, 0.0, tz_ref[at, :])
            tzl = pltpu.roll(tz, 1, 1)
            ty_ref[at, :] = ty
            tyl_ref[at, :] = tyl
            tz_ref[at, :] = tz
            tzl_ref[at, :] = tzl
            tsum = tx + ty + tyl + tz + tzl
            if x > 0:
                tsum = tsum + txl
            accel = ip_ref[at, :]
            coupling = cc_ref[at, :]
            upwind = uu_ref[at, :]
            to_p = accel * (1.0 + jnp.abs(coupling))
            to_s = accel * jnp.abs(upwind)
            dp = to_p * tsum + accel * cwi_ref[at, :]
            ds = to_s * tsum + raw_storage[at, :]
            if x == 0:
                here = pl.ds(y0, SUB)
                extra_ref[here, :] = to_p
                extra_ref[pl.ds(y0 + ny, SUB), :] = to_s
                extra_ref[pl.ds(y0 + 2 * ny, SUB), :] = ds
                ip_ref[at, :] = dp
            else:
                ip = 1.0 / dp
                is_ = 1.0 / ds
                ip_ref[at, :] = ip
                cc_ref[at, :] = coupling * ip
                rp_ref[at, :] = rp_ref[at, :] * ip
                rs_ref[at, :] = rs_ref[at, :] * is_
                uu_ref[at, :] = upwind * is_
                xx_ref[at, :] = xx_ref[at, :] * is_
            txl = tx


def own_lanes(ref, place, groups):
    shape = (groups, LANES)
    start = place * groups
    row = jnp.broadcast_to(ref[pl.ds(start // LANES, 1), :].astype(F32), shape)
    mine = iota(shape, 1) == iota(shape, 0) + start % LANES
    return spread(lane_sum(jnp.where(mine, row, 0.0)), groups)


def clear_ends(rows, *refs):
    zero = jnp.zeros((SUB, LANES), F32)
    for ref in refs:
        ref[0:SUB, :] = zero
        ref[rows + SUB : rows + 2 * SUB, :] = zero


def path_y(sizes, cell_ref, g):
    return (cell_ref[g * sizes.run] // LANES) % sizes.ny


def slab_of(sizes, cell_ref, g, pad):
    return pl.ds(path_y(sizes, cell_ref, g) + pad, sizes.planes, sizes.ny)


def add_wells(sizes, cell_ref, mu_ref, wp_ref, ws_ref, p_ref, s_ref, pad):
    for g in range(sizes.groups):
        slab = slab_of(sizes, cell_ref, g, pad)
        at = pl.ds(g * SUB, SUB)
        mu = mu_ref[g : g + 1, :]
        p_ref[slab, :] = p_ref[slab, :] + mu * wp_ref[at, :]
        s_ref[slab, :] = s_ref[slab, :] - mu * ws_ref[at, :]


def add_wells_to_plane(sizes, cell_ref, mu_ref, wp_ref, ws_ref, x, send_ref):
    for g in range(sizes.groups):
        y = path_y(sizes, cell_ref, g)
        in_p, in_s, at = pl.ds(y, 1), pl.ds(y + sizes.ny, 1), pl.ds(x + g * SUB, 1)
        mu = mu_ref[g : g + 1, :]
        send_ref[in_p, :] = send_ref[in_p, :] + mu * wp_ref[at, :]
        send_ref[in_s, :] = send_ref[in_s, :] - mu * ws_ref[at, :]


def path_rows(sizes, cell_ref, weight_ref, p_ref, rows_ref):
    for g in range(sizes.groups):
        slab = slab_of(sizes, cell_ref, g, SUB)
        at = pl.ds(g * SUB, SUB)
        rows_ref[g : g + 1, :] = jnp.sum(p_ref[slab, :] * weight_ref[at, :], axis=0, keepdims=True)


def facing(sizes, even):
    last = sizes.planes - 1
    return jnp.where(even, 0, last), jnp.where(even, last, 0)


def finish_plane(sizes, x, p_ref, s_ref, halo_ref, plane_ref, send_ref):
    ny = sizes.ny
    start = pl.multiple_of(x * ny + SUB, SUB)
    for r in range(0, ny, SUB):
        at = slice(r, r + SUB)
        at_s = slice(ny + r, ny + r + SUB)
        p, s = p_ref[pl.ds(start + r, SUB), :], s_ref[pl.ds(start + r, SUB), :]
        if halo_ref is not None:
            hp, hs = halo_ref[at, :], halo_ref[at_s, :]
            a, b, c, xx = [plane_ref[i * ny + r : i * ny + r + SUB, :] for i in range(4)]
            change = a * hp + b * hs
            p = p + change
            s = s + c * hs - xx * change
        send_ref[at, :] = p
        send_ref[at_s, :] = s


BEFORE, RHS_OWN, INV_OWN, SUM_OWN, RHS, INV, SLOT_OWN, SLOT_BEFORE, TABLE = range(9)


def shared_cells(sizes, cell_ref, weight_ref, wp_ref, out_ref):
    groups = sizes.groups
    shape = (groups, LANES)
    sub, lane = iota(shape, 0), iota(shape, 1)
    y_row = jnp.full(shape, -1, jnp.int32)
    y_col = y_row
    for g in range(groups):
        y = path_y(sizes, cell_ref, g)
        y_row = jnp.where(lane == g, y, y_row)
        y_col = jnp.where(sub == g, y, y_col)
    total = jnp.zeros(shape, F32)
    empty = jnp.zeros((LANES - groups, LANES), F32)
    for x in range(sizes.planes):
        at = pl.ds(x, groups, SUB)
        other = jnp.concatenate([wp_ref[at, :], empty], axis=0)
        total = total + lax.dot_general(
            weight_ref[at, :], other, (((1,), (1,)), ((), ())),
            precision=lax.Precision.HIGHEST, preferred_element_type=F32,
        )
    out_ref[...] = jnp.where(y_row == y_col, total, 0.0)


def start_kernel(
    sizes,
    cell_ref,
    from_o,
    from_e,
    wells_ref,
    rhs_hbm,
    slot_hbm,
    tx_ref,
    rp_ref,
    ip_ref,
    cc_ref,
    rs_ref,
    uu_ref,
    xx_ref,
    extra_ref,
    weight_ref,
    p_ref,
    s_ref,
    edge_ref,
    plane_e,
    plane_o,
    wp_ref,
    ws_ref,
    shared_ref,
    table_ref,
    mu_ref,
    parts_out,
    send_o,
    rows_ref,
    rhs_ref,
    slot_ref,
    sems,
):
    ny, planes, groups = sizes.ny, sizes.planes, sizes.groups
    rows = planes * ny
    place = lax.axis_index("gx")
    even = place % 2 == 0
    x_o, _ = facing(sizes, even)
    fetches = [
        pltpu.make_async_copy(rhs_hbm, rhs_ref, sems.at[0]),
        pltpu.make_async_copy(slot_hbm, slot_ref, sems.at[1]),
    ]
    for fetch in fetches:
        fetch.start()

    @pl.loop(0, ny // SUB)
    def _(r):
        y0 = pl.multiple_of(r * SUB, SUB)
        at = pl.ds(y0, SUB)
        txl = jnp.where(even, from_o[at, :], from_e[at, :])
        ip = 1.0 / (ip_ref[at, :] + extra_ref[at, :] * txl)
        is_ = 1.0 / (extra_ref[pl.ds(y0 + 2 * ny, SUB), :] + extra_ref[pl.ds(y0 + ny, SUB), :] * txl)
        cc, uu = cc_ref[at, :] * ip, uu_ref[at, :] * is_
        rp, rs, xx = rp_ref[at, :] * ip, rs_ref[at, :] * is_, xx_ref[at, :] * is_
        for i, value in enumerate([ip, cc, rp, rs, uu, xx]):
            edge_ref[pl.ds(y0 + i * ny, SUB), :] = value
        end = pl.ds(y0 + (planes - 1) * ny, SUB)
        tx = tx_ref[end, :]
        low = [ip * txl, cc * txl, uu * txl, xx]
        high = [ip_ref[end, :] * tx, cc_ref[end, :] * tx, uu_ref[end, :] * tx, xx_ref[end, :]]
        for i in range(4):
            to = pl.ds(y0 + i * ny, SUB)
            plane_o[to, :] = jnp.where(even, low[i], high[i])
            plane_e[to, :] = jnp.where(even, high[i], low[i])
        p_ref[pl.ds(y0 + SUB, SUB), :] = rp
        s_ref[pl.ds(y0 + SUB, SUB), :] = rs - xx * rp
        for x in range(1, planes):
            at = pl.ds(y0 + x * ny, SUB)
            to = pl.ds(y0 + (x * ny + SUB), SUB)
            rp = rp_ref[at, :]
            p_ref[to, :] = rp
            s_ref[to, :] = rs_ref[at, :] - xx_ref[at, :] * rp

    clear_ends(rows, p_ref, s_ref)
    sub = iota((SUB, LANES), 0)
    for g in range(groups):
        y = path_y(sizes, cell_ref, g)
        at = pl.ds(g * SUB, SUB)
        slab = pl.ds(y, planes, ny)
        ip = jnp.where(sub == 0, edge_ref[pl.ds(y, 1), :], ip_ref[slab, :])
        xx = jnp.where(sub == 0, edge_ref[pl.ds(y + 5 * ny, 1), :], xx_ref[slab, :])
        wp = weight_ref[at, :] * ip
        wp_ref[at, :] = wp
        ws_ref[at, :] = wp * xx
    shared_cells(sizes, cell_ref, weight_ref, wp_ref, shared_ref)

    tile_e, tile_o = from_e[ny : ny + SUB, :], from_o[ny : ny + SUB, :]
    low = jnp.where(even, tile_o, tile_e)
    high = jnp.where(even, tile_e, tile_o)
    before = wells_ref[0:groups, :]
    mine = wells_ref[groups : 2 * groups, :]
    is_before = before > 0.5
    sum_own = mine * (1.0 - before) + column_of(high[1:2, :], groups)
    sum_before = mine * before + column_of(low[0:1, :], groups)
    for fetch in fetches:
        fetch.wait()
    rhs_own = own_lanes(rhs_ref, place, groups)
    rhs_before = own_lanes(rhs_ref, jnp.maximum(place - 1, 0), groups)
    inv_own = 1.0 / (1.5 * sum_own + 0.5)
    inv_before = 1.0 / (1.5 * sum_before + 0.5)
    rhs = jnp.where(is_before, rhs_before, rhs_own)
    inv = jnp.where(is_before, inv_before, inv_own)
    entries = {
        BEFORE: before,
        RHS_OWN: rhs_own,
        INV_OWN: inv_own,
        SUM_OWN: sum_own,
        RHS: rhs,
        INV: inv,
        SLOT_OWN: own_lanes(slot_ref, place, groups),
        SLOT_BEFORE: own_lanes(slot_ref, jnp.maximum(place - 1, 0), groups),
    }
    for i, entry in entries.items():
        table_ref[i * groups : (i + 1) * groups, :] = entry
    mu = rhs * inv
    mu_ref[...] = mu

    finish_plane(sizes, x_o, p_ref, s_ref, None, None, send_o)
    add_wells_to_plane(sizes, cell_ref, mu_ref, wp_ref, ws_ref, x_o, send_o)
    path_rows(sizes, cell_ref, weight_ref, p_ref, rows_ref)
    put_sums(sizes, before, rows_ref[...] + shared_ref[...] * row_of(mu, groups), parts_out, send_o)


def put_sums(sizes, before, by_lane, parts_out, send_o):
    ny, groups = sizes.ny, sizes.groups
    total = spread(lane_sum(by_lane), groups)
    part_own, part_before = total * (1.0 - before), total * before
    parts_out[0:groups, :] = part_own
    parts_out[groups : 2 * groups, :] = part_before
    send_o[2 * ny : 2 * ny + SUB, :] = well_block(part_own, part_before, groups)
    return part_own, part_before


def finish_core_plane(sizes, cell_ref, p_ref, s_ref, mu_ref, wp_ref, ws_ref, send_o, halo, plane_e, send_e):
    even = lax.axis_index("gx") % 2 == 0
    _, x_e = facing(sizes, even)
    finish_plane(sizes, x_e, p_ref, s_ref, halo, plane_e, send_e)
    add_wells_to_plane(sizes, cell_ref, mu_ref, wp_ref, ws_ref, x_e, send_e)
    tail = slice(2 * sizes.ny, 2 * sizes.ny + SUB)
    send_e[tail, :] = send_o[tail, :]


def near_weights(sizes, cell_ref, weight_ref, plane_e, plane_o, near_ref):
    ny, groups = sizes.ny, sizes.groups
    even = lax.axis_index("gx") % 2 == 0
    x_o, x_e = facing(sizes, even)
    for g in range(groups):
        y = path_y(sizes, cell_ref, g)
        for i, (x, plane) in enumerate(((x_o, plane_o), (x_e, plane_e))):
            weight = weight_ref[pl.ds(x + g * SUB, 1), :]
            for j in range(2):
                to = (2 * i + j) * groups + g
                near_ref[to : to + 1, :] = weight * plane[pl.ds(y + j * ny, 1), :]


def put_planes(sizes, even, send_e, send_o, p_ref, s_ref, pad):
    ny = sizes.ny
    x_o, x_e = facing(sizes, even)
    for send, x in ((send_o, x_o), (send_e, x_e)):
        start = pl.multiple_of(x * ny + pad, SUB)
        for r in range(0, ny, SUB):
            p_ref[pl.ds(start + r, SUB), :] = send[r : r + SUB, :]
            s_ref[pl.ds(start + r, SUB), :] = send[ny + r : ny + r + SUB, :]


def inner_kernel(
    sizes,
    first,
    cell_ref,
    p_in,
    s_in,
    mu_ref,
    wp_ref,
    ws_ref,
    weight_ref,
    send_o,
    tx_ref,
    ty_ref,
    tyl_ref,
    tz_ref,
    tzl_ref,
    rp_ref,
    ip_ref,
    cc_ref,
    rs_ref,
    uu_ref,
    xx_ref,
    edge_ref,
    plane_e,
    *refs,
):
    ny, planes = sizes.ny, sizes.planes
    rows = planes * ny
    even = lax.axis_index("gx") % 2 == 0
    if first:
        plane_o, p_old, s_old, p_ref, s_ref, rows_ref, send_e, near_ref = refs
        halo = None
        near_weights(sizes, cell_ref, weight_ref, plane_e, plane_o, near_ref)
    else:
        halo, p_old, s_old, p_ref, s_ref, rows_ref, send_e = refs
    finish_core_plane(sizes, cell_ref, p_old, s_old, mu_ref, wp_ref, ws_ref, send_o, halo, plane_e, send_e)
    add_wells(sizes, cell_ref, mu_ref, wp_ref, ws_ref, p_old, s_old, SUB)
    put_planes(sizes, even, send_e, send_o, p_old, s_old, SUB)

    @pl.loop(0, ny // SUB)
    def _(r):
        y0 = pl.multiple_of(r * SUB, SUB)
        here = [pl.ds(y0 + (x * ny + SUB), SUB) for x in range(planes)]
        ps = [p_old[at, :] for at in here]
        ss = [s_old[at, :] for at in here]
        tx = None
        for x in range(planes):
            at = pl.ds(y0 + x * ny, SUB)
            up = pl.ds(y0 + (x * ny + SUB + 1), SUB)
            down = pl.ds(y0 + (x * ny + SUB - 1), SUB)
            txl = tx
            tx = tx_ref[at, :] if x < planes - 1 else None
            ty, tyl, tz, tzl = ty_ref[at, :], tyl_ref[at, :], tz_ref[at, :], tzl_ref[at, :]

            def neighbours(fields, old):
                mid = fields[x]
                total = tz * pltpu.roll(mid, LANES - 1, 1) + tzl * pltpu.roll(mid, 1, 1)
                total = total + (ty * old[up, :] + tyl * old[down, :])
                if x < planes - 1:
                    total = total + tx * fields[x + 1]
                if x > 0:
                    total = total + txl * fields[x - 1]
                return total

            sum_p = neighbours(ps, p_old)
            sum_s = neighbours(ss, s_old)
            if x == 0:
                ip, cc, rp, rs, uu, xx = [edge_ref[pl.ds(y0 + i * ny, SUB), :] for i in range(6)]
            else:
                ip, cc, rp, rs, uu, xx = [ref[at, :] for ref in (ip_ref, cc_ref, rp_ref, rs_ref, uu_ref, xx_ref)]
            p = rp + ip * sum_p + cc * sum_s
            p_ref[here[x], :] = p
            s_ref[here[x], :] = rs + uu * sum_s - xx * p

    clear_ends(rows, p_ref, s_ref)
    path_rows(sizes, cell_ref, weight_ref, p_ref, rows_ref)


def facing_kernel(sizes, cell_ref, from_o, p_ref, s_ref, plane_o, near_ref, send_o, sums_ref):
    even = lax.axis_index("gx") % 2 == 0
    x_o, _ = facing(sizes, even)
    finish_plane(sizes, x_o, p_ref, s_ref, from_o, plane_o, send_o)
    send_o[2 * sizes.ny :, :] = from_o[2 * sizes.ny :, :]
    near_sums(sizes, cell_ref, from_o, near_ref, 0, sums_ref)


def near_sums(sizes, cell_ref, halo, near_ref, side, sums_ref):
    groups = sizes.groups
    for g in range(groups):
        y = path_y(sizes, cell_ref, g)
        row = jnp.zeros((1, LANES), F32)
        for j in range(2):
            at = (2 * side + j) * groups + g
            row = row + near_ref[at : at + 1, :] * halo[pl.ds(y + j * sizes.ny, 1), :]
        sums_ref[g : g + 1, :] = row


def outer_kernel(
    sizes,
    final,
    cell_ref,
    send_in,
    from_e,
    rows_ref,
    sums_ref,
    parts_in,
    table_ref,
    wp_ref,
    ws_ref,
    shared_ref,
    near_ref,
    send_o,
    mu_ref,
    parts_out,
    *rest,
):
    ny, groups = sizes.ny, sizes.groups
    near_rows = rest[-1]
    even = lax.axis_index("gx") % 2 == 0
    x_o, _ = facing(sizes, even)

    def table(i):
        return table_ref[i * groups : (i + 1) * groups, :]

    tile_e, tile_o = from_e[2 * ny : 2 * ny + SUB, :], send_o[2 * ny : 2 * ny + SUB, :]
    low = jnp.where(even, tile_o, tile_e)
    high = jnp.where(even, tile_e, tile_o)
    before = table(BEFORE)
    total_own = parts_in[0:groups, :] + column_of(high[1:2, :], groups)
    total_before = parts_in[groups : 2 * groups, :] + column_of(low[0:1, :], groups)
    mu = (table(RHS) + jnp.where(before > 0.5, total_before, total_own)) * table(INV)
    mu_ref[...] = mu
    near_sums(sizes, cell_ref, from_e, near_ref, 1, near_rows)
    by_lane = rows_ref[...] + sums_ref[...] + near_rows[...] + shared_ref[...] * row_of(mu, groups)
    add_wells_to_plane(sizes, cell_ref, mu_ref, wp_ref, ws_ref, x_o, send_o)
    part_own, part_before = put_sums(sizes, before, by_lane, parts_out, send_o)
    if not final:
        return
    grads_ref = rest[0]
    mu_own = (table(RHS_OWN) + total_own) * table(INV_OWN)
    grad_own = mu_own * table(SUM_OWN) - part_own
    grad_before = -part_before
    lane = iota((groups, LANES), 1)
    slot_own, slot_before = table(SLOT_OWN), table(SLOT_BEFORE)
    inside = lane < groups
    for d in range(sizes.devices):
        want = (lane + d * groups).astype(F32)
        own = jnp.where(inside & (slot_own == want), grad_own, 0.0)
        other = jnp.where(inside & (slot_before == want), grad_before, 0.0)
        row = jnp.sum(own + other, axis=0, keepdims=True)
        grads_ref[d * SUB : (d + 1) * SUB, :] = jnp.where(
            iota((SUB, LANES), 0) == 0, jnp.broadcast_to(row, (SUB, LANES)), 0.0
        )


def final_kernel(
    sizes, cell_ref, p_in, s_in, mu_ref, wp_ref, ws_ref, plane_e, send_o, from_e, p_ref, s_ref, send_e
):
    rows = sizes.planes * sizes.ny
    even = lax.axis_index("gx") % 2 == 0

    @pl.loop(0, rows // SUB, unroll=8)
    def _(i):
        at = pl.ds(pl.multiple_of(i * SUB, SUB), SUB)
        come = pl.ds(pl.multiple_of(i * SUB + SUB, SUB), SUB)
        p_ref[at, :] = p_in[come, :]
        s_ref[at, :] = s_in[come, :]

    add_wells(sizes, cell_ref, mu_ref, wp_ref, ws_ref, p_ref, s_ref, 0)
    finish_core_plane(sizes, cell_ref, p_in, s_in, mu_ref, wp_ref, ws_ref, send_o, from_e, plane_e, send_e)
    put_planes(sizes, even, send_e, send_o, p_ref, s_ref, 0)


class Sizes:
    def __init__(self, planes, ny, groups, run, devices):
        self.planes, self.ny, self.groups, self.run, self.devices = planes, ny, groups, run, devices


def body(
    rhs_pressure,
    rhs_saturation,
    trans_x,
    trans_y,
    trans_z,
    coupling,
    upwind,
    storage,
    cross,
    accel,
    perf_cell,
    perf_well,
    perf_index,
    well_rhs,
    well_slot,
):
    planes, ny, nz = trans_x.shape
    devices = lax.axis_size("gx")
    groups = well_rhs.shape[0] // devices
    run = perf_cell.shape[0] // groups
    sizes = Sizes(planes, ny, groups, run, devices)
    rows = planes * ny
    padded = rows + 2 * SUB
    SMEM, VMEM, HBM, DMA = pltpu.SMEM, pltpu.VMEM, pltpu.HBM, pltpu.SemaphoreType.DMA

    def flat(array):
        return array.reshape(rows, nz)

    def lines(array):
        return array.reshape(-1, LANES)

    def call(kernel, args, spaces, outs, scratch, name, micros, aliases=None):
        return pl.pallas_call(
            kernel,
            in_specs=[spec(space) for space in spaces],
            out_specs=[spec(VMEM)] * len(outs),
            out_shape=outs,
            scratch_shapes=scratch,
            input_output_aliases=aliases or {},
            compiler_params=pltpu.CompilerParams(vmem_limit_bytes=16 * 1024 * 1024),
            cost_estimate=pl.CostEstimate(flops=int(micros * 4e6), bytes_accessed=int(micros * 3e6), transcendentals=0),
            name=name,
        )(*[placed(a, space) for a, space in zip(args, spaces)])

    def call_vmem(kernel, args, outs, scratch, name, micros, aliases=None):
        return call(
            functools.partial(kernel, sizes), [perf_cell] + args, [SMEM] + [VMEM] * len(args), outs, scratch,
            name, micros, aliases,
        )

    pairs_e = [(i, i ^ 1) for i in range(devices) if i ^ 1 < devices]
    pairs_o = []
    for i in range(1, devices - 1, 2):
        pairs_o += [(i, i + 1), (i + 1, i)]

    def to_core(block):
        return lax.ppermute(block, "gx", pairs_e)

    def to_chip(block):
        return lax.ppermute(block, "gx", pairs_o)

    tx = flat(trans_x)
    index = lines(perf_index)
    send, wells = call(
        functools.partial(first_kernel, sizes),
        [tx, lines(perf_well), index],
        [HBM, HBM, HBM],
        [vmem(ny + SUB), vmem(2 * groups)],
        [VMEM(index.shape, jnp.int32), VMEM(index.shape, F32), DMA((3,))],
        "first",
        1,
    )
    from_o = to_chip(send)
    from_e = to_core(send)
    big = [tx] + [
        flat(a)
        for a in (trans_y, trans_z, accel, coupling, upwind, storage, rhs_pressure, rhs_saturation, cross)
    ]
    made = call(
        functools.partial(setup_kernel, sizes),
        [perf_cell, perf_index] + big,
        [SMEM] + [HBM] * (1 + len(big)),
        [vmem(rows)] * 11 + [vmem(3 * ny), vmem(groups * SUB)],
        [
            VMEM((padded, LANES), F32),
            VMEM((rows, LANES), F32),
            VMEM((rows, LANES), F32),
            SMEM(perf_index.shape, F32),
            DMA((10,)),
            DMA,
        ],
        "setup",
        4,
    )
    coefficients, (extra, weight) = list(made[:11]), made[11:]
    group_row = VMEM((groups, LANES), F32)
    fields = [vmem(padded), vmem(padded)]
    block = vmem(2 * ny + SUB)
    slabs = vmem(groups * SUB)
    p, s, edge, plane_e, plane_o, wp, ws, shared, table, mu, parts, send_o = call(
        functools.partial(start_kernel, sizes),
        [perf_cell, from_o, from_e, wells, lines(well_rhs), lines(well_slot), coefficients[0]]
        + coefficients[5:]
        + [extra, weight],
        [SMEM] + [VMEM] * 3 + [HBM] * 2 + [VMEM] * 9,
        fields
        + [vmem(6 * ny), vmem(4 * ny), vmem(4 * ny), slabs, slabs, vmem(groups), vmem(TABLE * groups)]
        + [vmem(groups), vmem(2 * groups), block],
        [
            group_row,
            VMEM(lines(well_rhs).shape, F32),
            VMEM(lines(well_slot).shape, jnp.int32),
            DMA((2,)),
        ],
        "start",
        2,
    )
    near = None
    for sweep in range(1, SWEEPS):
        final = sweep == SWEEPS - 1
        next_o = to_chip(send_o)
        first = sweep == 1
        _, _, p, s, by_lane, send_e, *rest = call_vmem(
            lambda sz, *refs: inner_kernel(sz, first, *refs),
            [p, s, mu, wp, ws, weight, send_o] + coefficients + [edge, plane_e, plane_o if first else from_e],
            fields + fields + [vmem(groups), block] + ([vmem(4 * groups)] if first else []),
            [],
            "inner",
            2,
            {1: 0, 2: 1},
        )
        if first:
            near = rest[0]
        next_e = to_core(send_e)
        from_e, from_o = next_e, next_o
        half_o, sums = call_vmem(
            facing_kernel, [from_o, p, s, plane_o, near], [block, vmem(groups)], [], "facing", 0.5
        )
        send_o, mu, parts, *rest = call_vmem(
            lambda sz, *refs: outer_kernel(sz, final, *refs),
            [half_o, from_e, by_lane, sums, parts, table, wp, ws, shared, near],
            [block, vmem(groups), vmem(2 * groups)] + ([vmem(devices * SUB)] if final else []),
            [group_row],
            "outer",
            1,
            {1: 0},
        )
    grads = lax.all_to_all(rest[0].reshape(devices, SUB, LANES), "gx", 0, 0)
    p, s = call_vmem(
        final_kernel,
        [p, s, mu, wp, ws, plane_e, send_o, from_e],
        [vmem(rows), vmem(rows)],
        [VMEM((2 * ny + SUB, LANES), F32)],
        "final",
        2,
    )
    control = jnp.sum(grads, axis=(0, 1))[:groups]
    shape = trans_x.shape
    return p.reshape(shape), s.reshape(shape), control


def solution(mesh):
    grid = P(("ens", "gx"), None, None)
    line = P(("ens", "gx"))
    return jax.shard_map(
        body,
        mesh=mesh,
        in_specs=(grid,) * 10 + (line,) * 3 + (P("ens"), P("ens")),
        out_specs=(grid, grid, line),
        check_vma=False,
    )
```

time: 84.9 us -> 75.8 us (0.89)
  starting transfers between devices: 47.4 us -> 30.6 us
  Pallas kernels: 24.8 us -> 36.4 us
  waiting for transfers between devices: 7.23 us -> 4.78 us
  local copies, waits for them, and re-layouts: 3.7 us -> 2.27 us
    pallas_call x8 -> x19, Pallas kernels: 24.8 us -> 36.4 us  [call(): pl.pallas_call(kernel, in_specs=[spec(space) for space in spaces], out_sp...]
    ppermute x12, starting transfers between devices: 34.5 us -> 25.4 us  [the longest x6 21.2 us: to_core(): return lax.ppermute(block, 'gx', pairs_e)]
    all_to_all x1, starting transfers between devices: 12.9 us -> 5.28 us  [body(): grads = lax.all_to_all(rest[0].reshape(devices, SUB, LANES), 'gx', 0, 0)]
    slice x2 -> x0, local copies, waits for them, and re-layouts: 1.65 us -> none  [the longest x1 0.83 us: body(): p[SUB:SUB + rows].reshape(shape)]
    all_to_all x1, waiting for transfers between devices: 5.24 us -> 3.86 us  [body(): grads = lax.all_to_all(rest[0].reshape(devices, SUB, LANES), 'gx', 0, 0)]
    ppermute x12, waiting for transfers between devices: 1.99 us -> 0.92 us  [the longest x6 0.91 us: to_core(): return lax.ppermute(block, 'gx', pairs_e)]
    unnamed x10 -> x4, local copies, waits for them, and re-layouts: 2.04 us -> 2.27 us
  transfers between devices with their start and end apart: 13 -> 13, of which waited for: 6 -> 6; matrix products, arithmetic and copies ran while one was open for 2% -> 2% of each run, Pallas kernels for 6% -> 36%
where the time goes in v1:
time: 75.8 us; the launch traced here: 75.4 us
  Pallas kernels  36.4 us (48%)
  starting transfers between devices  30.6 us (40%)
  waiting for transfers between devices  4.78 us (6%)
  local copies, waits for them, and re-layouts  2.27 us (3%)
  between operations  0.82 us (1%)
    pallas_call x19, Pallas kernels, call(): pl.pallas_call(kernel, in_specs=[spec(space) for space in spaces], out_sp...  36.4 us
    ppermute x6, starting transfers between devices, to_core(): return lax.ppermute(block, 'gx', pairs_e)  21.2 us
    all_to_all x1, starting transfers between devices, body(): grads = lax.all_to_all(rest[0].reshape(devices, SUB, LANES), 'gx', 0, 0)  5.28 us
    ppermute x6, starting transfers between devices, to_chip(): return lax.ppermute(block, 'gx', pairs_o)  4.19 us
    all_to_all x1, waiting for transfers between devices, body(): grads = lax.all_to_all(rest[0].reshape(devices, SUB, LANES), 'gx', 0, 0)  3.86 us
    unnamed x4, local copies, waits for them, and re-layouts  2.27 us
  transfers between devices with their start and end apart: 13, of which 6 were waited for; matrix products, arithmetic and copies ran while one was open for 2% of the time, Pallas kernels for 36%

profile of v1, /device:TPU:0, one launch (start us, length us, event | category | flops | bytes accessed | tf_op | source)
XLA Modules:
  0.0 75.4 jit_solution(508260142378614683)
XLA Ops:
  0.6 0.9 %first.1 = (f32[136,128]{1,0:T(8,128)S(1)}, f32[64,128]{1,0:T(8,128)S(1)}) custom-call(f32[1024,128]{1,0:T(8,128)} %bitcast.20, s32[2,128]{1,0:T(2,128)} %bitcast.34, f32[2,128]{1,0:T(2,128)} %bitcast.31), custom_call_target="tpu_custom_call" | custom-call | flops 4000000 | bytes 3000000 | tf_op jit(solution)/shard_map/first/pallas_call | solution.py:692
  1.5 0.7 collective-permute-start
  2.2 4.4 %collective-permute-start.1 = (f32[136,128]{1,0:T(8,128)S(1)}, f32[136,128]{1,0:T(8,128)S(1)}, u32[]{:S(2)}, u32[]{:S(2)}) collective-permute-start(f32[136,128]{1,0:T(8,128)S(1)} %get-tuple-element.78), channel_id=1, source_target_pairs={{0,1},{1,0},{2,3},{3,2},{4,5},{5,4},{6,7},{7,6},{8,9},{9,8},{10,11... | collective-permute-start | bytes 208904 | tf_op jit(solution)/shard_map/ppermute | solution.py:716
  6.6 0.0 copy-start
  6.6 0.7 copy-done
  7.3 5.0 %setup.1 = (f32[1024,128]{1,0:T(8,128)S(1)}, f32[1024,128]{1,0:T(8,128)S(1)}, f32[1024,128]{1,0:T(8,128)S(1)}, f32[1024,128]{1,0:T(8,128)S(1)}, f32[1024,128]{1,...) custom-call(s32[256]{0:T(256)S(1)} %copy-done, ...), custom_call_target="tpu_custom_call" | custom-call | flops 16000000 | bytes 12000000 | tf_op jit(solution)/shard_map/setup/pallas_call | solution.py:692
  12.3 0.0 collective-permute-done.from_o
  12.3 0.0 collective-permute-done.1.from_e
  12.3 2.2 %start.1 = (f32[1040,128]{1,0:T(8,128)S(1)}, f32[1040,128]{1,0:T(8,128)S(1)}, f32[768,128]{1,0:T(8,128)S(1)}, f32[512,128]{1,0:T(8,128)S(1)}, f32[512,128]{1,0:T...) custom-call(s32[256]{0:T(256)S(1)} %copy-done, ...), custom_call_target="tpu_custom_call" | custom-call | flops 8000000 | bytes 6000000 | tf_op jit(solution)/shard_map/start/pallas_call | solution.py:692
  14.5 0.7 collective-permute-start.2
  15.2 3.6 %inner.5 = (f32[1040,128]{1,0:T(8,128)S(1)}, f32[1040,128]{1,0:T(8,128)S(1)}, f32[1040,128]{1,0:T(8,128)S(1)}, f32[1040,128]{1,0:T(8,128)S(1)}, f32[32,128]{1,0:...) custom-call(s32[256]{0:T(256)S(1)} %copy-done, ...), custom_call_target="tpu_custom_call", output_to_operand_aliasing={{0}: (1, {}), {1}: (2, {})} | custom-call | flops 8000000 | bytes 6000000 | tf_op jit(solution)/shard_map/inner/pallas_call | solution.py:692
  18.8 2.9 %collective-permute-start.3 = (f32[264,128]{1,0:T(8,128)S(1)}, f32[264,128]{1,0:T(8,128)S(1)}, u32[]{:S(2)}, u32[]{:S(2)}) collective-permute-start(f32[264,128]{1,0:T(8,128)S(1)} %get-tuple-element.106), channel_id=1, source_target_pairs={{0,1},{1,0},{2,3},{3,2},{4,5},{5,4},{6,7},{7,6},{8,9},{9,8},{10,11... | collective-permute-start | bytes 405512 | tf_op jit(solution)/shard_map/ppermute | solution.py:716
  21.7 0.0 collective-permute-done.2.from_o
  21.7 0.8 %facing.5 = (f32[264,128]{1,0:T(8,128)S(1)}, f32[32,128]{1,0:T(8,128)S(1)}) custom-call(s32[256]{0:T(256)S(1)} %copy-done, f32[264,128]{1,0:T(8,128)S(1)} %collective-permute-done.2.from_o, f32[1040,128]{1,0:T(8,128)S(1)} %get-tuple-element.102.p_ref.refs_1_, f32[1040,128]{1,0:T(8,128)S(1)} %get-tuple-element.103.s_ref.refs_2_, ...), custom_call_target="tpu_custom_call" | custom-call | flops 2000000 | bytes 1500000 | tf_op jit(solution)/shard_map/facing/pallas_call | solution.py:692
  22.6 0.2 collective-permute-done.3.refs_2_.refs_21_
  22.7 1.0 %outer.5 = (f32[264,128]{1,0:T(8,128)S(1)}, f32[32,128]{1,0:T(8,128)S(1)}, f32[64,128]{1,0:T(8,128)S(1)}) custom-call(s32[256]{0:T(256)S(1)} %copy-done, f32[264,128]{1,0:T(8,128)S(1)} %get-tuple-element.105.refs_1_, f32[264,128]{1,0:T(8,128)S(1)} %collective-permute-done.3.refs_2_.refs_21_, ...), custom_call_target="tpu_custom_call", output_to_operand_aliasing={{0}: (1, {})} | custom-call | flops 4000000 | bytes 3000000 | tf_op jit(solution)/shard_map/outer/pallas_call | solution.py:692
  23.8 0.7 collective-permute-start.4
  24.4 3.4 %inner.6 = (f32[1040,128]{1,0:T(8,128)S(1)}, f32[1040,128]{1,0:T(8,128)S(1)}, f32[1040,128]{1,0:T(8,128)S(1)}, f32[1040,128]{1,0:T(8,128)S(1)}, f32[32,128]{1,0:T(8,128)S(1)}, /*index=5*/f32[264,128]{1,0:T(8,128)S(1)}) custom-call(s32[256]{0:T(256)S(1)} %copy-done, ...), custom_call_target="tpu_custom_call", output_to_operand_aliasing={{0}: (1, {}), {1}: (2, {})} | custom-call | flops 8000000 | bytes 6000000 | tf_op jit(solution)/shard_map/inner/pallas_call | solution.py:692
  27.8 3.3 %collective-permute-start.5 = (f32[264,128]{1,0:T(8,128)S(1)}, f32[264,128]{1,0:T(8,128)S(1)}, u32[]{:S(2)}, u32[]{:S(2)}) collective-permute-start(f32[264,128]{1,0:T(8,128)S(1)} %get-tuple-element.117), channel_id=1, source_target_pairs={{0,1},{1,0},{2,3},{3,2},{4,5},{5,4},{6,7},{7,6},{8,9},{9,8},{10,11... | collective-permute-start | bytes 405512 | tf_op jit(solution)/shard_map/ppermute | solution.py:716
  31.1 0.0 collective-permute-done.4.from_o
  31.1 0.8 %facing.6 = (f32[264,128]{1,0:T(8,128)S(1)}, f32[32,128]{1,0:T(8,128)S(1)}) custom-call(s32[256]{0:T(256)S(1)} %copy-done, f32[264,128]{1,0:T(8,128)S(1)} %collective-permute-done.4.from_o, f32[1040,128]{1,0:T(8,128)S(1)} %get-tuple-element.114.p_ref.refs_1_, f32[1040,128]{1,0:T(8,128)S(1)} %get-tuple-element.115.s_ref.refs_2_, ...), custom_call_target="tpu_custom_call" | custom-call | flops 2000000 | bytes 1500000 | tf_op jit(solution)/shard_map/facing/pallas_call | solution.py:692
  32.0 0.2 collective-permute-done.5.refs_2_.refs_21_
  32.1 1.0 %outer.6 = (f32[264,128]{1,0:T(8,128)S(1)}, f32[32,128]{1,0:T(8,128)S(1)}, f32[64,128]{1,0:T(8,128)S(1)}) custom-call(s32[256]{0:T(256)S(1)} %copy-done, f32[264,128]{1,0:T(8,128)S(1)} %get-tuple-element.116.refs_1_, f32[264,128]{1,0:T(8,128)S(1)} %collective-permute-done.5.refs_2_.refs_21_, ...), custom_call_target="tpu_custom_call", output_to_operand_aliasing={{0}: (1, {})} | custom-call | flops 4000000 | bytes 3000000 | tf_op jit(solution)/shard_map/outer/pallas_call | solution.py:692
  33.2 0.7 collective-permute-start.6
  33.8 3.4 %inner.7 = (f32[1040,128]{1,0:T(8,128)S(1)}, f32[1040,128]{1,0:T(8,128)S(1)}, f32[1040,128]{1,0:T(8,128)S(1)}, f32[1040,128]{1,0:T(8,128)S(1)}, f32[32,128]{1,0:T(8,128)S(1)}, /*index=5*/f32[264,128]{1,0:T(8,128)S(1)}) custom-call(s32[256]{0:T(256)S(1)} %copy-done, ...), custom_call_target="tpu_custom_call", output_to_operand_aliasing={{0}: (1, {}), {1}: (2, {})} | custom-call | flops 8000000 | bytes 6000000 | tf_op jit(solution)/shard_map/inner/pallas_call | solution.py:692
  37.2 3.6 %collective-permute-start.7 = (f32[264,128]{1,0:T(8,128)S(1)}, f32[264,128]{1,0:T(8,128)S(1)}, u32[]{:S(2)}, u32[]{:S(2)}) collective-permute-start(f32[264,128]{1,0:T(8,128)S(1)} %get-tuple-element.126), channel_id=1, source_target_pairs={{0,1},{1,0},{2,3},{3,2},{4,5},{5,4},{6,7},{7,6},{8,9},{9,8},{10,11... | collective-permute-start | bytes 405512 | tf_op jit(solution)/shard_map/ppermute | solution.py:716
  40.8 0.0 collective-permute-done.6.from_o
  40.8 0.8 %facing.7 = (f32[264,128]{1,0:T(8,128)S(1)}, f32[32,128]{1,0:T(8,128)S(1)}) custom-call(s32[256]{0:T(256)S(1)} %copy-done, f32[264,128]{1,0:T(8,128)S(1)} %collective-permute-done.6.from_o, f32[1040,128]{1,0:T(8,128)S(1)} %get-tuple-element.123.p_ref.refs_1_, f32[1040,128]{1,0:T(8,128)S(1)} %get-tuple-element.124.s_ref.refs_2_, ...), custom_call_target="tpu_custom_call" | custom-call | flops 2000000 | bytes 1500000 | tf_op jit(solution)/shard_map/facing/pallas_call | solution.py:692
  41.6 0.2 collective-permute-done.7.refs_2_.refs_21_
  41.8 1.0 %outer.7 = (f32[264,128]{1,0:T(8,128)S(1)}, f32[32,128]{1,0:T(8,128)S(1)}, f32[64,128]{1,0:T(8,128)S(1)}) custom-call(s32[256]{0:T(256)S(1)} %copy-done, f32[264,128]{1,0:T(8,128)S(1)} %get-tuple-element.125.refs_1_, f32[264,128]{1,0:T(8,128)S(1)} %collective-permute-done.7.refs_2_.refs_21_, ...), custom_call_target="tpu_custom_call", output_to_operand_aliasing={{0}: (1, {})} | custom-call | flops 4000000 | bytes 3000000 | tf_op jit(solution)/shard_map/outer/pallas_call | solution.py:692
  42.8 0.8 %collective-permute-start.8 = (f32[264,128]{1,0:T(8,128)S(1)}, f32[264,128]{1,0:T(8,128)S(1)}, u32[]{:S(2)}, u32[]{:S(2)}) collective-permute-start(f32[264,128]{1,0:T(8,128)S(1)} %get-tuple-element.131.refs_7_), channel_id=1, source_target_pairs={{1,2},{2,1},{3,4},{4,3},{5,6},{6,5},{7,8},{8,7},{9,10},{10,9},{11,... | collective-permute-start | bytes 405512 | tf_op jit(solution)/shard_map/ppermute | solution.py:719
  43.7 3.4 %inner.8 = (f32[1040,128]{1,0:T(8,128)S(1)}, f32[1040,128]{1,0:T(8,128)S(1)}, f32[1040,128]{1,0:T(8,128)S(1)}, f32[1040,128]{1,0:T(8,128)S(1)}, f32[32,128]{1,0:T(8,128)S(1)}, /*index=5*/f32[264,128]{1,0:T(8,128)S(1)}) custom-call(s32[256]{0:T(256)S(1)} %copy-done, ...), custom_call_target="tpu_custom_call", output_to_operand_aliasing={{0}: (1, {}), {1}: (2, {})} | custom-call | flops 8000000 | bytes 6000000 | tf_op jit(solution)/shard_map/inner/pallas_call | solution.py:692
  47.0 3.6 %collective-permute-start.9 = (f32[264,128]{1,0:T(8,128)S(1)}, f32[264,128]{1,0:T(8,128)S(1)}, u32[]{:S(2)}, u32[]{:S(2)}) collective-permute-start(f32[264,128]{1,0:T(8,128)S(1)} %get-tuple-element.135), channel_id=1, source_target_pairs={{0,1},{1,0},{2,3},{3,2},{4,5},{5,4},{6,7},{7,6},{8,9},{9,8},{10,11... | collective-permute-start | bytes 405512 | tf_op jit(solution)/shard_map/ppermute | solution.py:716
  50.6 0.0 collective-permute-done.8.from_o
  50.6 0.8 %facing.8 = (f32[264,128]{1,0:T(8,128)S(1)}, f32[32,128]{1,0:T(8,128)S(1)}) custom-call(s32[256]{0:T(256)S(1)} %copy-done, f32[264,128]{1,0:T(8,128)S(1)} %collective-permute-done.8.from_o, f32[1040,128]{1,0:T(8,128)S(1)} %get-tuple-element.132.p_ref.refs_1_, f32[1040,128]{1,0:T(8,128)S(1)} %get-tuple-element.133.s_ref.refs_2_, ...), custom_call_target="tpu_custom_call" | custom-call | flops 2000000 | bytes 1500000 | tf_op jit(solution)/shard_map/facing/pallas_call | solution.py:692
  51.4 0.2 collective-permute-done.9.refs_2_.refs_21_
  51.6 1.0 %outer.8 = (f32[264,128]{1,0:T(8,128)S(1)}, f32[32,128]{1,0:T(8,128)S(1)}, f32[64,128]{1,0:T(8,128)S(1)}) custom-call(s32[256]{0:T(256)S(1)} %copy-done, f32[264,128]{1,0:T(8,128)S(1)} %get-tuple-element.134.refs_1_, f32[264,128]{1,0:T(8,128)S(1)} %collective-permute-done.9.refs_2_.refs_21_, ...), custom_call_target="tpu_custom_call", output_to_operand_aliasing={{0}: (1, {})} | custom-call | flops 4000000 | bytes 3000000 | tf_op jit(solution)/shard_map/outer/pallas_call | solution.py:692
  52.6 0.7 collective-permute-start.10
  53.3 3.4 %inner.9 = (f32[1040,128]{1,0:T(8,128)S(1)}, f32[1040,128]{1,0:T(8,128)S(1)}, f32[1040,128]{1,0:T(8,128)S(1)}, f32[1040,128]{1,0:T(8,128)S(1)}, f32[32,128]{1,0:T(8,128)S(1)}, /*index=5*/f32[264,128]{1,0:T(8,128)S(1)}) custom-call(s32[256]{0:T(256)S(1)} %copy-done, ...), custom_call_target="tpu_custom_call", output_to_operand_aliasing={{0}: (1, {}), {1}: (2, {})} | custom-call | flops 8000000 | bytes 6000000 | tf_op jit(solution)/shard_map/inner/pallas_call | solution.py:692
  56.7 3.4 %collective-permute-start.11 = (f32[264,128]{1,0:T(8,128)S(1)}, f32[264,128]{1,0:T(8,128)S(1)}, u32[]{:S(2)}, u32[]{:S(2)}) collective-permute-start(f32[264,128]{1,0:T(8,128)S(1)} %get-tuple-element.144), channel_id=1, source_target_pairs={{0,1},{1,0},{2,3},{3,2},{4,5},{5,4},{6,7},{7,6},{8,9},{9,8},{10,11... | collective-permute-start | bytes 405512 | tf_op jit(solution)/shard_map/ppermute | solution.py:716
  60.0 0.0 collective-permute-done.10.from_o
  60.0 0.8 %facing.9 = (f32[264,128]{1,0:T(8,128)S(1)}, f32[32,128]{1,0:T(8,128)S(1)}) custom-call(s32[256]{0:T(256)S(1)} %copy-done, f32[264,128]{1,0:T(8,128)S(1)} %collective-permute-done.10.from_o, f32[1040,128]{1,0:T(8,128)S(1)} %get-tuple-element.141.p_ref.p_in, f32[1040,128]{1,0:T(8,128)S(1)} %get-tuple-element.142.s_ref.s_in, ...), custom_call_target="tpu_custom_call" | custom-call | flops 2000000 | bytes 1500000 | tf_op jit(solution)/shard_map/facing/pallas_call | solution.py:692
  60.9 0.2 collective-permute-done.11.refs_2_.from_e
  61.0 1.7 %outer.9 = (f32[264,128]{1,0:T(8,128)S(1)}, f32[32,128]{1,0:T(8,128)S(1)}, f32[64,128]{1,0:T(8,128)}, f32[128,128]{1,0:T(8,128)}) custom-call(s32[256]{0:T(256)S(1)} %copy-done, f32[264,128]{1,0:T(8,128)S(1)} %get-tuple-element.143.refs_1_, f32[264,128]{1,0:T(8,128)S(1)} %collective-permute-done.11.refs_2_.from_e, ...), custom_call_target="tpu_custom_call", output_to_operand_aliasing={{0}: (1, {})} | custom-call | flops 4000000 | bytes 3000000 | tf_op jit(solution)/shard_map/outer/pallas_call | solution.py:692
  62.7 5.3 %all-to-all-start = ((f32[16,8,128]{2,1,0:T(8,128)}), f32[16,8,128]{2,1,0:T(8,128)S(1)}, u32[]{:S(2)}, u32[]{:S(2)}) async-start(f32[16,8,128]{2,1,0:T(8,128)} %bitcast.16), calls=%async_computation | async-start | bytes 131072 | tf_op jit(solution)/shard_map/all_to_all | solution.py:807
  68.0 1.4 %final.1 = (f32[1024,128]{1,0:T(8,128)S(1)}, f32[1024,128]{1,0:T(8,128)S(1)}) custom-call(s32[256]{0:T(256)S(1)} %copy-done, f32[1040,128]{1,0:T(8,128)S(1)} %get-tuple-element.141.p_ref.p_in, f32[1040,128]{1,0:T(8,128)S(1)} %get-tuple-element.142.s_ref.s_in, f32[32,128]{1,0:T(8,128)S(1)} %get-tuple-element.148.mu_ref, ...), custom_call_target="tpu_custom_call" | custom-call | flops 8000000 | bytes 6000000 | tf_op jit(solution)/shard_map/final/pallas_call | solution.py:692
  69.4 0.8 %copy.48 = f32[8,128,128]{2,1,0:T(8,128)} copy(f32[8,128,128]{2,1,0:T(8,128)S(1)} %bitcast.19) | data formatting | bytes 1048576
  70.2 0.8 %copy.49 = f32[8,128,128]{2,1,0:T(8,128)} copy(f32[8,128,128]{2,1,0:T(8,128)S(1)} %bitcast.18) | data formatting | bytes 1048576
  71.0 3.9 %all-to-all-done = f32[16,8,128]{2,1,0:T(8,128)S(1)} async-done(((f32[16,8,128]{2,1,0:T(8,128)}), f32[16,8,128]{2,1,0:T(8,128)S(1)}, u32[]{:S(2)}, u32[]{:S(2)}) %all-to-all-start) | async-done | bytes 65568 | tf_op jit(solution)/shard_map/all_to_all | solution.py:807
  74.9 0.5 reduce_sum.9
Async XLA Ops:
  1.5 10.7 %collective-permute-start = (f32[136,128]{1,0:T(8,128)S(1)}, f32[136,128]{1,0:T(8,128)S(1)}, u32[]{:S(2)}, u32[]{:S(2)}) collective-permute-start(f32[136,128]{1,0:T(8,128)S(1)} %get-tuple-element.78), channel_id=1, source_target_pairs={{1,2},{2,1},{3,4},{4,3},{5,6},{6,5},{7,8},{8,7},{9,10},{10,9},{11,... | collective-permute-start | bytes 208904 | tf_op jit(solution)/shard_map/ppermute | solution.py:719
  2.2 10.1 %collective-permute-start.1 = (f32[136,128]{1,0:T(8,128)S(1)}, f32[136,128]{1,0:T(8,128)S(1)}, u32[]{:S(2)}, u32[]{:S(2)}) collective-permute-start(f32[136,128]{1,0:T(8,128)S(1)} %get-tuple-element.78), channel_id=1, source_target_pairs={{0,1},{1,0},{2,3},{3,2},{4,5},{5,4},{6,7},{7,6},{8,9},{9,8},{10,11... | collective-permute-start | bytes 208904 | tf_op jit(solution)/shard_map/ppermute | solution.py:716
  6.6 0.7 copy-start
  14.5 7.2 %collective-permute-start.2 = (f32[264,128]{1,0:T(8,128)S(1)}, f32[264,128]{1,0:T(8,128)S(1)}, u32[]{:S(2)}, u32[]{:S(2)}) collective-permute-start(f32[264,128]{1,0:T(8,128)S(1)} %get-tuple-element.94.refs_7_), channel_id=1, source_target_pairs={{1,2},{2,1},{3,4},{4,3},{5,6},{6,5},{7,8},{8,7},{9,10},{10,9},{11,... | collective-permute-start | bytes 405512 | tf_op jit(solution)/shard_map/ppermute | solution.py:719
  18.8 3.9 %collective-permute-start.3 = (f32[264,128]{1,0:T(8,128)S(1)}, f32[264,128]{1,0:T(8,128)S(1)}, u32[]{:S(2)}, u32[]{:S(2)}) collective-permute-start(f32[264,128]{1,0:T(8,128)S(1)} %get-tuple-element.106), channel_id=1, source_target_pairs={{0,1},{1,0},{2,3},{3,2},{4,5},{5,4},{6,7},{7,6},{8,9},{9,8},{10,11... | collective-permute-start | bytes 405512 | tf_op jit(solution)/shard_map/ppermute | solution.py:716
  23.8 7.4 %collective-permute-start.4 = (f32[264,128]{1,0:T(8,128)S(1)}, f32[264,128]{1,0:T(8,128)S(1)}, u32[]{:S(2)}, u32[]{:S(2)}) collective-permute-start(f32[264,128]{1,0:T(8,128)S(1)} %get-tuple-element.113.refs_7_), channel_id=1, source_target_pairs={{1,2},{2,1},{3,4},{4,3},{5,6},{6,5},{7,8},{8,7},{9,10},{10,9},{11,... | collective-permute-start | bytes 405512 | tf_op jit(solution)/shard_map/ppermute | solution.py:719
  27.8 4.3 %collective-permute-start.5 = (f32[264,128]{1,0:T(8,128)S(1)}, f32[264,128]{1,0:T(8,128)S(1)}, u32[]{:S(2)}, u32[]{:S(2)}) collective-permute-start(f32[264,128]{1,0:T(8,128)S(1)} %get-tuple-element.117), channel_id=1, source_target_pairs={{0,1},{1,0},{2,3},{3,2},{4,5},{5,4},{6,7},{7,6},{8,9},{9,8},{10,11... | collective-permute-start | bytes 405512 | tf_op jit(solution)/shard_map/ppermute | solution.py:716
  33.2 7.6 %collective-permute-start.6 = (f32[264,128]{1,0:T(8,128)S(1)}, f32[264,128]{1,0:T(8,128)S(1)}, u32[]{:S(2)}, u32[]{:S(2)}) collective-permute-start(f32[264,128]{1,0:T(8,128)S(1)} %get-tuple-element.122.refs_7_), channel_id=1, source_target_pairs={{1,2},{2,1},{3,4},{4,3},{5,6},{6,5},{7,8},{8,7},{9,10},{10,9},{11,... | collective-permute-start | bytes 405512 | tf_op jit(solution)/shard_map/ppermute | solution.py:719
  37.2 4.6 %collective-permute-start.7 = (f32[264,128]{1,0:T(8,128)S(1)}, f32[264,128]{1,0:T(8,128)S(1)}, u32[]{:S(2)}, u32[]{:S(2)}) collective-permute-start(f32[264,128]{1,0:T(8,128)S(1)} %get-tuple-element.126), channel_id=1, source_target_pairs={{0,1},{1,0},{2,3},{3,2},{4,5},{5,4},{6,7},{7,6},{8,9},{9,8},{10,11... | collective-permute-start | bytes 405512 | tf_op jit(solution)/shard_map/ppermute | solution.py:716
  42.8 7.8 %collective-permute-start.8 = (f32[264,128]{1,0:T(8,128)S(1)}, f32[264,128]{1,0:T(8,128)S(1)}, u32[]{:S(2)}, u32[]{:S(2)}) collective-permute-start(f32[264,128]{1,0:T(8,128)S(1)} %get-tuple-element.131.refs_7_), channel_id=1, source_target_pairs={{1,2},{2,1},{3,4},{4,3},{5,6},{6,5},{7,8},{8,7},{9,10},{10,9},{11,... | collective-permute-start | bytes 405512 | tf_op jit(solution)/shard_map/ppermute | solution.py:719
  47.0 4.6 %collective-permute-start.9 = (f32[264,128]{1,0:T(8,128)S(1)}, f32[264,128]{1,0:T(8,128)S(1)}, u32[]{:S(2)}, u32[]{:S(2)}) collective-permute-start(f32[264,128]{1,0:T(8,128)S(1)} %get-tuple-element.135), channel_id=1, source_target_pairs={{0,1},{1,0},{2,3},{3,2},{4,5},{5,4},{6,7},{7,6},{8,9},{9,8},{10,11... | collective-permute-start | bytes 405512 | tf_op jit(solution)/shard_map/ppermute | solution.py:716
  52.6 7.4 %collective-permute-start.10 = (f32[264,128]{1,0:T(8,128)S(1)}, f32[264,128]{1,0:T(8,128)S(1)}, u32[]{:S(2)}, u32[]{:S(2)}) collective-permute-start(f32[264,128]{1,0:T(8,128)S(1)} %get-tuple-element.140.refs_7_), channel_id=1, source_target_pairs={{1,2},{2,1},{3,4},{4,3},{5,6},{6,5},{7,8},{8,7},{9,10},{10,9},{11,... | collective-permute-start | bytes 405512 | tf_op jit(solution)/shard_map/ppermute | solution.py:719
  56.7 4.4 %collective-permute-start.11 = (f32[264,128]{1,0:T(8,128)S(1)}, f32[264,128]{1,0:T(8,128)S(1)}, u32[]{:S(2)}, u32[]{:S(2)}) collective-permute-start(f32[264,128]{1,0:T(8,128)S(1)} %get-tuple-element.144), channel_id=1, source_target_pairs={{0,1},{1,0},{2,3},{3,2},{4,5},{5,4},{6,7},{7,6},{8,9},{9,8},{10,11... | collective-permute-start | bytes 405512 | tf_op jit(solution)/shard_map/ppermute | solution.py:716
  62.7 12.2 %all-to-all-start = ((f32[16,8,128]{2,1,0:T(8,128)}), f32[16,8,128]{2,1,0:T(8,128)S(1)}, u32[]{:S(2)}, u32[]{:S(2)}) async-start(f32[16,8,128]{2,1,0:T(8,128)} %bitcast.16), calls=%async_computation | async-start | bytes 131072 | tf_op jit(solution)/shard_map/all_to_all | solution.py:807

commit v2 on v1

--- a/solution.py
+++ b/solution.py
@@ -92,7 +92,7 @@
 
 def setup_kernel(
     sizes,
-    cell_ref,
+    cell_hbm,
     index_hbm,
     tx_hbm,
     ty_hbm,
@@ -117,18 +117,20 @@
     xx_ref,
     extra_ref,
     weight_ref,
+    y_ref,
     raw_ty,
     raw_storage,
     cwi_ref,
+    cell_ref,
     index_ref,
     sems,
-    index_sem,
+    fetch_sems,
 ):
     ny, planes, groups, run = sizes.ny, sizes.planes, sizes.groups, sizes.run
     rows = planes * ny
     moves = [
         (tx_hbm, tx_ref),
-        (ty_hbm, raw_ty.at[pl.ds(SUB, rows)]),
+        (ty_hbm, raw_ty),
         (tz_hbm, tz_ref),
         (accel_hbm, ip_ref),
         (coupling_hbm, cc_ref),
@@ -138,9 +140,19 @@
         (rhs_s_hbm, rs_ref),
         (cross_hbm, xx_ref),
     ]
-    copies = [pltpu.make_async_copy(src, dst, sems.at[i]) for i, (src, dst) in enumerate(moves)]
-    fetch = pltpu.make_async_copy(index_hbm, index_ref, index_sem)
-    fetch.start()
+    fetches = [
+        pltpu.make_async_copy(src, dst, fetch_sems.at[i])
+        for i, (src, dst) in enumerate(((cell_hbm, cell_ref), (index_hbm, index_ref)))
+    ]
+    for fetch in fetches:
+        fetch.start()
+    copies = []
+    for x in range(planes):
+        for i, (src, dst) in enumerate(moves):
+            to = x * ny + SUB if dst is raw_ty else x * ny
+            copies.append(
+                pltpu.make_async_copy(src.at[pl.ds(x * ny, ny)], dst.at[pl.ds(to, ny)], sems.at[x, i])
+            )
     for copy in copies:
         copy.start()
 
@@ -152,9 +164,11 @@
     def _(i):
         cwi_ref[pl.ds(pl.multiple_of(i * SUB, SUB), SUB), :] = zero
 
-    fetch.wait()
+    for fetch in fetches:
+        fetch.wait()
     spot = iota((SUB, LANES), 0) * LANES + iota((SUB, LANES), 1)
     for g in range(groups):
+        y_ref[g] = (cell_ref[g * run] // LANES) % ny
         weight = zero
         for k in range(g * run, (g + 1) * run):
             cell = cell_ref[k]
@@ -164,18 +178,16 @@
         slab = pl.ds((cell_ref[g * run] // LANES) % ny, planes, ny)
         cwi_ref[slab, :] = cwi_ref[slab, :] + weight
 
-    for copy in copies:
-        copy.wait()
-
     lane = iota((SUB, LANES), 1)
     sub = iota((SUB, LANES), 0)
-
-    @pl.loop(0, ny // SUB)
-    def _(r):
-        y0 = pl.multiple_of(r * SUB, SUB)
-        ypos = sub + y0
-        txl = None
-        for x in range(planes):
+    for x in range(planes):
+        for copy in copies[x * len(moves) : (x + 1) * len(moves)]:
+            copy.wait()
+
+        @pl.loop(0, ny // SUB, unroll=4)
+        def _(r):
+            y0 = pl.multiple_of(r * SUB, SUB)
+            ypos = sub + y0
             at = pl.ds(y0 + x * ny, SUB)
             tx = tx_ref[at, :]
             if x == planes - 1:
@@ -191,7 +203,7 @@
             tzl_ref[at, :] = tzl
             tsum = tx + ty + tyl + tz + tzl
             if x > 0:
-                tsum = tsum + txl
+                tsum = tsum + tx_ref[pl.ds(y0 + (x - 1) * ny, SUB), :]
             accel = ip_ref[at, :]
             coupling = cc_ref[at, :]
             upwind = uu_ref[at, :]
@@ -214,7 +226,6 @@
                 rs_ref[at, :] = rs_ref[at, :] * is_
                 uu_ref[at, :] = upwind * is_
                 xx_ref[at, :] = xx_ref[at, :] * is_
-            txl = tx
 
 
 def own_lanes(ref, place, groups):
@@ -233,7 +244,7 @@
 
 
 def path_y(sizes, cell_ref, g):
-    return (cell_ref[g * sizes.run] // LANES) % sizes.ny
+    return cell_ref[g]
 
 
 def slab_of(sizes, cell_ref, g, pad):
@@ -339,7 +350,7 @@
     shared_ref,
     table_ref,
     mu_ref,
-    parts_out,
+    sums_out,
     send_o,
     rows_ref,
     rhs_ref,
@@ -433,26 +444,20 @@
     finish_plane(sizes, x_o, p_ref, s_ref, None, None, send_o)
     add_wells_to_plane(sizes, cell_ref, mu_ref, wp_ref, ws_ref, x_o, send_o)
     path_rows(sizes, cell_ref, weight_ref, p_ref, rows_ref)
-    put_sums(sizes, before, rows_ref[...] + shared_ref[...] * row_of(mu, groups), parts_out, send_o)
-
-
-def put_sums(sizes, before, by_lane, parts_out, send_o):
+    put_sums(sizes, even, before, rows_ref[...] + shared_ref[...] * row_of(mu, groups), sums_out, send_o)
+
+
+def put_sums(sizes, to_before, before, by_lane, rows_out, send_ref):
     ny, groups = sizes.ny, sizes.groups
-    total = spread(lane_sum(by_lane), groups)
-    part_own, part_before = total * (1.0 - before), total * before
-    parts_out[0:groups, :] = part_own
-    parts_out[groups : 2 * groups, :] = part_before
-    send_o[2 * ny : 2 * ny + SUB, :] = well_block(part_own, part_before, groups)
-    return part_own, part_before
-
-
-def finish_core_plane(sizes, cell_ref, p_ref, s_ref, mu_ref, wp_ref, ws_ref, send_o, halo, plane_e, send_e):
+    rows_out[...] = by_lane
+    send_ref[2 * ny : 2 * ny + groups, :] = by_lane * jnp.where(to_before, before, 1.0 - before)
+
+
+def finish_core_plane(sizes, cell_ref, p_ref, s_ref, mu_ref, wp_ref, ws_ref, halo, plane_e, send_e):
     even = lax.axis_index("gx") % 2 == 0
     _, x_e = facing(sizes, even)
     finish_plane(sizes, x_e, p_ref, s_ref, halo, plane_e, send_e)
     add_wells_to_plane(sizes, cell_ref, mu_ref, wp_ref, ws_ref, x_e, send_e)
-    tail = slice(2 * sizes.ny, 2 * sizes.ny + SUB)
-    send_e[tail, :] = send_o[tail, :]
 
 
 def near_weights(sizes, cell_ref, weight_ref, plane_e, plane_o, near_ref):
@@ -489,6 +494,8 @@
     ws_ref,
     weight_ref,
     send_o,
+    sums_in,
+    table_ref,
     tx_ref,
     ty_ref,
     tyl_ref,
@@ -508,12 +515,14 @@
     rows = planes * ny
     even = lax.axis_index("gx") % 2 == 0
     if first:
-        plane_o, p_old, s_old, p_ref, s_ref, rows_ref, send_e, near_ref = refs
+        plane_o, p_old, s_old, p_ref, s_ref, rows_ref, sums_out, send_e, near_ref = refs
         halo = None
         near_weights(sizes, cell_ref, weight_ref, plane_e, plane_o, near_ref)
     else:
-        halo, p_old, s_old, p_ref, s_ref, rows_ref, send_e = refs
-    finish_core_plane(sizes, cell_ref, p_old, s_old, mu_ref, wp_ref, ws_ref, send_o, halo, plane_e, send_e)
+        halo, p_old, s_old, p_ref, s_ref, rows_ref, sums_out, send_e = refs
+    finish_core_plane(sizes, cell_ref, p_old, s_old, mu_ref, wp_ref, ws_ref, halo, plane_e, send_e)
+    before = table_ref[BEFORE * sizes.groups : (BEFORE + 1) * sizes.groups, :]
+    put_sums(sizes, jnp.logical_not(even), before, sums_in[...], sums_out, send_e)
     add_wells(sizes, cell_ref, mu_ref, wp_ref, ws_ref, p_old, s_old, SUB)
     put_planes(sizes, even, send_e, send_o, p_old, s_old, SUB)
 
@@ -560,7 +569,6 @@
     even = lax.axis_index("gx") % 2 == 0
     x_o, _ = facing(sizes, even)
     finish_plane(sizes, x_o, p_ref, s_ref, from_o, plane_o, send_o)
-    send_o[2 * sizes.ny :, :] = from_o[2 * sizes.ny :, :]
     near_sums(sizes, cell_ref, from_o, near_ref, 0, sums_ref)
 
 
@@ -580,10 +588,11 @@
     final,
     cell_ref,
     send_in,
+    from_o,
     from_e,
     rows_ref,
-    sums_ref,
-    parts_in,
+    near_o,
+    sums_in,
     table_ref,
     wp_ref,
     ws_ref,
@@ -591,31 +600,33 @@
     near_ref,
     send_o,
     mu_ref,
-    parts_out,
     *rest,
 ):
     ny, groups = sizes.ny, sizes.groups
-    near_rows = rest[-1]
+    near_e = rest[-1]
     even = lax.axis_index("gx") % 2 == 0
     x_o, _ = facing(sizes, even)
 
     def table(i):
         return table_ref[i * groups : (i + 1) * groups, :]
 
-    tile_e, tile_o = from_e[2 * ny : 2 * ny + SUB, :], send_o[2 * ny : 2 * ny + SUB, :]
-    low = jnp.where(even, tile_o, tile_e)
-    high = jnp.where(even, tile_e, tile_o)
+    tail = slice(2 * ny, 2 * ny + groups)
+    come_e, come_o = from_e[tail, :], from_o[tail, :]
+    low = jnp.where(even, come_o, come_e)
+    high = jnp.where(even, come_e, come_o)
     before = table(BEFORE)
-    total_own = parts_in[0:groups, :] + column_of(high[1:2, :], groups)
-    total_before = parts_in[groups : 2 * groups, :] + column_of(low[0:1, :], groups)
-    mu = (table(RHS) + jnp.where(before > 0.5, total_before, total_own)) * table(INV)
+    total = spread(lane_sum(sums_in[...] + jnp.where(before > 0.5, low, high)), groups)
+    mu = (table(RHS) + total) * table(INV)
     mu_ref[...] = mu
-    near_sums(sizes, cell_ref, from_e, near_ref, 1, near_rows)
-    by_lane = rows_ref[...] + sums_ref[...] + near_rows[...] + shared_ref[...] * row_of(mu, groups)
+    near_sums(sizes, cell_ref, from_e, near_ref, 1, near_e)
+    by_lane = rows_ref[...] + near_o[...] + near_e[...] + shared_ref[...] * row_of(mu, groups)
     add_wells_to_plane(sizes, cell_ref, mu_ref, wp_ref, ws_ref, x_o, send_o)
-    part_own, part_before = put_sums(sizes, before, by_lane, parts_out, send_o)
     if not final:
+        put_sums(sizes, even, before, by_lane, rest[0], send_o)
         return
+    total_own = spread(lane_sum(sums_in[...] * (1.0 - before) + high), groups)
+    total = spread(lane_sum(by_lane), groups)
+    part_own, part_before = total * (1.0 - before), total * before
     grads_ref = rest[0]
     mu_own = (table(RHS_OWN) + total_own) * table(INV_OWN)
     grad_own = mu_own * table(SUM_OWN) - part_own
@@ -634,21 +645,36 @@
 
 
 def final_kernel(
-    sizes, cell_ref, p_in, s_in, mu_ref, wp_ref, ws_ref, plane_e, send_o, from_e, p_ref, s_ref, send_e
+    sizes,
+    cell_ref,
+    p_in,
+    s_in,
+    mu_ref,
+    wp_ref,
+    ws_ref,
+    plane_e,
+    send_o,
+    from_e,
+    p_old,
+    s_old,
+    p_out,
+    s_out,
+    send_e,
+    sems,
 ):
     rows = sizes.planes * sizes.ny
     even = lax.axis_index("gx") % 2 == 0
-
-    @pl.loop(0, rows // SUB, unroll=8)
-    def _(i):
-        at = pl.ds(pl.multiple_of(i * SUB, SUB), SUB)
-        come = pl.ds(pl.multiple_of(i * SUB + SUB, SUB), SUB)
-        p_ref[at, :] = p_in[come, :]
-        s_ref[at, :] = s_in[come, :]
-
-    add_wells(sizes, cell_ref, mu_ref, wp_ref, ws_ref, p_ref, s_ref, 0)
-    finish_core_plane(sizes, cell_ref, p_in, s_in, mu_ref, wp_ref, ws_ref, send_o, from_e, plane_e, send_e)
-    put_planes(sizes, even, send_e, send_o, p_ref, s_ref, 0)
+    finish_core_plane(sizes, cell_ref, p_old, s_old, mu_ref, wp_ref, ws_ref, from_e, plane_e, send_e)
+    add_wells(sizes, cell_ref, mu_ref, wp_ref, ws_ref, p_old, s_old, SUB)
+    put_planes(sizes, even, send_e, send_o, p_old, s_old, SUB)
+    copies = [
+        pltpu.make_async_copy(field.at[pl.ds(SUB, rows)], out, sems.at[i])
+        for i, (field, out) in enumerate(((p_old, p_out), (s_old, s_out)))
+    ]
+    for copy in copies:
+        copy.start()
+    for copy in copies:
+        copy.wait()
 
 
 class Sizes:
@@ -692,7 +718,7 @@
         return pl.pallas_call(
             kernel,
             in_specs=[spec(space) for space in spaces],
-            out_specs=[spec(VMEM)] * len(outs),
+            out_specs=[spec(out.memory_space) for out in outs],
             out_shape=outs,
             scratch_shapes=scratch,
             input_output_aliases=aliases or {},
@@ -703,7 +729,7 @@
 
     def call_vmem(kernel, args, outs, scratch, name, micros, aliases=None):
         return call(
-            functools.partial(kernel, sizes), [perf_cell] + args, [SMEM] + [VMEM] * len(args), outs, scratch,
+            functools.partial(kernel, sizes), [y] + args, [SMEM] + [VMEM] * len(args), outs, scratch,
             name, micros, aliases,
         )
 
@@ -738,33 +764,34 @@
     made = call(
         functools.partial(setup_kernel, sizes),
         [perf_cell, perf_index] + big,
-        [SMEM] + [HBM] * (1 + len(big)),
-        [vmem(rows)] * 11 + [vmem(3 * ny), vmem(groups * SUB)],
+        [HBM] * (2 + len(big)),
+        [vmem(rows)] * 11 + [vmem(3 * ny), vmem(groups * SUB), SMEM((groups,), jnp.int32)],
         [
             VMEM((padded, LANES), F32),
             VMEM((rows, LANES), F32),
             VMEM((rows, LANES), F32),
+            SMEM(perf_cell.shape, jnp.int32),
             SMEM(perf_index.shape, F32),
-            DMA((10,)),
-            DMA,
+            DMA((planes, 10)),
+            DMA((2,)),
         ],
         "setup",
         4,
     )
-    coefficients, (extra, weight) = list(made[:11]), made[11:]
+    coefficients, (extra, weight, y) = list(made[:11]), made[11:]
     group_row = VMEM((groups, LANES), F32)
     fields = [vmem(padded), vmem(padded)]
-    block = vmem(2 * ny + SUB)
+    block = vmem(2 * ny + groups)
     slabs = vmem(groups * SUB)
-    p, s, edge, plane_e, plane_o, wp, ws, shared, table, mu, parts, send_o = call(
+    p, s, edge, plane_e, plane_o, wp, ws, shared, table, mu, sums, send_o = call(
         functools.partial(start_kernel, sizes),
-        [perf_cell, from_o, from_e, wells, lines(well_rhs), lines(well_slot), coefficients[0]]
+        [y, from_o, from_e, wells, lines(well_rhs), lines(well_slot), coefficients[0]]
         + coefficients[5:]
         + [extra, weight],
         [SMEM] + [VMEM] * 3 + [HBM] * 2 + [VMEM] * 9,
         fields
         + [vmem(6 * ny), vmem(4 * ny), vmem(4 * ny), slabs, slabs, vmem(groups), vmem(TABLE * groups)]
-        + [vmem(groups), vmem(2 * groups), block],
+        + [vmem(groups), vmem(groups), block],
         [
             group_row,
             VMEM(lines(well_rhs).shape, F32),
@@ -779,10 +806,10 @@
         final = sweep == SWEEPS - 1
         next_o = to_chip(send_o)
         first = sweep == 1
-        _, _, p, s, by_lane, send_e, *rest = call_vmem(
+        _, _, p, s, by_lane, sums, send_e, *rest = call_vmem(
             lambda sz, *refs: inner_kernel(sz, first, *refs),
-            [p, s, mu, wp, ws, weight, send_o] + coefficients + [edge, plane_e, plane_o if first else from_e],
-            fields + fields + [vmem(groups), block] + ([vmem(4 * groups)] if first else []),
+            [p, s, mu, wp, ws, weight, send_o, sums, table] + coefficients + [edge, plane_e, plane_o if first else from_e],
+            fields + fields + [vmem(groups), vmem(groups), block] + ([vmem(4 * groups)] if first else []),
             [],
             "inner",
             2,
@@ -792,26 +819,28 @@
             near = rest[0]
         next_e = to_core(send_e)
         from_e, from_o = next_e, next_o
-        half_o, sums = call_vmem(
+        half_o, near_o = call_vmem(
             facing_kernel, [from_o, p, s, plane_o, near], [block, vmem(groups)], [], "facing", 0.5
         )
-        send_o, mu, parts, *rest = call_vmem(
+        send_o, mu, sums = call_vmem(
             lambda sz, *refs: outer_kernel(sz, final, *refs),
-            [half_o, from_e, by_lane, sums, parts, table, wp, ws, shared, near],
-            [block, vmem(groups), vmem(2 * groups)] + ([vmem(devices * SUB)] if final else []),
+            [half_o, from_o, from_e, by_lane, near_o, sums, table, wp, ws, shared, near],
+            [block, vmem(groups), vmem(devices * SUB if final else groups)],
             [group_row],
             "outer",
             1,
             {1: 0},
         )
-    grads = lax.all_to_all(rest[0].reshape(devices, SUB, LANES), "gx", 0, 0)
-    p, s = call_vmem(
+    grads = lax.all_to_all(sums.reshape(devices, SUB, LANES), "gx", 0, 0)
+    result = pltpu.HBM((rows, nz), F32)
+    _, _, p, s = call_vmem(
         final_kernel,
         [p, s, mu, wp, ws, plane_e, send_o, from_e],
-        [vmem(rows), vmem(rows)],
-        [VMEM((2 * ny + SUB, LANES), F32)],
+        fields + [result, result],
+        [VMEM((2 * ny + groups, LANES), F32), DMA((2,))],
         "final",
         2,
+        {1: 0, 2: 1},
     )
     control = jnp.sum(grads, axis=(0, 1))[:groups]
     shape = trans_x.shape

time: 75.8 us -> 68.9 us (0.909)
  Pallas kernels: 36.4 us -> 25.4 us
  waiting for transfers between devices: 4.78 us -> 10.1 us
  local copies, waits for them, and re-layouts: 2.27 us -> 0 us
  starting transfers between devices: 30.6 us -> 31.6 us
    pallas_call x19, Pallas kernels: 36.4 us -> 25.4 us  [call(): pl.pallas_call(kernel, in_specs=[spec(space) for space in spaces], out_sp...]
    ppermute x6, waiting for transfers between devices: 0.91 us -> 4.69 us  [to_core(): return lax.ppermute(block, 'gx', pairs_e)]
    unnamed x4 -> x0, local copies, waits for them, and re-layouts: 2.27 us -> none
    all_to_all x1, waiting for transfers between devices: 3.86 us -> 5.39 us  [body(): grads = lax.all_to_all(sums.reshape(devices, SUB, LANES), 'gx', 0, 0)]
    ppermute x6, starting transfers between devices: 21.2 us -> 22.3 us  [to_core(): return lax.ppermute(block, 'gx', pairs_e)]
  transfers between devices with their start and end apart: 13 -> 13, of which waited for: 6 -> 6; matrix products, arithmetic and copies ran while one was open for 2% -> 0% of each run, Pallas kernels for 36% -> 31%
where the time goes in v2:
time: 68.9 us; the launch traced here: 68.5 us
  starting transfers between devices  31.6 us (46%)
  Pallas kernels  25.4 us (37%)
  waiting for transfers between devices  10.1 us (15%)
  between operations  0.8 us (1%)
    pallas_call x19, Pallas kernels, call(): pl.pallas_call(kernel, in_specs=[spec(space) for space in spaces], out_sp...  25.4 us
    ppermute x6, starting transfers between devices, to_core(): return lax.ppermute(block, 'gx', pairs_e)  22.3 us
    all_to_all x1, waiting for transfers between devices, body(): grads = lax.all_to_all(sums.reshape(devices, SUB, LANES), 'gx', 0, 0)  5.39 us
    all_to_all x1, starting transfers between devices, body(): grads = lax.all_to_all(sums.reshape(devices, SUB, LANES), 'gx', 0, 0)  5.33 us
    ppermute x6, waiting for transfers between devices, to_core(): return lax.ppermute(block, 'gx', pairs_e)  4.69 us
    ppermute x6, starting transfers between devices, to_chip(): return lax.ppermute(block, 'gx', pairs_o)  4.02 us
  transfers between devices with their start and end apart: 13, of which 6 were waited for; matrix products, arithmetic and copies ran while one was open for 0% of the time, Pallas kernels for 31%

profile of v2, /device:TPU:0, one launch (start us, length us, event | category | flops | bytes accessed | tf_op | source)
XLA Modules:
  0.0 68.5 jit_solution(12732737624513290885)
XLA Ops:
  0.6 0.9 %first.1 = (f32[136,128]{1,0:T(8,128)S(1)}, f32[64,128]{1,0:T(8,128)S(1)}) custom-call(f32[1024,128]{1,0:T(8,128)} %bitcast.18, s32[2,128]{1,0:T(2,128)} %bitcast.32, f32[2,128]{1,0:T(2,128)} %bitcast.29), custom_call_target="tpu_custom_call" | custom-call | flops 4000000 | bytes 3000000 | tf_op jit(solution)/shard_map/first/pallas_call | solution.py:718
  1.5 0.7 collective-permute-start
  2.2 4.4 %collective-permute-start.1 = (f32[136,128]{1,0:T(8,128)S(1)}, f32[136,128]{1,0:T(8,128)S(1)}, u32[]{:S(2)}, u32[]{:S(2)}) collective-permute-start(f32[136,128]{1,0:T(8,128)S(1)} %get-tuple-element.85), channel_id=1, source_target_pairs={{0,1},{1,0},{2,3},{3,2},{4,5},{5,4},{6,7},{7,6},{8,9},{9,8},{10,11... | collective-permute-start | bytes 208904 | tf_op jit(solution)/shard_map/ppermute | solution.py:742
  6.6 6.5 %setup.1 = (f32[1024,128]{1,0:T(8,128)S(1)}, f32[1024,128]{1,0:T(8,128)S(1)}, f32[1024,128]{1,0:T(8,128)S(1)}, f32[1024,128]{1,0:T(8,128)S(1)}, f32[1024,128]{1,...) custom-call(s32[256]{0:T(256)} %cell_hbm.1, ...), custom_call_target="tpu_custom_call" | custom-call | flops 16000000 | bytes 12000000 | tf_op jit(solution)/shard_map/setup/pallas_call | solution.py:718
  13.1 0.0 collective-permute-done.from_o
  13.1 0.0 collective-permute-done.1.from_e
  13.2 1.4 %start.1 = (f32[1040,128]{1,0:T(8,128)S(1)}, f32[1040,128]{1,0:T(8,128)S(1)}, f32[768,128]{1,0:T(8,128)S(1)}, f32[512,128]{1,0:T(8,128)S(1)}, f32[512,128]{1,0:T...) custom-call(s32[32]{0:T(128)S(4)} %get-tuple-element.84.cell_ref.ref, ...), custom_call_target="tpu_custom_call" | custom-call | flops 8000000 | bytes 6000000 | tf_op jit(solution)/shard_map/start/pallas_call | solution.py:718
  14.6 0.7 collective-permute-start.2
  15.2 2.7 %inner.5 = (f32[1040,128]{1,0:T(8,128)S(1)}, f32[1040,128]{1,0:T(8,128)S(1)}, f32[1040,128]{1,0:T(8,128)S(1)}, f32[1040,128]{1,0:T(8,128)S(1)}, f32[32,128]{1,0:...) custom-call(s32[32]{0:T(128)S(4)} %get-tuple-element.84.cell_ref.ref, ...), custom_call_target="tpu_custom_call", output_to_operand_aliasing={{0}: (1, {}), {1}: (2, {})} | custom-call | flops 8000000 | bytes 6000000 | tf_op jit(solution)/shard_map/inner/pallas_call | solution.py:718
  18.0 2.9 %collective-permute-start.3 = (f32[288,128]{1,0:T(8,128)S(1)}, f32[288,128]{1,0:T(8,128)S(1)}, u32[]{:S(2)}, u32[]{:S(2)}) collective-permute-start(f32[288,128]{1,0:T(8,128)S(1)} %get-tuple-element.115), channel_id=1, source_target_pairs={{0,1},{1,0},{2,3},{3,2},{4,5},{5,4},{6,7},{7,6},{8,9},{9,8},{10,11... | collective-permute-start | bytes 442376 | tf_op jit(solution)/shard_map/ppermute | solution.py:742
  20.9 0.0 collective-permute-done.2.from_o.refs_2_
  20.9 0.1 facing.5
  21.0 0.9 %collective-permute-done.3.refs_3_.refs_23_ = f32[288,128]{1,0:T(8,128)S(1)} collective-permute-done((f32[288,128]{1,0:T(8,128)S(1)}, f32[288,128]{1,0:T(8,128)S(1)}, u32[]{:S(2)}, u32[]{:S(2)}) %collective-permute-start.3) | collective-permute-done | bytes 147488 | tf_op jit(solution)/shard_map/ppermute | solution.py:742
  21.9 0.2 outer.5
  22.2 0.7 collective-permute-start.4
  22.8 2.5 %inner.6 = (f32[1040,128]{1,0:T(8,128)S(1)}, f32[1040,128]{1,0:T(8,128)S(1)}, f32[1040,128]{1,0:T(8,128)S(1)}, f32[1040,128]{1,0:T(8,128)S(1)}, f32[32,128]{1,0:...) custom-call(s32[32]{0:T(128)S(4)} %get-tuple-element.84.cell_ref.refs_0, ...), custom_call_target="tpu_custom_call", output_to_operand_aliasing={{0}: (1, {}), {1}: (2, {})} | custom-call | flops 8000000 | bytes 6000000 | tf_op jit(solution)/shard_map/inner/pallas_call | solution.py:718
  25.4 3.7 %collective-permute-start.5 = (f32[288,128]{1,0:T(8,128)S(1)}, f32[288,128]{1,0:T(8,128)S(1)}, u32[]{:S(2)}, u32[]{:S(2)}) collective-permute-start(f32[288,128]{1,0:T(8,128)S(1)} %get-tuple-element.126), channel_id=1, source_target_pairs={{0,1},{1,0},{2,3},{3,2},{4,5},{5,4},{6,7},{7,6},{8,9},{9,8},{10,11... | collective-permute-start | bytes 442376 | tf_op jit(solution)/shard_map/ppermute | solution.py:742
  29.1 0.0 collective-permute-done.4.from_o.refs_2_
  29.1 0.1 facing.6
  29.2 0.9 %collective-permute-done.5.refs_3_.refs_23_ = f32[288,128]{1,0:T(8,128)S(1)} collective-permute-done((f32[288,128]{1,0:T(8,128)S(1)}, f32[288,128]{1,0:T(8,128)S(1)}, u32[]{:S(2)}, u32[]{:S(2)}) %collective-permute-start.5) | collective-permute-done | bytes 147488 | tf_op jit(solution)/shard_map/ppermute | solution.py:742
  30.1 0.2 outer.6
  30.4 0.7 collective-permute-start.6
  31.0 2.6 %inner.7 = (f32[1040,128]{1,0:T(8,128)S(1)}, f32[1040,128]{1,0:T(8,128)S(1)}, f32[1040,128]{1,0:T(8,128)S(1)}, f32[1040,128]{1,0:T(8,128)S(1)}, f32[32,128]{1,0:...) custom-call(s32[32]{0:T(128)S(4)} %get-tuple-element.84.cell_ref.refs_0, ...), custom_call_target="tpu_custom_call", output_to_operand_aliasing={{0}: (1, {}), {1}: (2, {})} | custom-call | flops 8000000 | bytes 6000000 | tf_op jit(solution)/shard_map/inner/pallas_call | solution.py:718
  33.7 3.9 %collective-permute-start.7 = (f32[288,128]{1,0:T(8,128)S(1)}, f32[288,128]{1,0:T(8,128)S(1)}, u32[]{:S(2)}, u32[]{:S(2)}) collective-permute-start(f32[288,128]{1,0:T(8,128)S(1)} %get-tuple-element.136), channel_id=1, source_target_pairs={{0,1},{1,0},{2,3},{3,2},{4,5},{5,4},{6,7},{7,6},{8,9},{9,8},{10,11... | collective-permute-start | bytes 442376 | tf_op jit(solution)/shard_map/ppermute | solution.py:742
  37.6 0.0 collective-permute-done.6.from_o.refs_2_
  37.6 0.1 facing.7
  37.7 0.9 %collective-permute-done.7.refs_3_.refs_23_ = f32[288,128]{1,0:T(8,128)S(1)} collective-permute-done((f32[288,128]{1,0:T(8,128)S(1)}, f32[288,128]{1,0:T(8,128)S(1)}, u32[]{:S(2)}, u32[]{:S(2)}) %collective-permute-start.7) | collective-permute-done | bytes 147488 | tf_op jit(solution)/shard_map/ppermute | solution.py:742
  38.6 0.2 outer.7
  38.8 0.7 collective-permute-start.8
  39.5 2.5 %inner.8 = (f32[1040,128]{1,0:T(8,128)S(1)}, f32[1040,128]{1,0:T(8,128)S(1)}, f32[1040,128]{1,0:T(8,128)S(1)}, f32[1040,128]{1,0:T(8,128)S(1)}, f32[32,128]{1,0:...) custom-call(s32[32]{0:T(128)S(4)} %get-tuple-element.84.cell_ref.refs_0, ...), custom_call_target="tpu_custom_call", output_to_operand_aliasing={{0}: (1, {}), {1}: (2, {})} | custom-call | flops 8000000 | bytes 6000000 | tf_op jit(solution)/shard_map/inner/pallas_call | solution.py:718
  42.1 3.8 %collective-permute-start.9 = (f32[288,128]{1,0:T(8,128)S(1)}, f32[288,128]{1,0:T(8,128)S(1)}, u32[]{:S(2)}, u32[]{:S(2)}) collective-permute-start(f32[288,128]{1,0:T(8,128)S(1)} %get-tuple-element.146), channel_id=1, source_target_pairs={{0,1},{1,0},{2,3},{3,2},{4,5},{5,4},{6,7},{7,6},{8,9},{9,8},{10,11... | collective-permute-start | bytes 442376 | tf_op jit(solution)/shard_map/ppermute | solution.py:742
  45.9 0.0 collective-permute-done.8.from_o.refs_2_
  45.9 0.1 facing.8
  45.9 0.9 %collective-permute-done.9.refs_3_.refs_23_ = f32[288,128]{1,0:T(8,128)S(1)} collective-permute-done((f32[288,128]{1,0:T(8,128)S(1)}, f32[288,128]{1,0:T(8,128)S(1)}, u32[]{:S(2)}, u32[]{:S(2)}) %collective-permute-start.9) | collective-permute-done | bytes 147488 | tf_op jit(solution)/shard_map/ppermute | solution.py:742
  46.9 0.2 outer.8
  47.1 0.7 collective-permute-start.10
  47.8 2.5 %inner.9 = (f32[1040,128]{1,0:T(8,128)S(1)}, f32[1040,128]{1,0:T(8,128)S(1)}, f32[1040,128]{1,0:T(8,128)S(1)}, f32[1040,128]{1,0:T(8,128)S(1)}, f32[32,128]{1,0:...) custom-call(s32[32]{0:T(128)S(4)} %get-tuple-element.84.cell_ref.refs_0, ...), custom_call_target="tpu_custom_call", output_to_operand_aliasing={{0}: (1, {}), {1}: (2, {})} | custom-call | flops 8000000 | bytes 6000000 | tf_op jit(solution)/shard_map/inner/pallas_call | solution.py:718
  50.3 3.5 %collective-permute-start.11 = (f32[288,128]{1,0:T(8,128)S(1)}, f32[288,128]{1,0:T(8,128)S(1)}, u32[]{:S(2)}, u32[]{:S(2)}) collective-permute-start(f32[288,128]{1,0:T(8,128)S(1)} %get-tuple-element.156), channel_id=1, source_target_pairs={{0,1},{1,0},{2,3},{3,2},{4,5},{5,4},{6,7},{7,6},{8,9},{9,8},{10,11... | collective-permute-start | bytes 442376 | tf_op jit(solution)/shard_map/ppermute | solution.py:742
  53.8 0.0 collective-permute-done.10.from_o.refs_2_
  53.8 0.1 facing.9
  53.9 0.9 %collective-permute-done.11.refs_3_.from_e = f32[288,128]{1,0:T(8,128)S(1)} collective-permute-done((f32[288,128]{1,0:T(8,128)S(1)}, f32[288,128]{1,0:T(8,128)S(1)}, u32[]{:S(2)}, u32[]{:S(2)}) %collective-permute-start.11) | collective-permute-done | bytes 147488 | tf_op jit(solution)/shard_map/ppermute | solution.py:742
  54.8 0.9 %outer.9 = (f32[288,128]{1,0:T(8,128)S(1)}, f32[32,128]{1,0:T(8,128)S(1)}, f32[128,128]{1,0:T(8,128)}) custom-call(s32[32]{0:T(128)S(4)} %get-tuple-element.84.cell_ref.refs_0_, f32[288,128]{1,0:T(8,128)S(1)} %get-tuple-element.155.refs_1_, f32[288,128]{1,0:T(8,128)S(1)} %collective-permute-done.10.from_o.refs_2_, ...), custom_call_target="tpu_custom_call", output_to_operand_aliasing={{0}: (1, {})} | custom-call | flops 4000000 | bytes 3000000 | tf_op jit(solution)/shard_map/outer/pallas_call | solution.py:718
  55.7 5.3 %all-to-all-start = ((f32[16,8,128]{2,1,0:T(8,128)}), f32[16,8,128]{2,1,0:T(8,128)S(1)}, u32[]{:S(2)}, u32[]{:S(2)}) async-start(f32[16,8,128]{2,1,0:T(8,128)} %bitcast.16), calls=%async_computation | async-start | bytes 131072 | tf_op jit(solution)/shard_map/all_to_all | solution.py:834
  61.1 1.5 %final.1 = (f32[1040,128]{1,0:T(8,128)S(1)}, f32[1040,128]{1,0:T(8,128)S(1)}, f32[1024,128]{1,0:T(8,128)}, f32[1024,128]{1,0:T(8,128)}) custom-call(s32[32]{0:T(128)S(4)} %get-tuple-element.84.cell_ref.refs_0_, f32[1040,128]{1,0:T(8,128)S(1)} %get-tuple-element.153.p_ref.p_in, ...), custom_call_target="tpu_custom_call", output_to_operand_aliasing={{0}: (1, {}), {1}: (2, {})} | custom-call | flops 8000000 | bytes 6000000 | tf_op jit(solution)/shard_map/final/pallas_call | solution.py:718
  62.6 5.4 %all-to-all-done = f32[16,8,128]{2,1,0:T(8,128)S(1)} async-done(((f32[16,8,128]{2,1,0:T(8,128)}), f32[16,8,128]{2,1,0:T(8,128)S(1)}, u32[]{:S(2)}, u32[]{:S(2)}) %all-to-all-start) | async-done | bytes 65568 | tf_op jit(solution)/shard_map/all_to_all | solution.py:834
  68.0 0.5 reduce_sum.9
Async XLA Ops:
  1.5 11.6 %collective-permute-start = (f32[136,128]{1,0:T(8,128)S(1)}, f32[136,128]{1,0:T(8,128)S(1)}, u32[]{:S(2)}, u32[]{:S(2)}) collective-permute-start(f32[136,128]{1,0:T(8,128)S(1)} %get-tuple-element.85), channel_id=1, source_target_pairs={{1,2},{2,1},{3,4},{4,3},{5,6},{6,5},{7,8},{8,7},{9,10},{10,9},{11,... | collective-permute-start | bytes 208904 | tf_op jit(solution)/shard_map/ppermute | solution.py:745
  2.2 10.9 %collective-permute-start.1 = (f32[136,128]{1,0:T(8,128)S(1)}, f32[136,128]{1,0:T(8,128)S(1)}, u32[]{:S(2)}, u32[]{:S(2)}) collective-permute-start(f32[136,128]{1,0:T(8,128)S(1)} %get-tuple-element.85), channel_id=1, source_target_pairs={{0,1},{1,0},{2,3},{3,2},{4,5},{5,4},{6,7},{7,6},{8,9},{9,8},{10,11... | collective-permute-start | bytes 208904 | tf_op jit(solution)/shard_map/ppermute | solution.py:742
  14.6 6.3 %collective-permute-start.2 = (f32[288,128]{1,0:T(8,128)S(1)}, f32[288,128]{1,0:T(8,128)S(1)}, u32[]{:S(2)}, u32[]{:S(2)}) collective-permute-start(f32[288,128]{1,0:T(8,128)S(1)} %get-tuple-element.101.refs_7_), channel_id=1, source_target_pairs={{1,2},{2,1},{3,4},{4,3},{5,6},{6,5},{7,8},{8,7},{9,10},{10,9},{11,... | collective-permute-start | bytes 442376 | tf_op jit(solution)/shard_map/ppermute | solution.py:745
  18.0 3.9 %collective-permute-start.3 = (f32[288,128]{1,0:T(8,128)S(1)}, f32[288,128]{1,0:T(8,128)S(1)}, u32[]{:S(2)}, u32[]{:S(2)}) collective-permute-start(f32[288,128]{1,0:T(8,128)S(1)} %get-tuple-element.115), channel_id=1, source_target_pairs={{0,1},{1,0},{2,3},{3,2},{4,5},{5,4},{6,7},{7,6},{8,9},{9,8},{10,11... | collective-permute-start | bytes 442376 | tf_op jit(solution)/shard_map/ppermute | solution.py:742
  22.2 6.9 %collective-permute-start.4 = (f32[288,128]{1,0:T(8,128)S(1)}, f32[288,128]{1,0:T(8,128)S(1)}, u32[]{:S(2)}, u32[]{:S(2)}) collective-permute-start(f32[288,128]{1,0:T(8,128)S(1)} %get-tuple-element.121.refs_7_), channel_id=1, source_target_pairs={{1,2},{2,1},{3,4},{4,3},{5,6},{6,5},{7,8},{8,7},{9,10},{10,9},{11,... | collective-permute-start | bytes 442376 | tf_op jit(solution)/shard_map/ppermute | solution.py:745
  25.4 4.7 %collective-permute-start.5 = (f32[288,128]{1,0:T(8,128)S(1)}, f32[288,128]{1,0:T(8,128)S(1)}, u32[]{:S(2)}, u32[]{:S(2)}) collective-permute-start(f32[288,128]{1,0:T(8,128)S(1)} %get-tuple-element.126), channel_id=1, source_target_pairs={{0,1},{1,0},{2,3},{3,2},{4,5},{5,4},{6,7},{7,6},{8,9},{9,8},{10,11... | collective-permute-start | bytes 442376 | tf_op jit(solution)/shard_map/ppermute | solution.py:742
  30.4 7.2 %collective-permute-start.6 = (f32[288,128]{1,0:T(8,128)S(1)}, f32[288,128]{1,0:T(8,128)S(1)}, u32[]{:S(2)}, u32[]{:S(2)}) collective-permute-start(f32[288,128]{1,0:T(8,128)S(1)} %get-tuple-element.131.refs_7_), channel_id=1, source_target_pairs={{1,2},{2,1},{3,4},{4,3},{5,6},{6,5},{7,8},{8,7},{9,10},{10,9},{11,... | collective-permute-start | bytes 442376 | tf_op jit(solution)/shard_map/ppermute | solution.py:745
  33.7 4.9 %collective-permute-start.7 = (f32[288,128]{1,0:T(8,128)S(1)}, f32[288,128]{1,0:T(8,128)S(1)}, u32[]{:S(2)}, u32[]{:S(2)}) collective-permute-start(f32[288,128]{1,0:T(8,128)S(1)} %get-tuple-element.136), channel_id=1, source_target_pairs={{0,1},{1,0},{2,3},{3,2},{4,5},{5,4},{6,7},{7,6},{8,9},{9,8},{10,11... | collective-permute-start | bytes 442376 | tf_op jit(solution)/shard_map/ppermute | solution.py:742
  38.8 7.0 %collective-permute-start.8 = (f32[288,128]{1,0:T(8,128)S(1)}, f32[288,128]{1,0:T(8,128)S(1)}, u32[]{:S(2)}, u32[]{:S(2)}) collective-permute-start(f32[288,128]{1,0:T(8,128)S(1)} %get-tuple-element.141.refs_7_), channel_id=1, source_target_pairs={{1,2},{2,1},{3,4},{4,3},{5,6},{6,5},{7,8},{8,7},{9,10},{10,9},{11,... | collective-permute-start | bytes 442376 | tf_op jit(solution)/shard_map/ppermute | solution.py:745
  42.1 4.8 %collective-permute-start.9 = (f32[288,128]{1,0:T(8,128)S(1)}, f32[288,128]{1,0:T(8,128)S(1)}, u32[]{:S(2)}, u32[]{:S(2)}) collective-permute-start(f32[288,128]{1,0:T(8,128)S(1)} %get-tuple-element.146), channel_id=1, source_target_pairs={{0,1},{1,0},{2,3},{3,2},{4,5},{5,4},{6,7},{7,6},{8,9},{9,8},{10,11... | collective-permute-start | bytes 442376 | tf_op jit(solution)/shard_map/ppermute | solution.py:742
  47.1 6.7 %collective-permute-start.10 = (f32[288,128]{1,0:T(8,128)S(1)}, f32[288,128]{1,0:T(8,128)S(1)}, u32[]{:S(2)}, u32[]{:S(2)}) collective-permute-start(f32[288,128]{1,0:T(8,128)S(1)} %get-tuple-element.151.refs_7_), channel_id=1, source_target_pairs={{1,2},{2,1},{3,4},{4,3},{5,6},{6,5},{7,8},{8,7},{9,10},{10,9},{11,... | collective-permute-start | bytes 442376 | tf_op jit(solution)/shard_map/ppermute | solution.py:745
  50.3 4.5 %collective-permute-start.11 = (f32[288,128]{1,0:T(8,128)S(1)}, f32[288,128]{1,0:T(8,128)S(1)}, u32[]{:S(2)}, u32[]{:S(2)}) collective-permute-start(f32[288,128]{1,0:T(8,128)S(1)} %get-tuple-element.156), channel_id=1, source_target_pairs={{0,1},{1,0},{2,3},{3,2},{4,5},{5,4},{6,7},{7,6},{8,9},{9,8},{10,11... | collective-permute-start | bytes 442376 | tf_op jit(solution)/shard_map/ppermute | solution.py:742
  55.7 12.2 %all-to-all-start = ((f32[16,8,128]{2,1,0:T(8,128)}), f32[16,8,128]{2,1,0:T(8,128)S(1)}, u32[]{:S(2)}, u32[]{:S(2)}) async-start(f32[16,8,128]{2,1,0:T(8,128)} %bitcast.16), calls=%async_computation | async-start | bytes 131072 | tf_op jit(solution)/shard_map/all_to_all | solution.py:834

commit v3 on v2

--- a/solution.py
+++ b/solution.py
@@ -11,6 +11,7 @@
 SUB = 8
 LANES = 128
 F32 = jnp.float32
+CHUNKS = 4
 
 
 def vmem(rows):
@@ -118,8 +119,16 @@
     extra_ref,
     weight_ref,
     y_ref,
+    raw_tx,
     raw_ty,
+    raw_tz,
+    raw_accel,
+    raw_coupling,
+    raw_upwind,
     raw_storage,
+    raw_rhs_p,
+    raw_rhs_s,
+    raw_cross,
     cwi_ref,
     cell_ref,
     index_ref,
@@ -128,33 +137,39 @@
 ):
     ny, planes, groups, run = sizes.ny, sizes.planes, sizes.groups, sizes.run
     rows = planes * ny
+    part = ny // CHUNKS
     moves = [
-        (tx_hbm, tx_ref),
+        (tx_hbm, raw_tx),
         (ty_hbm, raw_ty),
-        (tz_hbm, tz_ref),
-        (accel_hbm, ip_ref),
-        (coupling_hbm, cc_ref),
-        (upwind_hbm, uu_ref),
+        (tz_hbm, raw_tz),
+        (accel_hbm, raw_accel),
+        (coupling_hbm, raw_coupling),
+        (upwind_hbm, raw_upwind),
         (storage_hbm, raw_storage),
-        (rhs_p_hbm, rp_ref),
-        (rhs_s_hbm, rs_ref),
-        (cross_hbm, xx_ref),
+        (rhs_p_hbm, raw_rhs_p),
+        (rhs_s_hbm, raw_rhs_s),
+        (cross_hbm, raw_cross),
     ]
+
+    def copies(c):
+        found = []
+        for i, (src, dst) in enumerate(moves):
+            start = pl.multiple_of(c * part, SUB)
+            to = pl.multiple_of(start + SUB, SUB) if dst is raw_ty else start
+            found.append(
+                pltpu.make_async_copy(src.at[:, pl.ds(start, part)], dst.at[:, pl.ds(to, part)], sems.at[c, i])
+            )
+        return found
+
     fetches = [
         pltpu.make_async_copy(src, dst, fetch_sems.at[i])
         for i, (src, dst) in enumerate(((cell_hbm, cell_ref), (index_hbm, index_ref)))
     ]
     for fetch in fetches:
         fetch.start()
-    copies = []
-    for x in range(planes):
-        for i, (src, dst) in enumerate(moves):
-            to = x * ny + SUB if dst is raw_ty else x * ny
-            copies.append(
-                pltpu.make_async_copy(src.at[pl.ds(x * ny, ny)], dst.at[pl.ds(to, ny)], sems.at[x, i])
-            )
-    for copy in copies:
-        copy.start()
+    for c in range(CHUNKS):
+        for copy in copies(c):
+            copy.start()
 
     last = lax.axis_index("gx") == lax.axis_size("gx") - 1
     keep_last = jnp.where(last, 0.0, 1.0)
@@ -180,52 +195,59 @@
 
     lane = iota((SUB, LANES), 1)
     sub = iota((SUB, LANES), 0)
-    for x in range(planes):
-        for copy in copies[x * len(moves) : (x + 1) * len(moves)]:
+
+    @pl.loop(0, CHUNKS)
+    def _(c):
+        for copy in copies(c):
             copy.wait()
 
-        @pl.loop(0, ny // SUB, unroll=4)
+        @pl.loop(0, part // SUB)
         def _(r):
-            y0 = pl.multiple_of(r * SUB, SUB)
+            y0 = pl.multiple_of(c * part + r * SUB, SUB)
             ypos = sub + y0
-            at = pl.ds(y0 + x * ny, SUB)
-            tx = tx_ref[at, :]
-            if x == planes - 1:
-                tx = tx * keep_last
+            here = pl.ds(y0, SUB)
+            txl = None
+            for x in range(planes):
+                at = pl.ds(y0 + x * ny, SUB)
+                tx = raw_tx[x, here, :]
+                if x == planes - 1:
+                    tx = tx * keep_last
                 tx_ref[at, :] = tx
-            ty = jnp.where(ypos == ny - 1, 0.0, raw_ty[pl.ds(y0 + (x * ny + SUB), SUB), :])
-            tyl = jnp.where(ypos == 0, 0.0, raw_ty[pl.ds(y0 + (x * ny + SUB - 1), SUB), :])
-            tz = jnp.where(lane == LANES - 1, 0.0, tz_ref[at, :])
-            tzl = pltpu.roll(tz, 1, 1)
-            ty_ref[at, :] = ty
-            tyl_ref[at, :] = tyl
-            tz_ref[at, :] = tz
-            tzl_ref[at, :] = tzl
-            tsum = tx + ty + tyl + tz + tzl
-            if x > 0:
-                tsum = tsum + tx_ref[pl.ds(y0 + (x - 1) * ny, SUB), :]
-            accel = ip_ref[at, :]
-            coupling = cc_ref[at, :]
-            upwind = uu_ref[at, :]
-            to_p = accel * (1.0 + jnp.abs(coupling))
-            to_s = accel * jnp.abs(upwind)
-            dp = to_p * tsum + accel * cwi_ref[at, :]
-            ds = to_s * tsum + raw_storage[at, :]
-            if x == 0:
-                here = pl.ds(y0, SUB)
-                extra_ref[here, :] = to_p
-                extra_ref[pl.ds(y0 + ny, SUB), :] = to_s
-                extra_ref[pl.ds(y0 + 2 * ny, SUB), :] = ds
-                ip_ref[at, :] = dp
-            else:
-                ip = 1.0 / dp
-                is_ = 1.0 / ds
-                ip_ref[at, :] = ip
+                ty = jnp.where(ypos == ny - 1, 0.0, raw_ty[x, pl.ds(y0 + SUB, SUB), :])
+                tyl = jnp.where(ypos == 0, 0.0, raw_ty[x, pl.ds(y0 + SUB - 1, SUB), :])
+                tz = jnp.where(lane == LANES - 1, 0.0, raw_tz[x, here, :])
+                tzl = pltpu.roll(tz, 1, 1)
+                ty_ref[at, :] = ty
+                tyl_ref[at, :] = tyl
+                tz_ref[at, :] = tz
+                tzl_ref[at, :] = tzl
+                tsum = tx + ty + tyl + tz + tzl
+                if x > 0:
+                    tsum = tsum + txl
+                accel = raw_accel[x, here, :]
+                coupling = raw_coupling[x, here, :]
+                upwind = raw_upwind[x, here, :]
+                to_p = accel * (1.0 + jnp.abs(coupling))
+                to_s = accel * jnp.abs(upwind)
+                dp = to_p * tsum + accel * cwi_ref[at, :]
+                ds = to_s * tsum + raw_storage[x, here, :]
+                rhs_p, rhs_s, cross = raw_rhs_p[x, here, :], raw_rhs_s[x, here, :], raw_cross[x, here, :]
+                if x == 0:
+                    extra_ref[here, :] = to_p
+                    extra_ref[pl.ds(y0 + ny, SUB), :] = to_s
+                    extra_ref[pl.ds(y0 + 2 * ny, SUB), :] = ds
+                    ip_ref[at, :] = dp
+                    ip, is_ = 1.0, 1.0
+                else:
+                    ip = 1.0 / dp
+                    is_ = 1.0 / ds
+                    ip_ref[at, :] = ip
                 cc_ref[at, :] = coupling * ip
-                rp_ref[at, :] = rp_ref[at, :] * ip
-                rs_ref[at, :] = rs_ref[at, :] * is_
+                rp_ref[at, :] = rhs_p * ip
+                rs_ref[at, :] = rhs_s * is_
                 uu_ref[at, :] = upwind * is_
-                xx_ref[at, :] = xx_ref[at, :] * is_
+                xx_ref[at, :] = cross * is_
+                txl = tx
 
 
 def own_lanes(ref, place, groups):
@@ -744,11 +766,10 @@
     def to_chip(block):
         return lax.ppermute(block, "gx", pairs_o)
 
-    tx = flat(trans_x)
     index = lines(perf_index)
     send, wells = call(
         functools.partial(first_kernel, sizes),
-        [tx, lines(perf_well), index],
+        [flat(trans_x), lines(perf_well), index],
         [HBM, HBM, HBM],
         [vmem(ny + SUB), vmem(2 * groups)],
         [VMEM(index.shape, jnp.int32), VMEM(index.shape, F32), DMA((3,))],
@@ -757,22 +778,22 @@
     )
     from_o = to_chip(send)
     from_e = to_core(send)
-    big = [tx] + [
-        flat(a)
-        for a in (trans_y, trans_z, accel, coupling, upwind, storage, rhs_pressure, rhs_saturation, cross)
-    ]
+    big = [trans_x, trans_y, trans_z, accel, coupling, upwind, storage, rhs_pressure, rhs_saturation, cross]
     made = call(
         functools.partial(setup_kernel, sizes),
         [perf_cell, perf_index] + big,
         [HBM] * (2 + len(big)),
         [vmem(rows)] * 11 + [vmem(3 * ny), vmem(groups * SUB), SMEM((groups,), jnp.int32)],
         [
-            VMEM((padded, LANES), F32),
-            VMEM((rows, LANES), F32),
+            VMEM((planes, ny, LANES), F32),
+            VMEM((planes, ny + SUB, LANES), F32),
+        ]
+        + [VMEM((planes, ny, LANES), F32)] * 8
+        + [
             VMEM((rows, LANES), F32),
             SMEM(perf_cell.shape, jnp.int32),
             SMEM(perf_index.shape, F32),
-            DMA((planes, 10)),
+            DMA((CHUNKS, 10)),
             DMA((2,)),
         ],
         "setup",

time: 68.9 us -> 67.3 us (0.977)
  Pallas kernels: 25.4 us -> 23.9 us
    pallas_call x19, Pallas kernels: 25.4 us -> 23.9 us  [call(): pl.pallas_call(kernel, in_specs=[spec(space) for space in spaces], out_sp...]
  transfers between devices with their start and end apart: 13 -> 13, of which waited for: 6 -> 6; matrix products, arithmetic and copies ran while one was open for 0% -> 0% of each run, Pallas kernels for 31% -> 29%
where the time goes in v3:
time: 67.3 us; the launch traced here: 67 us
  starting transfers between devices  31.6 us (47%)
  Pallas kernels  23.9 us (36%)
  waiting for transfers between devices  10.1 us (15%)
  between operations  0.8 us (1%)
    pallas_call x19, Pallas kernels, call(): pl.pallas_call(kernel, in_specs=[spec(space) for space in spaces], out_sp...  23.9 us
    ppermute x6, starting transfers between devices, to_core(): return lax.ppermute(block, 'gx', pairs_e)  22.3 us
    all_to_all x1, waiting for transfers between devices, body(): grads = lax.all_to_all(sums.reshape(devices, SUB, LANES), 'gx', 0, 0)  5.39 us
    all_to_all x1, starting transfers between devices, body(): grads = lax.all_to_all(sums.reshape(devices, SUB, LANES), 'gx', 0, 0)  5.33 us
    ppermute x6, waiting for transfers between devices, to_core(): return lax.ppermute(block, 'gx', pairs_e)  4.69 us
    ppermute x6, starting transfers between devices, to_chip(): return lax.ppermute(block, 'gx', pairs_o)  4.02 us
  transfers between devices with their start and end apart: 13, of which 6 were waited for; matrix products, arithmetic and copies ran while one was open for 0% of the time, Pallas kernels for 29%

profile of v3, /device:TPU:0, one launch (start us, length us, event | category | flops | bytes accessed | tf_op | source)
XLA Modules:
  0.0 67.0 jit_solution(11457417128264448151)
XLA Ops:
  0.6 0.9 %first.1 = (f32[136,128]{1,0:T(8,128)S(1)}, f32[64,128]{1,0:T(8,128)S(1)}) custom-call(f32[1024,128]{1,0:T(8,128)} %bitcast.9, s32[2,128]{1,0:T(2,128)} %bitcast.13, f32[2,128]{1,0:T(2,128)} %bitcast.10), custom_call_target="tpu_custom_call" | custom-call | flops 4000000 | bytes 3000000 | tf_op jit(solution)/shard_map/first/pallas_call | solution.py:740
  1.5 0.7 collective-permute-start
  2.2 4.4 %collective-permute-start.1 = (f32[136,128]{1,0:T(8,128)S(1)}, f32[136,128]{1,0:T(8,128)S(1)}, u32[]{:S(2)}, u32[]{:S(2)}) collective-permute-start(f32[136,128]{1,0:T(8,128)S(1)} %get-tuple-element.85), channel_id=1, source_target_pairs={{0,1},{1,0},{2,3},{3,2},{4,5},{5,4},{6,7},{7,6},{8,9},{9,8},{10,11... | collective-permute-start | bytes 208904 | tf_op jit(solution)/shard_map/ppermute | solution.py:764
  6.6 5.0 %setup.1 = (f32[1024,128]{1,0:T(8,128)S(1)}, f32[1024,128]{1,0:T(8,128)S(1)}, f32[1024,128]{1,0:T(8,128)S(1)}, f32[1024,128]{1,0:T(8,128)S(1)}, f32[1024,128]{1,...) custom-call(s32[256]{0:T(256)} %cell_hbm.1, ...), custom_call_target="tpu_custom_call" | custom-call | flops 16000000 | bytes 12000000 | tf_op jit(solution)/shard_map/setup/pallas_call | solution.py:740
  11.6 0.0 collective-permute-done.from_o
  11.6 0.0 collective-permute-done.1.from_e
  11.6 1.4 %start.1 = (f32[1040,128]{1,0:T(8,128)S(1)}, f32[1040,128]{1,0:T(8,128)S(1)}, f32[768,128]{1,0:T(8,128)S(1)}, f32[512,128]{1,0:T(8,128)S(1)}, f32[512,128]{1,0:T...) custom-call(s32[32]{0:T(128)S(4)} %get-tuple-element.84.cell_ref.ref, ...), custom_call_target="tpu_custom_call" | custom-call | flops 8000000 | bytes 6000000 | tf_op jit(solution)/shard_map/start/pallas_call | solution.py:740
  13.0 0.7 %collective-permute-start.2 = (f32[288,128]{1,0:T(8,128)S(1)}, f32[288,128]{1,0:T(8,128)S(1)}, u32[]{:S(2)}, u32[]{:S(2)}) collective-permute-start(f32[288,128]{1,0:T(8,128)S(1)} %get-tuple-element.101.refs_7_), channel_id=1, source_target_pairs={{1,2},{2,1},{3,4},{4,3},{5,6},{6,5},{7,8},{8,7},{9,10},{10,9},{11,... | collective-permute-start | bytes 442376 | tf_op jit(solution)/shard_map/ppermute | solution.py:767
  13.7 2.7 %inner.5 = (f32[1040,128]{1,0:T(8,128)S(1)}, f32[1040,128]{1,0:T(8,128)S(1)}, f32[1040,128]{1,0:T(8,128)S(1)}, f32[1040,128]{1,0:T(8,128)S(1)}, f32[32,128]{1,0:...) custom-call(s32[32]{0:T(128)S(4)} %get-tuple-element.84.cell_ref.ref, ...), custom_call_target="tpu_custom_call", output_to_operand_aliasing={{0}: (1, {}), {1}: (2, {})} | custom-call | flops 8000000 | bytes 6000000 | tf_op jit(solution)/shard_map/inner/pallas_call | solution.py:740
  16.4 2.9 %collective-permute-start.3 = (f32[288,128]{1,0:T(8,128)S(1)}, f32[288,128]{1,0:T(8,128)S(1)}, u32[]{:S(2)}, u32[]{:S(2)}) collective-permute-start(f32[288,128]{1,0:T(8,128)S(1)} %get-tuple-element.115), channel_id=1, source_target_pairs={{0,1},{1,0},{2,3},{3,2},{4,5},{5,4},{6,7},{7,6},{8,9},{9,8},{10,11... | collective-permute-start | bytes 442376 | tf_op jit(solution)/shard_map/ppermute | solution.py:764
  19.4 0.0 collective-permute-done.2.from_o.refs_2_
  19.4 0.1 facing.5
  19.4 0.9 %collective-permute-done.3.refs_3_.refs_23_ = f32[288,128]{1,0:T(8,128)S(1)} collective-permute-done((f32[288,128]{1,0:T(8,128)S(1)}, f32[288,128]{1,0:T(8,128)S(1)}, u32[]{:S(2)}, u32[]{:S(2)}) %collective-permute-start.3) | collective-permute-done | bytes 147488 | tf_op jit(solution)/shard_map/ppermute | solution.py:764
  20.4 0.2 outer.5
  20.6 0.7 %collective-permute-start.4 = (f32[288,128]{1,0:T(8,128)S(1)}, f32[288,128]{1,0:T(8,128)S(1)}, u32[]{:S(2)}, u32[]{:S(2)}) collective-permute-start(f32[288,128]{1,0:T(8,128)S(1)} %get-tuple-element.121.refs_7_), channel_id=1, source_target_pairs={{1,2},{2,1},{3,4},{4,3},{5,6},{6,5},{7,8},{8,7},{9,10},{10,9},{11,... | collective-permute-start | bytes 442376 | tf_op jit(solution)/shard_map/ppermute | solution.py:767
  21.3 2.5 %inner.6 = (f32[1040,128]{1,0:T(8,128)S(1)}, f32[1040,128]{1,0:T(8,128)S(1)}, f32[1040,128]{1,0:T(8,128)S(1)}, f32[1040,128]{1,0:T(8,128)S(1)}, f32[32,128]{1,0:...) custom-call(s32[32]{0:T(128)S(4)} %get-tuple-element.84.cell_ref.refs_0, ...), custom_call_target="tpu_custom_call", output_to_operand_aliasing={{0}: (1, {}), {1}: (2, {})} | custom-call | flops 8000000 | bytes 6000000 | tf_op jit(solution)/shard_map/inner/pallas_call | solution.py:740
  23.8 3.7 %collective-permute-start.5 = (f32[288,128]{1,0:T(8,128)S(1)}, f32[288,128]{1,0:T(8,128)S(1)}, u32[]{:S(2)}, u32[]{:S(2)}) collective-permute-start(f32[288,128]{1,0:T(8,128)S(1)} %get-tuple-element.126), channel_id=1, source_target_pairs={{0,1},{1,0},{2,3},{3,2},{4,5},{5,4},{6,7},{7,6},{8,9},{9,8},{10,11... | collective-permute-start | bytes 442376 | tf_op jit(solution)/shard_map/ppermute | solution.py:764
  27.5 0.0 collective-permute-done.4.from_o.refs_2_
  27.6 0.1 facing.6
  27.6 0.9 %collective-permute-done.5.refs_3_.refs_23_ = f32[288,128]{1,0:T(8,128)S(1)} collective-permute-done((f32[288,128]{1,0:T(8,128)S(1)}, f32[288,128]{1,0:T(8,128)S(1)}, u32[]{:S(2)}, u32[]{:S(2)}) %collective-permute-start.5) | collective-permute-done | bytes 147488 | tf_op jit(solution)/shard_map/ppermute | solution.py:764
  28.6 0.2 outer.6
  28.8 0.7 %collective-permute-start.6 = (f32[288,128]{1,0:T(8,128)S(1)}, f32[288,128]{1,0:T(8,128)S(1)}, u32[]{:S(2)}, u32[]{:S(2)}) collective-permute-start(f32[288,128]{1,0:T(8,128)S(1)} %get-tuple-element.131.refs_7_), channel_id=1, source_target_pairs={{1,2},{2,1},{3,4},{4,3},{5,6},{6,5},{7,8},{8,7},{9,10},{10,9},{11,... | collective-permute-start | bytes 442376 | tf_op jit(solution)/shard_map/ppermute | solution.py:767
  29.5 2.6 %inner.7 = (f32[1040,128]{1,0:T(8,128)S(1)}, f32[1040,128]{1,0:T(8,128)S(1)}, f32[1040,128]{1,0:T(8,128)S(1)}, f32[1040,128]{1,0:T(8,128)S(1)}, f32[32,128]{1,0:...) custom-call(s32[32]{0:T(128)S(4)} %get-tuple-element.84.cell_ref.refs_0, ...), custom_call_target="tpu_custom_call", output_to_operand_aliasing={{0}: (1, {}), {1}: (2, {})} | custom-call | flops 8000000 | bytes 6000000 | tf_op jit(solution)/shard_map/inner/pallas_call | solution.py:740
  32.1 3.9 %collective-permute-start.7 = (f32[288,128]{1,0:T(8,128)S(1)}, f32[288,128]{1,0:T(8,128)S(1)}, u32[]{:S(2)}, u32[]{:S(2)}) collective-permute-start(f32[288,128]{1,0:T(8,128)S(1)} %get-tuple-element.136), channel_id=1, source_target_pairs={{0,1},{1,0},{2,3},{3,2},{4,5},{5,4},{6,7},{7,6},{8,9},{9,8},{10,11... | collective-permute-start | bytes 442376 | tf_op jit(solution)/shard_map/ppermute | solution.py:764
  36.0 0.0 collective-permute-done.6.from_o.refs_2_
  36.0 0.1 facing.7
  36.1 0.9 %collective-permute-done.7.refs_3_.refs_23_ = f32[288,128]{1,0:T(8,128)S(1)} collective-permute-done((f32[288,128]{1,0:T(8,128)S(1)}, f32[288,128]{1,0:T(8,128)S(1)}, u32[]{:S(2)}, u32[]{:S(2)}) %collective-permute-start.7) | collective-permute-done | bytes 147488 | tf_op jit(solution)/shard_map/ppermute | solution.py:764
  37.0 0.2 outer.7
  37.3 0.7 %collective-permute-start.8 = (f32[288,128]{1,0:T(8,128)S(1)}, f32[288,128]{1,0:T(8,128)S(1)}, u32[]{:S(2)}, u32[]{:S(2)}) collective-permute-start(f32[288,128]{1,0:T(8,128)S(1)} %get-tuple-element.141.refs_7_), channel_id=1, source_target_pairs={{1,2},{2,1},{3,4},{4,3},{5,6},{6,5},{7,8},{8,7},{9,10},{10,9},{11,... | collective-permute-start | bytes 442376 | tf_op jit(solution)/shard_map/ppermute | solution.py:767
  38.0 2.6 %inner.8 = (f32[1040,128]{1,0:T(8,128)S(1)}, f32[1040,128]{1,0:T(8,128)S(1)}, f32[1040,128]{1,0:T(8,128)S(1)}, f32[1040,128]{1,0:T(8,128)S(1)}, f32[32,128]{1,0:...) custom-call(s32[32]{0:T(128)S(4)} %get-tuple-element.84.cell_ref.refs_0, ...), custom_call_target="tpu_custom_call", output_to_operand_aliasing={{0}: (1, {}), {1}: (2, {})} | custom-call | flops 8000000 | bytes 6000000 | tf_op jit(solution)/shard_map/inner/pallas_call | solution.py:740
  40.5 3.8 %collective-permute-start.9 = (f32[288,128]{1,0:T(8,128)S(1)}, f32[288,128]{1,0:T(8,128)S(1)}, u32[]{:S(2)}, u32[]{:S(2)}) collective-permute-start(f32[288,128]{1,0:T(8,128)S(1)} %get-tuple-element.146), channel_id=1, source_target_pairs={{0,1},{1,0},{2,3},{3,2},{4,5},{5,4},{6,7},{7,6},{8,9},{9,8},{10,11... | collective-permute-start | bytes 442376 | tf_op jit(solution)/shard_map/ppermute | solution.py:764
  44.3 0.0 collective-permute-done.8.from_o.refs_2_
  44.3 0.1 facing.8
  44.4 0.9 %collective-permute-done.9.refs_3_.refs_23_ = f32[288,128]{1,0:T(8,128)S(1)} collective-permute-done((f32[288,128]{1,0:T(8,128)S(1)}, f32[288,128]{1,0:T(8,128)S(1)}, u32[]{:S(2)}, u32[]{:S(2)}) %collective-permute-start.9) | collective-permute-done | bytes 147488 | tf_op jit(solution)/shard_map/ppermute | solution.py:764
  45.3 0.2 outer.8
  45.6 0.7 %collective-permute-start.10 = (f32[288,128]{1,0:T(8,128)S(1)}, f32[288,128]{1,0:T(8,128)S(1)}, u32[]{:S(2)}, u32[]{:S(2)}) collective-permute-start(f32[288,128]{1,0:T(8,128)S(1)} %get-tuple-element.151.refs_7_), channel_id=1, source_target_pairs={{1,2},{2,1},{3,4},{4,3},{5,6},{6,5},{7,8},{8,7},{9,10},{10,9},{11,... | collective-permute-start | bytes 442376 | tf_op jit(solution)/shard_map/ppermute | solution.py:767
  46.3 2.5 %inner.9 = (f32[1040,128]{1,0:T(8,128)S(1)}, f32[1040,128]{1,0:T(8,128)S(1)}, f32[1040,128]{1,0:T(8,128)S(1)}, f32[1040,128]{1,0:T(8,128)S(1)}, f32[32,128]{1,0:...) custom-call(s32[32]{0:T(128)S(4)} %get-tuple-element.84.cell_ref.refs_0, ...), custom_call_target="tpu_custom_call", output_to_operand_aliasing={{0}: (1, {}), {1}: (2, {})} | custom-call | flops 8000000 | bytes 6000000 | tf_op jit(solution)/shard_map/inner/pallas_call | solution.py:740
  48.8 3.5 %collective-permute-start.11 = (f32[288,128]{1,0:T(8,128)S(1)}, f32[288,128]{1,0:T(8,128)S(1)}, u32[]{:S(2)}, u32[]{:S(2)}) collective-permute-start(f32[288,128]{1,0:T(8,128)S(1)} %get-tuple-element.156), channel_id=1, source_target_pairs={{0,1},{1,0},{2,3},{3,2},{4,5},{5,4},{6,7},{7,6},{8,9},{9,8},{10,11... | collective-permute-start | bytes 442376 | tf_op jit(solution)/shard_map/ppermute | solution.py:764
  52.3 0.0 collective-permute-done.10.from_o.refs_2_
  52.3 0.1 facing.9
  52.3 0.9 %collective-permute-done.11.refs_3_.from_e = f32[288,128]{1,0:T(8,128)S(1)} collective-permute-done((f32[288,128]{1,0:T(8,128)S(1)}, f32[288,128]{1,0:T(8,128)S(1)}, u32[]{:S(2)}, u32[]{:S(2)}) %collective-permute-start.11) | collective-permute-done | bytes 147488 | tf_op jit(solution)/shard_map/ppermute | solution.py:764
  53.3 0.9 %outer.9 = (f32[288,128]{1,0:T(8,128)S(1)}, f32[32,128]{1,0:T(8,128)S(1)}, f32[128,128]{1,0:T(8,128)}) custom-call(s32[32]{0:T(128)S(4)} %get-tuple-element.84.cell_ref.refs_0_, f32[288,128]{1,0:T(8,128)S(1)} %get-tuple-element.155.refs_1_, f32[288,128]{1,0:T(8,128)S(1)} %collective-permute-done.10.from_o.refs_2_, ...), custom_call_target="tpu_custom_call", output_to_operand_aliasing={{0}: (1, {})} | custom-call | flops 4000000 | bytes 3000000 | tf_op jit(solution)/shard_map/outer/pallas_call | solution.py:740
  54.2 5.3 %all-to-all-start = ((f32[16,8,128]{2,1,0:T(8,128)}), f32[16,8,128]{2,1,0:T(8,128)S(1)}, u32[]{:S(2)}, u32[]{:S(2)}) async-start(f32[16,8,128]{2,1,0:T(8,128)} %bitcast.7), calls=%async_computation | async-start | bytes 131072 | tf_op jit(solution)/shard_map/all_to_all | solution.py:855
  59.5 1.5 %final.1 = (f32[1040,128]{1,0:T(8,128)S(1)}, f32[1040,128]{1,0:T(8,128)S(1)}, f32[1024,128]{1,0:T(8,128)}, f32[1024,128]{1,0:T(8,128)}) custom-call(s32[32]{0:T(128)S(4)} %get-tuple-element.84.cell_ref.refs_0_, f32[1040,128]{1,0:T(8,128)S(1)} %get-tuple-element.153.p_ref.p_in, ...), custom_call_target="tpu_custom_call", output_to_operand_aliasing={{0}: (1, {}), {1}: (2, {})} | custom-call | flops 8000000 | bytes 6000000 | tf_op jit(solution)/shard_map/final/pallas_call | solution.py:740
  61.0 5.4 %all-to-all-done = f32[16,8,128]{2,1,0:T(8,128)S(1)} async-done(((f32[16,8,128]{2,1,0:T(8,128)}), f32[16,8,128]{2,1,0:T(8,128)S(1)}, u32[]{:S(2)}, u32[]{:S(2)}) %all-to-all-start) | async-done | bytes 65568 | tf_op jit(solution)/shard_map/all_to_all | solution.py:855
  66.4 0.5 reduce_sum.9
Async XLA Ops:
  1.5 10.1 %collective-permute-start = (f32[136,128]{1,0:T(8,128)S(1)}, f32[136,128]{1,0:T(8,128)S(1)}, u32[]{:S(2)}, u32[]{:S(2)}) collective-permute-start(f32[136,128]{1,0:T(8,128)S(1)} %get-tuple-element.85), channel_id=1, source_target_pairs={{1,2},{2,1},{3,4},{4,3},{5,6},{6,5},{7,8},{8,7},{9,10},{10,9},{11,... | collective-permute-start | bytes 208904 | tf_op jit(solution)/shard_map/ppermute | solution.py:767
  2.2 9.4 %collective-permute-start.1 = (f32[136,128]{1,0:T(8,128)S(1)}, f32[136,128]{1,0:T(8,128)S(1)}, u32[]{:S(2)}, u32[]{:S(2)}) collective-permute-start(f32[136,128]{1,0:T(8,128)S(1)} %get-tuple-element.85), channel_id=1, source_target_pairs={{0,1},{1,0},{2,3},{3,2},{4,5},{5,4},{6,7},{7,6},{8,9},{9,8},{10,11... | collective-permute-start | bytes 208904 | tf_op jit(solution)/shard_map/ppermute | solution.py:764
  13.0 6.3 %collective-permute-start.2 = (f32[288,128]{1,0:T(8,128)S(1)}, f32[288,128]{1,0:T(8,128)S(1)}, u32[]{:S(2)}, u32[]{:S(2)}) collective-permute-start(f32[288,128]{1,0:T(8,128)S(1)} %get-tuple-element.101.refs_7_), channel_id=1, source_target_pairs={{1,2},{2,1},{3,4},{4,3},{5,6},{6,5},{7,8},{8,7},{9,10},{10,9},{11,... | collective-permute-start | bytes 442376 | tf_op jit(solution)/shard_map/ppermute | solution.py:767
  16.4 3.9 %collective-permute-start.3 = (f32[288,128]{1,0:T(8,128)S(1)}, f32[288,128]{1,0:T(8,128)S(1)}, u32[]{:S(2)}, u32[]{:S(2)}) collective-permute-start(f32[288,128]{1,0:T(8,128)S(1)} %get-tuple-element.115), channel_id=1, source_target_pairs={{0,1},{1,0},{2,3},{3,2},{4,5},{5,4},{6,7},{7,6},{8,9},{9,8},{10,11... | collective-permute-start | bytes 442376 | tf_op jit(solution)/shard_map/ppermute | solution.py:764
  20.6 6.9 %collective-permute-start.4 = (f32[288,128]{1,0:T(8,128)S(1)}, f32[288,128]{1,0:T(8,128)S(1)}, u32[]{:S(2)}, u32[]{:S(2)}) collective-permute-start(f32[288,128]{1,0:T(8,128)S(1)} %get-tuple-element.121.refs_7_), channel_id=1, source_target_pairs={{1,2},{2,1},{3,4},{4,3},{5,6},{6,5},{7,8},{8,7},{9,10},{10,9},{11,... | collective-permute-start | bytes 442376 | tf_op jit(solution)/shard_map/ppermute | solution.py:767
  23.8 4.7 %collective-permute-start.5 = (f32[288,128]{1,0:T(8,128)S(1)}, f32[288,128]{1,0:T(8,128)S(1)}, u32[]{:S(2)}, u32[]{:S(2)}) collective-permute-start(f32[288,128]{1,0:T(8,128)S(1)} %get-tuple-element.126), channel_id=1, source_target_pairs={{0,1},{1,0},{2,3},{3,2},{4,5},{5,4},{6,7},{7,6},{8,9},{9,8},{10,11... | collective-permute-start | bytes 442376 | tf_op jit(solution)/shard_map/ppermute | solution.py:764
  28.8 7.2 %collective-permute-start.6 = (f32[288,128]{1,0:T(8,128)S(1)}, f32[288,128]{1,0:T(8,128)S(1)}, u32[]{:S(2)}, u32[]{:S(2)}) collective-permute-start(f32[288,128]{1,0:T(8,128)S(1)} %get-tuple-element.131.refs_7_), channel_id=1, source_target_pairs={{1,2},{2,1},{3,4},{4,3},{5,6},{6,5},{7,8},{8,7},{9,10},{10,9},{11,... | collective-permute-start | bytes 442376 | tf_op jit(solution)/shard_map/ppermute | solution.py:767
  32.1 4.9 %collective-permute-start.7 = (f32[288,128]{1,0:T(8,128)S(1)}, f32[288,128]{1,0:T(8,128)S(1)}, u32[]{:S(2)}, u32[]{:S(2)}) collective-permute-start(f32[288,128]{1,0:T(8,128)S(1)} %get-tuple-element.136), channel_id=1, source_target_pairs={{0,1},{1,0},{2,3},{3,2},{4,5},{5,4},{6,7},{7,6},{8,9},{9,8},{10,11... | collective-permute-start | bytes 442376 | tf_op jit(solution)/shard_map/ppermute | solution.py:764
  37.3 7.0 %collective-permute-start.8 = (f32[288,128]{1,0:T(8,128)S(1)}, f32[288,128]{1,0:T(8,128)S(1)}, u32[]{:S(2)}, u32[]{:S(2)}) collective-permute-start(f32[288,128]{1,0:T(8,128)S(1)} %get-tuple-element.141.refs_7_), channel_id=1, source_target_pairs={{1,2},{2,1},{3,4},{4,3},{5,6},{6,5},{7,8},{8,7},{9,10},{10,9},{11,... | collective-permute-start | bytes 442376 | tf_op jit(solution)/shard_map/ppermute | solution.py:767
  40.5 4.8 %collective-permute-start.9 = (f32[288,128]{1,0:T(8,128)S(1)}, f32[288,128]{1,0:T(8,128)S(1)}, u32[]{:S(2)}, u32[]{:S(2)}) collective-permute-start(f32[288,128]{1,0:T(8,128)S(1)} %get-tuple-element.146), channel_id=1, source_target_pairs={{0,1},{1,0},{2,3},{3,2},{4,5},{5,4},{6,7},{7,6},{8,9},{9,8},{10,11... | collective-permute-start | bytes 442376 | tf_op jit(solution)/shard_map/ppermute | solution.py:764
  45.6 6.7 %collective-permute-start.10 = (f32[288,128]{1,0:T(8,128)S(1)}, f32[288,128]{1,0:T(8,128)S(1)}, u32[]{:S(2)}, u32[]{:S(2)}) collective-permute-start(f32[288,128]{1,0:T(8,128)S(1)} %get-tuple-element.151.refs_7_), channel_id=1, source_target_pairs={{1,2},{2,1},{3,4},{4,3},{5,6},{6,5},{7,8},{8,7},{9,10},{10,9},{11,... | collective-permute-start | bytes 442376 | tf_op jit(solution)/shard_map/ppermute | solution.py:767
  48.8 4.5 %collective-permute-start.11 = (f32[288,128]{1,0:T(8,128)S(1)}, f32[288,128]{1,0:T(8,128)S(1)}, u32[]{:S(2)}, u32[]{:S(2)}) collective-permute-start(f32[288,128]{1,0:T(8,128)S(1)} %get-tuple-element.156), channel_id=1, source_target_pairs={{0,1},{1,0},{2,3},{3,2},{4,5},{5,4},{6,7},{7,6},{8,9},{9,8},{10,11... | collective-permute-start | bytes 442376 | tf_op jit(solution)/shard_map/ppermute | solution.py:764
  54.2 12.2 %all-to-all-start = ((f32[16,8,128]{2,1,0:T(8,128)}), f32[16,8,128]{2,1,0:T(8,128)S(1)}, u32[]{:S(2)}, u32[]{:S(2)}) async-start(f32[16,8,128]{2,1,0:T(8,128)} %bitcast.7), calls=%async_computation | async-start | bytes 131072 | tf_op jit(solution)/shard_map/all_to_all | solution.py:855

commit v4 on v3

--- a/solution.py
+++ b/solution.py
@@ -89,6 +89,15 @@
     wells_ref[groups : 2 * groups, :] = total
     send_ref[ny : ny + SUB, :] = well_block(total * (1.0 - before), total * before, groups)
     plane.wait()
+
+
+def split_cell(cell, ny):
+    if ny & (ny - 1):
+        row = lax.div(cell, LANES)
+        return lax.div(row, ny), lax.rem(row, ny), lax.rem(cell, LANES)
+    bits_z, bits_y = LANES.bit_length() - 1, ny.bit_length() - 1
+    row = lax.shift_right_logical(cell, bits_z)
+    return lax.shift_right_logical(row, bits_y), row & (ny - 1), cell & (LANES - 1)
 
 
 def setup_kernel(
@@ -183,14 +192,14 @@
         fetch.wait()
     spot = iota((SUB, LANES), 0) * LANES + iota((SUB, LANES), 1)
     for g in range(groups):
-        y_ref[g] = (cell_ref[g * run] // LANES) % ny
+        _, y, _ = split_cell(cell_ref[g * run], ny)
+        y_ref[g] = y
         weight = zero
         for k in range(g * run, (g + 1) * run):
-            cell = cell_ref[k]
-            at = (cell // (ny * LANES)) * LANES + cell % LANES
-            weight = weight + jnp.where(spot == at, index_ref[k], 0.0)
+            x, _, z = split_cell(cell_ref[k], ny)
+            weight = weight + jnp.where(spot == x * LANES + z, index_ref[k], 0.0)
         weight_ref[g * SUB : (g + 1) * SUB, :] = weight
-        slab = pl.ds((cell_ref[g * run] // LANES) % ny, planes, ny)
+        slab = pl.ds(y, planes, ny)
         cwi_ref[slab, :] = cwi_ref[slab, :] + weight
 
     lane = iota((SUB, LANES), 1)
@@ -472,7 +481,26 @@
 def put_sums(sizes, to_before, before, by_lane, rows_out, send_ref):
     ny, groups = sizes.ny, sizes.groups
     rows_out[...] = by_lane
-    send_ref[2 * ny : 2 * ny + groups, :] = by_lane * jnp.where(to_before, before, 1.0 - before)
+    shared = by_lane * jnp.where(to_before, before, 1.0 - before)
+    parts = groups // SUB
+    lane = iota((SUB, LANES), 1)
+    tile = jnp.zeros((SUB, LANES), F32)
+    for q in range(parts):
+        part = shared[q * SUB : (q + 1) * SUB, :]
+        width = LANES
+        while width > LANES // parts:
+            width //= 2
+            part = part + pltpu.roll(part, width, 1)
+        tile = jnp.where(lane // (LANES // parts) == q, part, tile)
+    send_ref[2 * ny : 2 * ny + SUB, :] = tile
+
+
+def rows_of(tile, groups):
+    parts = groups // SUB
+    lane = iota((SUB, LANES), 1)
+    return jnp.concatenate(
+        [jnp.where(lane // (LANES // parts) == q, tile, 0.0) for q in range(parts)], axis=0
+    )
 
 
 def finish_core_plane(sizes, cell_ref, p_ref, s_ref, mu_ref, wp_ref, ws_ref, halo, plane_e, send_e):
@@ -632,10 +660,10 @@
     def table(i):
         return table_ref[i * groups : (i + 1) * groups, :]
 
-    tail = slice(2 * ny, 2 * ny + groups)
+    tail = slice(2 * ny, 2 * ny + SUB)
     come_e, come_o = from_e[tail, :], from_o[tail, :]
-    low = jnp.where(even, come_o, come_e)
-    high = jnp.where(even, come_e, come_o)
+    low = rows_of(jnp.where(even, come_o, come_e), groups)
+    high = rows_of(jnp.where(even, come_e, come_o), groups)
     before = table(BEFORE)
     total = spread(lane_sum(sums_in[...] + jnp.where(before > 0.5, low, high)), groups)
     mu = (table(RHS) + total) * table(INV)
@@ -653,17 +681,18 @@
     mu_own = (table(RHS_OWN) + total_own) * table(INV_OWN)
     grad_own = mu_own * table(SUM_OWN) - part_own
     grad_before = -part_before
-    lane = iota((groups, LANES), 1)
-    slot_own, slot_before = table(SLOT_OWN), table(SLOT_BEFORE)
-    inside = lane < groups
+    lane = iota((SUB, LANES), 1).astype(F32)
+    outside = lane >= groups
+    values = []
+    for slots, grad in ((table(SLOT_OWN), grad_own), (table(SLOT_BEFORE), grad_before)):
+        for q in range(groups // SUB):
+            part = slice(q * SUB, (q + 1) * SUB)
+            values.append((jnp.where(outside, -1.0, slots[part, :] - lane), grad[part, :]))
     for d in range(sizes.devices):
-        want = (lane + d * groups).astype(F32)
-        own = jnp.where(inside & (slot_own == want), grad_own, 0.0)
-        other = jnp.where(inside & (slot_before == want), grad_before, 0.0)
-        row = jnp.sum(own + other, axis=0, keepdims=True)
-        grads_ref[d * SUB : (d + 1) * SUB, :] = jnp.where(
-            iota((SUB, LANES), 0) == 0, jnp.broadcast_to(row, (SUB, LANES)), 0.0
-        )
+        total = jnp.zeros((SUB, LANES), F32)
+        for slot, grad in values:
+            total = total + jnp.where(slot == float(d * groups), grad, 0.0)
+        grads_ref[d * SUB : (d + 1) * SUB, :] = total
 
 
 def final_kernel(
@@ -802,7 +831,7 @@
     coefficients, (extra, weight, y) = list(made[:11]), made[11:]
     group_row = VMEM((groups, LANES), F32)
     fields = [vmem(padded), vmem(padded)]
-    block = vmem(2 * ny + groups)
+    block = vmem(2 * ny + SUB)
     slabs = vmem(groups * SUB)
     p, s, edge, plane_e, plane_o, wp, ws, shared, table, mu, sums, send_o = call(
         functools.partial(start_kernel, sizes),
@@ -858,7 +887,7 @@
         final_kernel,
         [p, s, mu, wp, ws, plane_e, send_o, from_e],
         fields + [result, result],
-        [VMEM((2 * ny + groups, LANES), F32), DMA((2,))],
+        [VMEM((2 * ny + SUB, LANES), F32), DMA((2,))],
         "final",
         2,
         {1: 0, 2: 1},

time: 67.3 us -> 64.9 us (0.964)
  Pallas kernels: 23.9 us -> 22.1 us
    pallas_call x19, Pallas kernels: 23.9 us -> 22.1 us  [call(): pl.pallas_call(kernel, in_specs=[spec(space) for space in spaces], out_sp...]
  transfers between devices with their start and end apart: 13 -> 13, of which waited for: 6 -> 6; matrix products, arithmetic and copies ran while one was open for 0% -> 0% of each run, Pallas kernels for 29% -> 28%
where the time goes in v4:
time: 64.9 us; the launch traced here: 64.5 us
  starting transfers between devices  31.1 us (48%)
  Pallas kernels  22.1 us (34%)
  waiting for transfers between devices  10 us (15%)
  between operations  0.79 us (1%)
    pallas_call x19, Pallas kernels, call(): pl.pallas_call(kernel, in_specs=[spec(space) for space in spaces], out_sp...  22.1 us
    ppermute x6, starting transfers between devices, to_core(): return lax.ppermute(block, 'gx', pairs_e)  22 us
    all_to_all x1, waiting for transfers between devices, body(): grads = lax.all_to_all(sums.reshape(devices, SUB, LANES), 'gx', 0, 0)  5.38 us
    all_to_all x1, starting transfers between devices, body(): grads = lax.all_to_all(sums.reshape(devices, SUB, LANES), 'gx', 0, 0)  5.08 us
    ppermute x6, waiting for transfers between devices, to_core(): return lax.ppermute(block, 'gx', pairs_e)  4.6 us
    ppermute x6, starting transfers between devices, to_chip(): return lax.ppermute(block, 'gx', pairs_o)  4.01 us
  transfers between devices with their start and end apart: 13, of which 6 were waited for; matrix products, arithmetic and copies ran while one was open for 0% of the time, Pallas kernels for 28%

profile of v4, /device:TPU:0, one launch (start us, length us, event | category | flops | bytes accessed | tf_op | source)
XLA Modules:
  0.0 64.5 jit_solution(14165909951600180473)
XLA Ops:
  0.6 0.9 %first.1 = (f32[136,128]{1,0:T(8,128)S(1)}, f32[64,128]{1,0:T(8,128)S(1)}) custom-call(f32[1024,128]{1,0:T(8,128)} %bitcast.9, s32[2,128]{1,0:T(2,128)} %bitcast.13, f32[2,128]{1,0:T(2,128)} %bitcast.10), custom_call_target="tpu_custom_call" | custom-call | flops 4000000 | bytes 3000000 | tf_op jit(solution)/shard_map/first/pallas_call | solution.py:769
  1.5 0.7 %collective-permute-start = (f32[136,128]{1,0:T(8,128)S(1)}, f32[136,128]{1,0:T(8,128)S(1)}, u32[]{:S(2)}, u32[]{:S(2)}) collective-permute-start(f32[136,128]{1,0:T(8,128)S(1)} %get-tuple-element.85), channel_id=1, source_target_pairs={{1,2},{2,1},{3,4},{4,3},{5,6},{6,5},{7,8},{8,7},{9,10},{10,9},{11,... | collective-permute-start | bytes 208904 | tf_op jit(solution)/shard_map/ppermute | solution.py:796
  2.2 4.4 %collective-permute-start.1 = (f32[136,128]{1,0:T(8,128)S(1)}, f32[136,128]{1,0:T(8,128)S(1)}, u32[]{:S(2)}, u32[]{:S(2)}) collective-permute-start(f32[136,128]{1,0:T(8,128)S(1)} %get-tuple-element.85), channel_id=1, source_target_pairs={{0,1},{1,0},{2,3},{3,2},{4,5},{5,4},{6,7},{7,6},{8,9},{9,8},{10,11... | collective-permute-start | bytes 208904 | tf_op jit(solution)/shard_map/ppermute | solution.py:793
  6.6 3.4 %setup.1 = (f32[1024,128]{1,0:T(8,128)S(1)}, f32[1024,128]{1,0:T(8,128)S(1)}, f32[1024,128]{1,0:T(8,128)S(1)}, f32[1024,128]{1,0:T(8,128)S(1)}, f32[1024,128]{1,...) custom-call(s32[256]{0:T(256)} %cell_hbm.1, ...), custom_call_target="tpu_custom_call" | custom-call | flops 16000000 | bytes 12000000 | tf_op jit(solution)/shard_map/setup/pallas_call | solution.py:769
  10.0 0.0 collective-permute-done.from_o
  10.0 0.0 collective-permute-done.1.from_e
  10.0 1.4 %start.1 = (f32[1040,128]{1,0:T(8,128)S(1)}, f32[1040,128]{1,0:T(8,128)S(1)}, f32[768,128]{1,0:T(8,128)S(1)}, f32[512,128]{1,0:T(8,128)S(1)}, f32[512,128]{1,0:T...) custom-call(s32[32]{0:T(128)S(4)} %get-tuple-element.84.cell_ref.ref, ...), custom_call_target="tpu_custom_call" | custom-call | flops 8000000 | bytes 6000000 | tf_op jit(solution)/shard_map/start/pallas_call | solution.py:769
  11.5 0.7 %collective-permute-start.2 = (f32[264,128]{1,0:T(8,128)S(1)}, f32[264,128]{1,0:T(8,128)S(1)}, u32[]{:S(2)}, u32[]{:S(2)}) collective-permute-start(f32[264,128]{1,0:T(8,128)S(1)} %get-tuple-element.101.refs_7_), channel_id=1, source_target_pairs={{1,2},{2,1},{3,4},{4,3},{5,6},{6,5},{7,8},{8,7},{9,10},{10,9},{11,... | collective-permute-start | bytes 405512 | tf_op jit(solution)/shard_map/ppermute | solution.py:796
  12.1 2.5 %inner.5 = (f32[1040,128]{1,0:T(8,128)S(1)}, f32[1040,128]{1,0:T(8,128)S(1)}, f32[1040,128]{1,0:T(8,128)S(1)}, f32[1040,128]{1,0:T(8,128)S(1)}, f32[32,128]{1,0:...) custom-call(s32[32]{0:T(128)S(4)} %get-tuple-element.84.cell_ref.ref, ...), custom_call_target="tpu_custom_call", output_to_operand_aliasing={{0}: (1, {}), {1}: (2, {})} | custom-call | flops 8000000 | bytes 6000000 | tf_op jit(solution)/shard_map/inner/pallas_call | solution.py:769
  14.7 2.9 %collective-permute-start.3 = (f32[264,128]{1,0:T(8,128)S(1)}, f32[264,128]{1,0:T(8,128)S(1)}, u32[]{:S(2)}, u32[]{:S(2)}) collective-permute-start(f32[264,128]{1,0:T(8,128)S(1)} %get-tuple-element.115), channel_id=1, source_target_pairs={{0,1},{1,0},{2,3},{3,2},{4,5},{5,4},{6,7},{7,6},{8,9},{9,8},{10,11... | collective-permute-start | bytes 405512 | tf_op jit(solution)/shard_map/ppermute | solution.py:793
  17.6 0.0 collective-permute-done.2.from_o.refs_2_
  17.6 0.1 facing.5
  17.7 0.9 %collective-permute-done.3.refs_3_.refs_23_ = f32[264,128]{1,0:T(8,128)S(1)} collective-permute-done((f32[264,128]{1,0:T(8,128)S(1)}, f32[264,128]{1,0:T(8,128)S(1)}, u32[]{:S(2)}, u32[]{:S(2)}) %collective-permute-start.3) | collective-permute-done | bytes 135200 | tf_op jit(solution)/shard_map/ppermute | solution.py:793
  18.6 0.3 outer.5
  18.9 0.7 %collective-permute-start.4 = (f32[264,128]{1,0:T(8,128)S(1)}, f32[264,128]{1,0:T(8,128)S(1)}, u32[]{:S(2)}, u32[]{:S(2)}) collective-permute-start(f32[264,128]{1,0:T(8,128)S(1)} %get-tuple-element.121.refs_7_), channel_id=1, source_target_pairs={{1,2},{2,1},{3,4},{4,3},{5,6},{6,5},{7,8},{8,7},{9,10},{10,9},{11,... | collective-permute-start | bytes 405512 | tf_op jit(solution)/shard_map/ppermute | solution.py:796
  19.6 2.5 %inner.6 = (f32[1040,128]{1,0:T(8,128)S(1)}, f32[1040,128]{1,0:T(8,128)S(1)}, f32[1040,128]{1,0:T(8,128)S(1)}, f32[1040,128]{1,0:T(8,128)S(1)}, f32[32,128]{1,0:...) custom-call(s32[32]{0:T(128)S(4)} %get-tuple-element.84.cell_ref.refs_0, ...), custom_call_target="tpu_custom_call", output_to_operand_aliasing={{0}: (1, {}), {1}: (2, {})} | custom-call | flops 8000000 | bytes 6000000 | tf_op jit(solution)/shard_map/inner/pallas_call | solution.py:769
  22.1 3.7 %collective-permute-start.5 = (f32[264,128]{1,0:T(8,128)S(1)}, f32[264,128]{1,0:T(8,128)S(1)}, u32[]{:S(2)}, u32[]{:S(2)}) collective-permute-start(f32[264,128]{1,0:T(8,128)S(1)} %get-tuple-element.126), channel_id=1, source_target_pairs={{0,1},{1,0},{2,3},{3,2},{4,5},{5,4},{6,7},{7,6},{8,9},{9,8},{10,11... | collective-permute-start | bytes 405512 | tf_op jit(solution)/shard_map/ppermute | solution.py:793
  25.7 0.0 collective-permute-done.4.from_o.refs_2_
  25.7 0.1 facing.6
  25.8 0.9 %collective-permute-done.5.refs_3_.refs_23_ = f32[264,128]{1,0:T(8,128)S(1)} collective-permute-done((f32[264,128]{1,0:T(8,128)S(1)}, f32[264,128]{1,0:T(8,128)S(1)}, u32[]{:S(2)}, u32[]{:S(2)}) %collective-permute-start.5) | collective-permute-done | bytes 135200 | tf_op jit(solution)/shard_map/ppermute | solution.py:793
  26.7 0.3 outer.6
  27.0 0.7 %collective-permute-start.6 = (f32[264,128]{1,0:T(8,128)S(1)}, f32[264,128]{1,0:T(8,128)S(1)}, u32[]{:S(2)}, u32[]{:S(2)}) collective-permute-start(f32[264,128]{1,0:T(8,128)S(1)} %get-tuple-element.131.refs_7_), channel_id=1, source_target_pairs={{1,2},{2,1},{3,4},{4,3},{5,6},{6,5},{7,8},{8,7},{9,10},{10,9},{11,... | collective-permute-start | bytes 405512 | tf_op jit(solution)/shard_map/ppermute | solution.py:796
  27.7 2.5 %inner.7 = (f32[1040,128]{1,0:T(8,128)S(1)}, f32[1040,128]{1,0:T(8,128)S(1)}, f32[1040,128]{1,0:T(8,128)S(1)}, f32[1040,128]{1,0:T(8,128)S(1)}, f32[32,128]{1,0:...) custom-call(s32[32]{0:T(128)S(4)} %get-tuple-element.84.cell_ref.refs_0, ...), custom_call_target="tpu_custom_call", output_to_operand_aliasing={{0}: (1, {}), {1}: (2, {})} | custom-call | flops 8000000 | bytes 6000000 | tf_op jit(solution)/shard_map/inner/pallas_call | solution.py:769
  30.2 3.7 %collective-permute-start.7 = (f32[264,128]{1,0:T(8,128)S(1)}, f32[264,128]{1,0:T(8,128)S(1)}, u32[]{:S(2)}, u32[]{:S(2)}) collective-permute-start(f32[264,128]{1,0:T(8,128)S(1)} %get-tuple-element.136), channel_id=1, source_target_pairs={{0,1},{1,0},{2,3},{3,2},{4,5},{5,4},{6,7},{7,6},{8,9},{9,8},{10,11... | collective-permute-start | bytes 405512 | tf_op jit(solution)/shard_map/ppermute | solution.py:793
  33.9 0.0 collective-permute-done.6.from_o.refs_2_
  33.9 0.1 facing.7
  34.0 0.9 %collective-permute-done.7.refs_3_.refs_23_ = f32[264,128]{1,0:T(8,128)S(1)} collective-permute-done((f32[264,128]{1,0:T(8,128)S(1)}, f32[264,128]{1,0:T(8,128)S(1)}, u32[]{:S(2)}, u32[]{:S(2)}) %collective-permute-start.7) | collective-permute-done | bytes 135200 | tf_op jit(solution)/shard_map/ppermute | solution.py:793
  34.9 0.3 outer.7
  35.1 0.7 %collective-permute-start.8 = (f32[264,128]{1,0:T(8,128)S(1)}, f32[264,128]{1,0:T(8,128)S(1)}, u32[]{:S(2)}, u32[]{:S(2)}) collective-permute-start(f32[264,128]{1,0:T(8,128)S(1)} %get-tuple-element.141.refs_7_), channel_id=1, source_target_pairs={{1,2},{2,1},{3,4},{4,3},{5,6},{6,5},{7,8},{8,7},{9,10},{10,9},{11,... | collective-permute-start | bytes 405512 | tf_op jit(solution)/shard_map/ppermute | solution.py:796
  35.8 2.5 %inner.8 = (f32[1040,128]{1,0:T(8,128)S(1)}, f32[1040,128]{1,0:T(8,128)S(1)}, f32[1040,128]{1,0:T(8,128)S(1)}, f32[1040,128]{1,0:T(8,128)S(1)}, f32[32,128]{1,0:...) custom-call(s32[32]{0:T(128)S(4)} %get-tuple-element.84.cell_ref.refs_0, ...), custom_call_target="tpu_custom_call", output_to_operand_aliasing={{0}: (1, {}), {1}: (2, {})} | custom-call | flops 8000000 | bytes 6000000 | tf_op jit(solution)/shard_map/inner/pallas_call | solution.py:769
  38.3 3.7 %collective-permute-start.9 = (f32[264,128]{1,0:T(8,128)S(1)}, f32[264,128]{1,0:T(8,128)S(1)}, u32[]{:S(2)}, u32[]{:S(2)}) collective-permute-start(f32[264,128]{1,0:T(8,128)S(1)} %get-tuple-element.146), channel_id=1, source_target_pairs={{0,1},{1,0},{2,3},{3,2},{4,5},{5,4},{6,7},{7,6},{8,9},{9,8},{10,11... | collective-permute-start | bytes 405512 | tf_op jit(solution)/shard_map/ppermute | solution.py:793
  42.0 0.0 collective-permute-done.8.from_o.refs_2_
  42.0 0.1 facing.8
  42.1 0.9 %collective-permute-done.9.refs_3_.refs_23_ = f32[264,128]{1,0:T(8,128)S(1)} collective-permute-done((f32[264,128]{1,0:T(8,128)S(1)}, f32[264,128]{1,0:T(8,128)S(1)}, u32[]{:S(2)}, u32[]{:S(2)}) %collective-permute-start.9) | collective-permute-done | bytes 135200 | tf_op jit(solution)/shard_map/ppermute | solution.py:793
  43.0 0.3 outer.8
  43.3 0.7 %collective-permute-start.10 = (f32[264,128]{1,0:T(8,128)S(1)}, f32[264,128]{1,0:T(8,128)S(1)}, u32[]{:S(2)}, u32[]{:S(2)}) collective-permute-start(f32[264,128]{1,0:T(8,128)S(1)} %get-tuple-element.151.refs_7_), channel_id=1, source_target_pairs={{1,2},{2,1},{3,4},{4,3},{5,6},{6,5},{7,8},{8,7},{9,10},{10,9},{11,... | collective-permute-start | bytes 405512 | tf_op jit(solution)/shard_map/ppermute | solution.py:796
  43.9 2.5 %inner.9 = (f32[1040,128]{1,0:T(8,128)S(1)}, f32[1040,128]{1,0:T(8,128)S(1)}, f32[1040,128]{1,0:T(8,128)S(1)}, f32[1040,128]{1,0:T(8,128)S(1)}, f32[32,128]{1,0:...) custom-call(s32[32]{0:T(128)S(4)} %get-tuple-element.84.cell_ref.refs_0, ...), custom_call_target="tpu_custom_call", output_to_operand_aliasing={{0}: (1, {}), {1}: (2, {})} | custom-call | flops 8000000 | bytes 6000000 | tf_op jit(solution)/shard_map/inner/pallas_call | solution.py:769
  46.5 3.6 %collective-permute-start.11 = (f32[264,128]{1,0:T(8,128)S(1)}, f32[264,128]{1,0:T(8,128)S(1)}, u32[]{:S(2)}, u32[]{:S(2)}) collective-permute-start(f32[264,128]{1,0:T(8,128)S(1)} %get-tuple-element.156), channel_id=1, source_target_pairs={{0,1},{1,0},{2,3},{3,2},{4,5},{5,4},{6,7},{7,6},{8,9},{9,8},{10,11... | collective-permute-start | bytes 405512 | tf_op jit(solution)/shard_map/ppermute | solution.py:793
  50.1 0.0 collective-permute-done.10.from_o.refs_2_
  50.1 0.1 facing.9
  50.2 0.9 %collective-permute-done.11.refs_3_.from_e = f32[264,128]{1,0:T(8,128)S(1)} collective-permute-done((f32[264,128]{1,0:T(8,128)S(1)}, f32[264,128]{1,0:T(8,128)S(1)}, u32[]{:S(2)}, u32[]{:S(2)}) %collective-permute-start.11) | collective-permute-done | bytes 135200 | tf_op jit(solution)/shard_map/ppermute | solution.py:793
  51.1 0.9 %outer.9 = (f32[264,128]{1,0:T(8,128)S(1)}, f32[32,128]{1,0:T(8,128)S(1)}, f32[128,128]{1,0:T(8,128)}) custom-call(s32[32]{0:T(128)S(4)} %get-tuple-element.84.cell_ref.refs_0_, f32[264,128]{1,0:T(8,128)S(1)} %get-tuple-element.155.refs_1_, f32[264,128]{1,0:T(8,128)S(1)} %collective-permute-done.10.from_o.refs_2_, ...), custom_call_target="tpu_custom_call", output_to_operand_aliasing={{0}: (1, {})} | custom-call | flops 4000000 | bytes 3000000 | tf_op jit(solution)/shard_map/outer/pallas_call | solution.py:769
  52.0 5.1 %all-to-all-start = ((f32[16,8,128]{2,1,0:T(8,128)}), f32[16,8,128]{2,1,0:T(8,128)S(1)}, u32[]{:S(2)}, u32[]{:S(2)}) async-start(f32[16,8,128]{2,1,0:T(8,128)} %bitcast.7), calls=%async_computation | async-start | bytes 131072 | tf_op jit(solution)/shard_map/all_to_all | solution.py:884
  57.1 1.5 %final.1 = (f32[1040,128]{1,0:T(8,128)S(1)}, f32[1040,128]{1,0:T(8,128)S(1)}, f32[1024,128]{1,0:T(8,128)}, f32[1024,128]{1,0:T(8,128)}) custom-call(s32[32]{0:T(128)S(4)} %get-tuple-element.84.cell_ref.refs_0_, f32[1040,128]{1,0:T(8,128)S(1)} %get-tuple-element.153.p_ref.p_in, ...), custom_call_target="tpu_custom_call", output_to_operand_aliasing={{0}: (1, {}), {1}: (2, {})} | custom-call | flops 8000000 | bytes 6000000 | tf_op jit(solution)/shard_map/final/pallas_call | solution.py:769
  58.6 5.4 %all-to-all-done = f32[16,8,128]{2,1,0:T(8,128)S(1)} async-done(((f32[16,8,128]{2,1,0:T(8,128)}), f32[16,8,128]{2,1,0:T(8,128)S(1)}, u32[]{:S(2)}, u32[]{:S(2)}) %all-to-all-start) | async-done | bytes 65568 | tf_op jit(solution)/shard_map/all_to_all | solution.py:884
  64.0 0.5 reduce_sum.9
Async XLA Ops:
  1.5 8.5 %collective-permute-start = (f32[136,128]{1,0:T(8,128)S(1)}, f32[136,128]{1,0:T(8,128)S(1)}, u32[]{:S(2)}, u32[]{:S(2)}) collective-permute-start(f32[136,128]{1,0:T(8,128)S(1)} %get-tuple-element.85), channel_id=1, source_target_pairs={{1,2},{2,1},{3,4},{4,3},{5,6},{6,5},{7,8},{8,7},{9,10},{10,9},{11,... | collective-permute-start | bytes 208904 | tf_op jit(solution)/shard_map/ppermute | solution.py:796
  2.2 7.8 %collective-permute-start.1 = (f32[136,128]{1,0:T(8,128)S(1)}, f32[136,128]{1,0:T(8,128)S(1)}, u32[]{:S(2)}, u32[]{:S(2)}) collective-permute-start(f32[136,128]{1,0:T(8,128)S(1)} %get-tuple-element.85), channel_id=1, source_target_pairs={{0,1},{1,0},{2,3},{3,2},{4,5},{5,4},{6,7},{7,6},{8,9},{9,8},{10,11... | collective-permute-start | bytes 208904 | tf_op jit(solution)/shard_map/ppermute | solution.py:793
  11.5 6.2 %collective-permute-start.2 = (f32[264,128]{1,0:T(8,128)S(1)}, f32[264,128]{1,0:T(8,128)S(1)}, u32[]{:S(2)}, u32[]{:S(2)}) collective-permute-start(f32[264,128]{1,0:T(8,128)S(1)} %get-tuple-element.101.refs_7_), channel_id=1, source_target_pairs={{1,2},{2,1},{3,4},{4,3},{5,6},{6,5},{7,8},{8,7},{9,10},{10,9},{11,... | collective-permute-start | bytes 405512 | tf_op jit(solution)/shard_map/ppermute | solution.py:796
  14.7 3.9 %collective-permute-start.3 = (f32[264,128]{1,0:T(8,128)S(1)}, f32[264,128]{1,0:T(8,128)S(1)}, u32[]{:S(2)}, u32[]{:S(2)}) collective-permute-start(f32[264,128]{1,0:T(8,128)S(1)} %get-tuple-element.115), channel_id=1, source_target_pairs={{0,1},{1,0},{2,3},{3,2},{4,5},{5,4},{6,7},{7,6},{8,9},{9,8},{10,11... | collective-permute-start | bytes 405512 | tf_op jit(solution)/shard_map/ppermute | solution.py:793
  18.9 6.9 %collective-permute-start.4 = (f32[264,128]{1,0:T(8,128)S(1)}, f32[264,128]{1,0:T(8,128)S(1)}, u32[]{:S(2)}, u32[]{:S(2)}) collective-permute-start(f32[264,128]{1,0:T(8,128)S(1)} %get-tuple-element.121.refs_7_), channel_id=1, source_target_pairs={{1,2},{2,1},{3,4},{4,3},{5,6},{6,5},{7,8},{8,7},{9,10},{10,9},{11,... | collective-permute-start | bytes 405512 | tf_op jit(solution)/shard_map/ppermute | solution.py:796
  22.1 4.7 %collective-permute-start.5 = (f32[264,128]{1,0:T(8,128)S(1)}, f32[264,128]{1,0:T(8,128)S(1)}, u32[]{:S(2)}, u32[]{:S(2)}) collective-permute-start(f32[264,128]{1,0:T(8,128)S(1)} %get-tuple-element.126), channel_id=1, source_target_pairs={{0,1},{1,0},{2,3},{3,2},{4,5},{5,4},{6,7},{7,6},{8,9},{9,8},{10,11... | collective-permute-start | bytes 405512 | tf_op jit(solution)/shard_map/ppermute | solution.py:793
  27.0 6.9 %collective-permute-start.6 = (f32[264,128]{1,0:T(8,128)S(1)}, f32[264,128]{1,0:T(8,128)S(1)}, u32[]{:S(2)}, u32[]{:S(2)}) collective-permute-start(f32[264,128]{1,0:T(8,128)S(1)} %get-tuple-element.131.refs_7_), channel_id=1, source_target_pairs={{1,2},{2,1},{3,4},{4,3},{5,6},{6,5},{7,8},{8,7},{9,10},{10,9},{11,... | collective-permute-start | bytes 405512 | tf_op jit(solution)/shard_map/ppermute | solution.py:796
  30.2 4.7 %collective-permute-start.7 = (f32[264,128]{1,0:T(8,128)S(1)}, f32[264,128]{1,0:T(8,128)S(1)}, u32[]{:S(2)}, u32[]{:S(2)}) collective-permute-start(f32[264,128]{1,0:T(8,128)S(1)} %get-tuple-element.136), channel_id=1, source_target_pairs={{0,1},{1,0},{2,3},{3,2},{4,5},{5,4},{6,7},{7,6},{8,9},{9,8},{10,11... | collective-permute-start | bytes 405512 | tf_op jit(solution)/shard_map/ppermute | solution.py:793
  35.1 6.9 %collective-permute-start.8 = (f32[264,128]{1,0:T(8,128)S(1)}, f32[264,128]{1,0:T(8,128)S(1)}, u32[]{:S(2)}, u32[]{:S(2)}) collective-permute-start(f32[264,128]{1,0:T(8,128)S(1)} %get-tuple-element.141.refs_7_), channel_id=1, source_target_pairs={{1,2},{2,1},{3,4},{4,3},{5,6},{6,5},{7,8},{8,7},{9,10},{10,9},{11,... | collective-permute-start | bytes 405512 | tf_op jit(solution)/shard_map/ppermute | solution.py:796
  38.3 4.7 %collective-permute-start.9 = (f32[264,128]{1,0:T(8,128)S(1)}, f32[264,128]{1,0:T(8,128)S(1)}, u32[]{:S(2)}, u32[]{:S(2)}) collective-permute-start(f32[264,128]{1,0:T(8,128)S(1)} %get-tuple-element.146), channel_id=1, source_target_pairs={{0,1},{1,0},{2,3},{3,2},{4,5},{5,4},{6,7},{7,6},{8,9},{9,8},{10,11... | collective-permute-start | bytes 405512 | tf_op jit(solution)/shard_map/ppermute | solution.py:793
  43.3 6.8 %collective-permute-start.10 = (f32[264,128]{1,0:T(8,128)S(1)}, f32[264,128]{1,0:T(8,128)S(1)}, u32[]{:S(2)}, u32[]{:S(2)}) collective-permute-start(f32[264,128]{1,0:T(8,128)S(1)} %get-tuple-element.151.refs_7_), channel_id=1, source_target_pairs={{1,2},{2,1},{3,4},{4,3},{5,6},{6,5},{7,8},{8,7},{9,10},{10,9},{11,... | collective-permute-start | bytes 405512 | tf_op jit(solution)/shard_map/ppermute | solution.py:796
  46.5 4.6 %collective-permute-start.11 = (f32[264,128]{1,0:T(8,128)S(1)}, f32[264,128]{1,0:T(8,128)S(1)}, u32[]{:S(2)}, u32[]{:S(2)}) collective-permute-start(f32[264,128]{1,0:T(8,128)S(1)} %get-tuple-element.156), channel_id=1, source_target_pairs={{0,1},{1,0},{2,3},{3,2},{4,5},{5,4},{6,7},{7,6},{8,9},{9,8},{10,11... | collective-permute-start | bytes 405512 | tf_op jit(solution)/shard_map/ppermute | solution.py:793
  52.0 12.0 %all-to-all-start = ((f32[16,8,128]{2,1,0:T(8,128)}), f32[16,8,128]{2,1,0:T(8,128)S(1)}, u32[]{:S(2)}, u32[]{:S(2)}) async-start(f32[16,8,128]{2,1,0:T(8,128)} %bitcast.7), calls=%async_computation | async-start | bytes 131072 | tf_op jit(solution)/shard_map/all_to_all | solution.py:884

commit v5 on v4

--- a/solution.py
+++ b/solution.py
@@ -692,7 +692,7 @@
         total = jnp.zeros((SUB, LANES), F32)
         for slot, grad in values:
             total = total + jnp.where(slot == float(d * groups), grad, 0.0)
-        grads_ref[d * SUB : (d + 1) * SUB, :] = total
+        grads_ref[d] = jnp.sum(total, axis=0, keepdims=True)
 
 
 def final_kernel(
@@ -875,13 +875,13 @@
         send_o, mu, sums = call_vmem(
             lambda sz, *refs: outer_kernel(sz, final, *refs),
             [half_o, from_o, from_e, by_lane, near_o, sums, table, wp, ws, shared, near],
-            [block, vmem(groups), vmem(devices * SUB if final else groups)],
+            [block, vmem(groups), pltpu.VMEM((devices, 1, LANES), F32) if final else vmem(groups)],
             [group_row],
             "outer",
             1,
             {1: 0},
         )
-    grads = lax.all_to_all(sums.reshape(devices, SUB, LANES), "gx", 0, 0)
+    grads = lax.all_to_all(sums, "gx", 0, 0)
     result = pltpu.HBM((rows, nz), F32)
     _, _, p, s = call_vmem(
         final_kernel,

time: 64.9 us -> 64.3 us (level)
  no operation moved by 1% of the time
where the time goes in v5:
time: 64.3 us; the launch traced here: 64 us
  starting transfers between devices  31.1 us (48%)
  Pallas kernels  22.1 us (34%)
  waiting for transfers between devices  9.51 us (15%)
  between operations  0.79 us (1%)
    pallas_call x19, Pallas kernels, call(): pl.pallas_call(kernel, in_specs=[spec(space) for space in spaces], out_sp...  22.1 us
    ppermute x6, starting transfers between devices, to_core(): return lax.ppermute(block, 'gx', pairs_e)  22 us
    all_to_all x1, starting transfers between devices, body(): grads = lax.all_to_all(sums, 'gx', 0, 0)  5.08 us
    all_to_all x1, waiting for transfers between devices, body(): grads = lax.all_to_all(sums, 'gx', 0, 0)  4.89 us
    ppermute x6, waiting for transfers between devices, to_core(): return lax.ppermute(block, 'gx', pairs_e)  4.6 us
    ppermute x6, starting transfers between devices, to_chip(): return lax.ppermute(block, 'gx', pairs_o)  4.01 us
  transfers between devices with their start and end apart: 13, of which 6 were waited for; matrix products, arithmetic and copies ran while one was open for 0% of the time, Pallas kernels for 28%

profile of v5, /device:TPU:0, one launch (start us, length us, event | category | flops | bytes accessed | tf_op | source)
XLA Modules:
  0.0 64.0 jit_solution(4911062451827763389)
XLA Ops:
  0.6 0.9 %first.1 = (f32[136,128]{1,0:T(8,128)S(1)}, f32[64,128]{1,0:T(8,128)S(1)}) custom-call(f32[1024,128]{1,0:T(8,128)} %bitcast.8, s32[2,128]{1,0:T(2,128)} %bitcast.12, f32[2,128]{1,0:T(2,128)} %bitcast.9), custom_call_target="tpu_custom_call" | custom-call | flops 4000000 | bytes 3000000 | tf_op jit(solution)/shard_map/first/pallas_call | solution.py:769
  1.5 0.7 %collective-permute-start = (f32[136,128]{1,0:T(8,128)S(1)}, f32[136,128]{1,0:T(8,128)S(1)}, u32[]{:S(2)}, u32[]{:S(2)}) collective-permute-start(f32[136,128]{1,0:T(8,128)S(1)} %get-tuple-element.85), channel_id=1, source_target_pairs={{1,2},{2,1},{3,4},{4,3},{5,6},{6,5},{7,8},{8,7},{9,10},{10,9},{11,... | collective-permute-start | bytes 208904 | tf_op jit(solution)/shard_map/ppermute | solution.py:796
  2.2 4.4 %collective-permute-start.1 = (f32[136,128]{1,0:T(8,128)S(1)}, f32[136,128]{1,0:T(8,128)S(1)}, u32[]{:S(2)}, u32[]{:S(2)}) collective-permute-start(f32[136,128]{1,0:T(8,128)S(1)} %get-tuple-element.85), channel_id=1, source_target_pairs={{0,1},{1,0},{2,3},{3,2},{4,5},{5,4},{6,7},{7,6},{8,9},{9,8},{10,11... | collective-permute-start | bytes 208904 | tf_op jit(solution)/shard_map/ppermute | solution.py:793
  6.6 3.4 %setup.1 = (f32[1024,128]{1,0:T(8,128)S(1)}, f32[1024,128]{1,0:T(8,128)S(1)}, f32[1024,128]{1,0:T(8,128)S(1)}, f32[1024,128]{1,0:T(8,128)S(1)}, f32[1024,128]{1,...) custom-call(s32[256]{0:T(256)} %cell_hbm.1, ...), custom_call_target="tpu_custom_call" | custom-call | flops 16000000 | bytes 12000000 | tf_op jit(solution)/shard_map/setup/pallas_call | solution.py:769
  10.0 0.0 collective-permute-done.from_o
  10.0 0.0 collective-permute-done.1.from_e
  10.0 1.4 %start.1 = (f32[1040,128]{1,0:T(8,128)S(1)}, f32[1040,128]{1,0:T(8,128)S(1)}, f32[768,128]{1,0:T(8,128)S(1)}, f32[512,128]{1,0:T(8,128)S(1)}, f32[512,128]{1,0:T...) custom-call(s32[32]{0:T(128)S(4)} %get-tuple-element.84.cell_ref.ref, ...), custom_call_target="tpu_custom_call" | custom-call | flops 8000000 | bytes 6000000 | tf_op jit(solution)/shard_map/start/pallas_call | solution.py:769
  11.5 0.7 %collective-permute-start.2 = (f32[264,128]{1,0:T(8,128)S(1)}, f32[264,128]{1,0:T(8,128)S(1)}, u32[]{:S(2)}, u32[]{:S(2)}) collective-permute-start(f32[264,128]{1,0:T(8,128)S(1)} %get-tuple-element.101.refs_7_), channel_id=1, source_target_pairs={{1,2},{2,1},{3,4},{4,3},{5,6},{6,5},{7,8},{8,7},{9,10},{10,9},{11,... | collective-permute-start | bytes 405512 | tf_op jit(solution)/shard_map/ppermute | solution.py:796
  12.1 2.5 %inner.5 = (f32[1040,128]{1,0:T(8,128)S(1)}, f32[1040,128]{1,0:T(8,128)S(1)}, f32[1040,128]{1,0:T(8,128)S(1)}, f32[1040,128]{1,0:T(8,128)S(1)}, f32[32,128]{1,0:...) custom-call(s32[32]{0:T(128)S(4)} %get-tuple-element.84.cell_ref.ref, ...), custom_call_target="tpu_custom_call", output_to_operand_aliasing={{0}: (1, {}), {1}: (2, {})} | custom-call | flops 8000000 | bytes 6000000 | tf_op jit(solution)/shard_map/inner/pallas_call | solution.py:769
  14.7 2.9 %collective-permute-start.3 = (f32[264,128]{1,0:T(8,128)S(1)}, f32[264,128]{1,0:T(8,128)S(1)}, u32[]{:S(2)}, u32[]{:S(2)}) collective-permute-start(f32[264,128]{1,0:T(8,128)S(1)} %get-tuple-element.115), channel_id=1, source_target_pairs={{0,1},{1,0},{2,3},{3,2},{4,5},{5,4},{6,7},{7,6},{8,9},{9,8},{10,11... | collective-permute-start | bytes 405512 | tf_op jit(solution)/shard_map/ppermute | solution.py:793
  17.6 0.0 collective-permute-done.2.from_o.refs_2_
  17.6 0.1 facing.5
  17.7 0.9 %collective-permute-done.3.refs_3_.refs_23_ = f32[264,128]{1,0:T(8,128)S(1)} collective-permute-done((f32[264,128]{1,0:T(8,128)S(1)}, f32[264,128]{1,0:T(8,128)S(1)}, u32[]{:S(2)}, u32[]{:S(2)}) %collective-permute-start.3) | collective-permute-done | bytes 135200 | tf_op jit(solution)/shard_map/ppermute | solution.py:793
  18.6 0.3 outer.5
  18.9 0.7 %collective-permute-start.4 = (f32[264,128]{1,0:T(8,128)S(1)}, f32[264,128]{1,0:T(8,128)S(1)}, u32[]{:S(2)}, u32[]{:S(2)}) collective-permute-start(f32[264,128]{1,0:T(8,128)S(1)} %get-tuple-element.121.refs_7_), channel_id=1, source_target_pairs={{1,2},{2,1},{3,4},{4,3},{5,6},{6,5},{7,8},{8,7},{9,10},{10,9},{11,... | collective-permute-start | bytes 405512 | tf_op jit(solution)/shard_map/ppermute | solution.py:796
  19.6 2.5 %inner.6 = (f32[1040,128]{1,0:T(8,128)S(1)}, f32[1040,128]{1,0:T(8,128)S(1)}, f32[1040,128]{1,0:T(8,128)S(1)}, f32[1040,128]{1,0:T(8,128)S(1)}, f32[32,128]{1,0:...) custom-call(s32[32]{0:T(128)S(4)} %get-tuple-element.84.cell_ref.refs_0, ...), custom_call_target="tpu_custom_call", output_to_operand_aliasing={{0}: (1, {}), {1}: (2, {})} | custom-call | flops 8000000 | bytes 6000000 | tf_op jit(solution)/shard_map/inner/pallas_call | solution.py:769
  22.1 3.7 %collective-permute-start.5 = (f32[264,128]{1,0:T(8,128)S(1)}, f32[264,128]{1,0:T(8,128)S(1)}, u32[]{:S(2)}, u32[]{:S(2)}) collective-permute-start(f32[264,128]{1,0:T(8,128)S(1)} %get-tuple-element.126), channel_id=1, source_target_pairs={{0,1},{1,0},{2,3},{3,2},{4,5},{5,4},{6,7},{7,6},{8,9},{9,8},{10,11... | collective-permute-start | bytes 405512 | tf_op jit(solution)/shard_map/ppermute | solution.py:793
  25.7 0.0 collective-permute-done.4.from_o.refs_2_
  25.7 0.1 facing.6
  25.8 0.9 %collective-permute-done.5.refs_3_.refs_23_ = f32[264,128]{1,0:T(8,128)S(1)} collective-permute-done((f32[264,128]{1,0:T(8,128)S(1)}, f32[264,128]{1,0:T(8,128)S(1)}, u32[]{:S(2)}, u32[]{:S(2)}) %collective-permute-start.5) | collective-permute-done | bytes 135200 | tf_op jit(solution)/shard_map/ppermute | solution.py:793
  26.7 0.3 outer.6
  27.0 0.7 %collective-permute-start.6 = (f32[264,128]{1,0:T(8,128)S(1)}, f32[264,128]{1,0:T(8,128)S(1)}, u32[]{:S(2)}, u32[]{:S(2)}) collective-permute-start(f32[264,128]{1,0:T(8,128)S(1)} %get-tuple-element.131.refs_7_), channel_id=1, source_target_pairs={{1,2},{2,1},{3,4},{4,3},{5,6},{6,5},{7,8},{8,7},{9,10},{10,9},{11,... | collective-permute-start | bytes 405512 | tf_op jit(solution)/shard_map/ppermute | solution.py:796
  27.7 2.5 %inner.7 = (f32[1040,128]{1,0:T(8,128)S(1)}, f32[1040,128]{1,0:T(8,128)S(1)}, f32[1040,128]{1,0:T(8,128)S(1)}, f32[1040,128]{1,0:T(8,128)S(1)}, f32[32,128]{1,0:...) custom-call(s32[32]{0:T(128)S(4)} %get-tuple-element.84.cell_ref.refs_0, ...), custom_call_target="tpu_custom_call", output_to_operand_aliasing={{0}: (1, {}), {1}: (2, {})} | custom-call | flops 8000000 | bytes 6000000 | tf_op jit(solution)/shard_map/inner/pallas_call | solution.py:769
  30.2 3.7 %collective-permute-start.7 = (f32[264,128]{1,0:T(8,128)S(1)}, f32[264,128]{1,0:T(8,128)S(1)}, u32[]{:S(2)}, u32[]{:S(2)}) collective-permute-start(f32[264,128]{1,0:T(8,128)S(1)} %get-tuple-element.136), channel_id=1, source_target_pairs={{0,1},{1,0},{2,3},{3,2},{4,5},{5,4},{6,7},{7,6},{8,9},{9,8},{10,11... | collective-permute-start | bytes 405512 | tf_op jit(solution)/shard_map/ppermute | solution.py:793
  33.9 0.0 collective-permute-done.6.from_o.refs_2_
  33.9 0.1 facing.7
  33.9 0.9 %collective-permute-done.7.refs_3_.refs_23_ = f32[264,128]{1,0:T(8,128)S(1)} collective-permute-done((f32[264,128]{1,0:T(8,128)S(1)}, f32[264,128]{1,0:T(8,128)S(1)}, u32[]{:S(2)}, u32[]{:S(2)}) %collective-permute-start.7) | collective-permute-done | bytes 135200 | tf_op jit(solution)/shard_map/ppermute | solution.py:793
  34.9 0.3 outer.7
  35.1 0.7 %collective-permute-start.8 = (f32[264,128]{1,0:T(8,128)S(1)}, f32[264,128]{1,0:T(8,128)S(1)}, u32[]{:S(2)}, u32[]{:S(2)}) collective-permute-start(f32[264,128]{1,0:T(8,128)S(1)} %get-tuple-element.141.refs_7_), channel_id=1, source_target_pairs={{1,2},{2,1},{3,4},{4,3},{5,6},{6,5},{7,8},{8,7},{9,10},{10,9},{11,... | collective-permute-start | bytes 405512 | tf_op jit(solution)/shard_map/ppermute | solution.py:796
  35.8 2.5 %inner.8 = (f32[1040,128]{1,0:T(8,128)S(1)}, f32[1040,128]{1,0:T(8,128)S(1)}, f32[1040,128]{1,0:T(8,128)S(1)}, f32[1040,128]{1,0:T(8,128)S(1)}, f32[32,128]{1,0:...) custom-call(s32[32]{0:T(128)S(4)} %get-tuple-element.84.cell_ref.refs_0, ...), custom_call_target="tpu_custom_call", output_to_operand_aliasing={{0}: (1, {}), {1}: (2, {})} | custom-call | flops 8000000 | bytes 6000000 | tf_op jit(solution)/shard_map/inner/pallas_call | solution.py:769
  38.3 3.7 %collective-permute-start.9 = (f32[264,128]{1,0:T(8,128)S(1)}, f32[264,128]{1,0:T(8,128)S(1)}, u32[]{:S(2)}, u32[]{:S(2)}) collective-permute-start(f32[264,128]{1,0:T(8,128)S(1)} %get-tuple-element.146), channel_id=1, source_target_pairs={{0,1},{1,0},{2,3},{3,2},{4,5},{5,4},{6,7},{7,6},{8,9},{9,8},{10,11... | collective-permute-start | bytes 405512 | tf_op jit(solution)/shard_map/ppermute | solution.py:793
  42.0 0.0 collective-permute-done.8.from_o.refs_2_
  42.0 0.1 facing.8
  42.1 0.9 %collective-permute-done.9.refs_3_.refs_23_ = f32[264,128]{1,0:T(8,128)S(1)} collective-permute-done((f32[264,128]{1,0:T(8,128)S(1)}, f32[264,128]{1,0:T(8,128)S(1)}, u32[]{:S(2)}, u32[]{:S(2)}) %collective-permute-start.9) | collective-permute-done | bytes 135200 | tf_op jit(solution)/shard_map/ppermute | solution.py:793
  43.0 0.3 outer.8
  43.3 0.7 %collective-permute-start.10 = (f32[264,128]{1,0:T(8,128)S(1)}, f32[264,128]{1,0:T(8,128)S(1)}, u32[]{:S(2)}, u32[]{:S(2)}) collective-permute-start(f32[264,128]{1,0:T(8,128)S(1)} %get-tuple-element.151.refs_7_), channel_id=1, source_target_pairs={{1,2},{2,1},{3,4},{4,3},{5,6},{6,5},{7,8},{8,7},{9,10},{10,9},{11,... | collective-permute-start | bytes 405512 | tf_op jit(solution)/shard_map/ppermute | solution.py:796
  43.9 2.5 %inner.9 = (f32[1040,128]{1,0:T(8,128)S(1)}, f32[1040,128]{1,0:T(8,128)S(1)}, f32[1040,128]{1,0:T(8,128)S(1)}, f32[1040,128]{1,0:T(8,128)S(1)}, f32[32,128]{1,0:...) custom-call(s32[32]{0:T(128)S(4)} %get-tuple-element.84.cell_ref.refs_0, ...), custom_call_target="tpu_custom_call", output_to_operand_aliasing={{0}: (1, {}), {1}: (2, {})} | custom-call | flops 8000000 | bytes 6000000 | tf_op jit(solution)/shard_map/inner/pallas_call | solution.py:769
  46.5 3.6 %collective-permute-start.11 = (f32[264,128]{1,0:T(8,128)S(1)}, f32[264,128]{1,0:T(8,128)S(1)}, u32[]{:S(2)}, u32[]{:S(2)}) collective-permute-start(f32[264,128]{1,0:T(8,128)S(1)} %get-tuple-element.156), channel_id=1, source_target_pairs={{0,1},{1,0},{2,3},{3,2},{4,5},{5,4},{6,7},{7,6},{8,9},{9,8},{10,11... | collective-permute-start | bytes 405512 | tf_op jit(solution)/shard_map/ppermute | solution.py:793
  50.1 0.0 collective-permute-done.10.from_o.refs_2_
  50.1 0.1 facing.9
  50.2 0.9 %collective-permute-done.11.refs_3_.from_e = f32[264,128]{1,0:T(8,128)S(1)} collective-permute-done((f32[264,128]{1,0:T(8,128)S(1)}, f32[264,128]{1,0:T(8,128)S(1)}, u32[]{:S(2)}, u32[]{:S(2)}) %collective-permute-start.11) | collective-permute-done | bytes 135200 | tf_op jit(solution)/shard_map/ppermute | solution.py:793
  51.1 0.9 %outer.9 = (f32[264,128]{1,0:T(8,128)S(1)}, f32[32,128]{1,0:T(8,128)S(1)}, f32[16,1,128]{2,1,0:T(1,128)}) custom-call(s32[32]{0:T(128)S(4)} %get-tuple-element.84.cell_ref.refs_0_, f32[264,128]{1,0:T(8,128)S(1)} %get-tuple-element.155.refs_1_, f32[264,128]{1,0:T(8,128)S(1)} %collective-permute-done.10.from_o.refs_2_, ...), custom_call_target="tpu_custom_call", output_to_operand_aliasing={{0}: (1, {})} | custom-call | flops 4000000 | bytes 3000000 | tf_op jit(solution)/shard_map/outer/pallas_call | solution.py:769
  52.0 5.1 %all-to-all-start = ((f32[16,1,128]{2,1,0:T(1,128)}), f32[16,1,128]{2,1,0:T(1,128)S(1)}, u32[]{:S(2)}, u32[]{:S(2)}) async-start(f32[16,1,128]{2,1,0:T(1,128)} %get-tuple-element.164), calls=%async_computation | async-start | bytes 16384 | tf_op jit(solution)/shard_map/all_to_all | solution.py:884
  57.0 1.5 %final.1 = (f32[1040,128]{1,0:T(8,128)S(1)}, f32[1040,128]{1,0:T(8,128)S(1)}, f32[1024,128]{1,0:T(8,128)}, f32[1024,128]{1,0:T(8,128)}) custom-call(s32[32]{0:T(128)S(4)} %get-tuple-element.84.cell_ref.refs_0_, f32[1040,128]{1,0:T(8,128)S(1)} %get-tuple-element.153.p_ref.p_in, ...), custom_call_target="tpu_custom_call", output_to_operand_aliasing={{0}: (1, {}), {1}: (2, {})} | custom-call | flops 8000000 | bytes 6000000 | tf_op jit(solution)/shard_map/final/pallas_call | solution.py:769
  58.6 4.9 %all-to-all-done = f32[16,1,128]{2,1,0:T(1,128)S(1)} async-done(((f32[16,1,128]{2,1,0:T(1,128)}), f32[16,1,128]{2,1,0:T(1,128)S(1)}, u32[]{:S(2)}, u32[]{:S(2)}) %all-to-all-start) | async-done | bytes 8224 | tf_op jit(solution)/shard_map/all_to_all | solution.py:884
  63.5 0.5 reduce_sum.9
Async XLA Ops:
  1.5 8.5 %collective-permute-start = (f32[136,128]{1,0:T(8,128)S(1)}, f32[136,128]{1,0:T(8,128)S(1)}, u32[]{:S(2)}, u32[]{:S(2)}) collective-permute-start(f32[136,128]{1,0:T(8,128)S(1)} %get-tuple-element.85), channel_id=1, source_target_pairs={{1,2},{2,1},{3,4},{4,3},{5,6},{6,5},{7,8},{8,7},{9,10},{10,9},{11,... | collective-permute-start | bytes 208904 | tf_op jit(solution)/shard_map/ppermute | solution.py:796
  2.2 7.8 %collective-permute-start.1 = (f32[136,128]{1,0:T(8,128)S(1)}, f32[136,128]{1,0:T(8,128)S(1)}, u32[]{:S(2)}, u32[]{:S(2)}) collective-permute-start(f32[136,128]{1,0:T(8,128)S(1)} %get-tuple-element.85), channel_id=1, source_target_pairs={{0,1},{1,0},{2,3},{3,2},{4,5},{5,4},{6,7},{7,6},{8,9},{9,8},{10,11... | collective-permute-start | bytes 208904 | tf_op jit(solution)/shard_map/ppermute | solution.py:793
  11.5 6.2 %collective-permute-start.2 = (f32[264,128]{1,0:T(8,128)S(1)}, f32[264,128]{1,0:T(8,128)S(1)}, u32[]{:S(2)}, u32[]{:S(2)}) collective-permute-start(f32[264,128]{1,0:T(8,128)S(1)} %get-tuple-element.101.refs_7_), channel_id=1, source_target_pairs={{1,2},{2,1},{3,4},{4,3},{5,6},{6,5},{7,8},{8,7},{9,10},{10,9},{11,... | collective-permute-start | bytes 405512 | tf_op jit(solution)/shard_map/ppermute | solution.py:796
  14.7 3.9 %collective-permute-start.3 = (f32[264,128]{1,0:T(8,128)S(1)}, f32[264,128]{1,0:T(8,128)S(1)}, u32[]{:S(2)}, u32[]{:S(2)}) collective-permute-start(f32[264,128]{1,0:T(8,128)S(1)} %get-tuple-element.115), channel_id=1, source_target_pairs={{0,1},{1,0},{2,3},{3,2},{4,5},{5,4},{6,7},{7,6},{8,9},{9,8},{10,11... | collective-permute-start | bytes 405512 | tf_op jit(solution)/shard_map/ppermute | solution.py:793
  18.9 6.9 %collective-permute-start.4 = (f32[264,128]{1,0:T(8,128)S(1)}, f32[264,128]{1,0:T(8,128)S(1)}, u32[]{:S(2)}, u32[]{:S(2)}) collective-permute-start(f32[264,128]{1,0:T(8,128)S(1)} %get-tuple-element.121.refs_7_), channel_id=1, source_target_pairs={{1,2},{2,1},{3,4},{4,3},{5,6},{6,5},{7,8},{8,7},{9,10},{10,9},{11,... | collective-permute-start | bytes 405512 | tf_op jit(solution)/shard_map/ppermute | solution.py:796
  22.1 4.7 %collective-permute-start.5 = (f32[264,128]{1,0:T(8,128)S(1)}, f32[264,128]{1,0:T(8,128)S(1)}, u32[]{:S(2)}, u32[]{:S(2)}) collective-permute-start(f32[264,128]{1,0:T(8,128)S(1)} %get-tuple-element.126), channel_id=1, source_target_pairs={{0,1},{1,0},{2,3},{3,2},{4,5},{5,4},{6,7},{7,6},{8,9},{9,8},{10,11... | collective-permute-start | bytes 405512 | tf_op jit(solution)/shard_map/ppermute | solution.py:793
  27.0 6.9 %collective-permute-start.6 = (f32[264,128]{1,0:T(8,128)S(1)}, f32[264,128]{1,0:T(8,128)S(1)}, u32[]{:S(2)}, u32[]{:S(2)}) collective-permute-start(f32[264,128]{1,0:T(8,128)S(1)} %get-tuple-element.131.refs_7_), channel_id=1, source_target_pairs={{1,2},{2,1},{3,4},{4,3},{5,6},{6,5},{7,8},{8,7},{9,10},{10,9},{11,... | collective-permute-start | bytes 405512 | tf_op jit(solution)/shard_map/ppermute | solution.py:796
  30.2 4.7 %collective-permute-start.7 = (f32[264,128]{1,0:T(8,128)S(1)}, f32[264,128]{1,0:T(8,128)S(1)}, u32[]{:S(2)}, u32[]{:S(2)}) collective-permute-start(f32[264,128]{1,0:T(8,128)S(1)} %get-tuple-element.136), channel_id=1, source_target_pairs={{0,1},{1,0},{2,3},{3,2},{4,5},{5,4},{6,7},{7,6},{8,9},{9,8},{10,11... | collective-permute-start | bytes 405512 | tf_op jit(solution)/shard_map/ppermute | solution.py:793
  35.1 6.9 %collective-permute-start.8 = (f32[264,128]{1,0:T(8,128)S(1)}, f32[264,128]{1,0:T(8,128)S(1)}, u32[]{:S(2)}, u32[]{:S(2)}) collective-permute-start(f32[264,128]{1,0:T(8,128)S(1)} %get-tuple-element.141.refs_7_), channel_id=1, source_target_pairs={{1,2},{2,1},{3,4},{4,3},{5,6},{6,5},{7,8},{8,7},{9,10},{10,9},{11,... | collective-permute-start | bytes 405512 | tf_op jit(solution)/shard_map/ppermute | solution.py:796
  38.3 4.7 %collective-permute-start.9 = (f32[264,128]{1,0:T(8,128)S(1)}, f32[264,128]{1,0:T(8,128)S(1)}, u32[]{:S(2)}, u32[]{:S(2)}) collective-permute-start(f32[264,128]{1,0:T(8,128)S(1)} %get-tuple-element.146), channel_id=1, source_target_pairs={{0,1},{1,0},{2,3},{3,2},{4,5},{5,4},{6,7},{7,6},{8,9},{9,8},{10,11... | collective-permute-start | bytes 405512 | tf_op jit(solution)/shard_map/ppermute | solution.py:793
  43.3 6.8 %collective-permute-start.10 = (f32[264,128]{1,0:T(8,128)S(1)}, f32[264,128]{1,0:T(8,128)S(1)}, u32[]{:S(2)}, u32[]{:S(2)}) collective-permute-start(f32[264,128]{1,0:T(8,128)S(1)} %get-tuple-element.151.refs_7_), channel_id=1, source_target_pairs={{1,2},{2,1},{3,4},{4,3},{5,6},{6,5},{7,8},{8,7},{9,10},{10,9},{11,... | collective-permute-start | bytes 405512 | tf_op jit(solution)/shard_map/ppermute | solution.py:796
  46.5 4.6 %collective-permute-start.11 = (f32[264,128]{1,0:T(8,128)S(1)}, f32[264,128]{1,0:T(8,128)S(1)}, u32[]{:S(2)}, u32[]{:S(2)}) collective-permute-start(f32[264,128]{1,0:T(8,128)S(1)} %get-tuple-element.156), channel_id=1, source_target_pairs={{0,1},{1,0},{2,3},{3,2},{4,5},{5,4},{6,7},{7,6},{8,9},{9,8},{10,11... | collective-permute-start | bytes 405512 | tf_op jit(solution)/shard_map/ppermute | solution.py:793
  52.0 11.5 %all-to-all-start = ((f32[16,1,128]{2,1,0:T(1,128)}), f32[16,1,128]{2,1,0:T(1,128)S(1)}, u32[]{:S(2)}, u32[]{:S(2)}) async-start(f32[16,1,128]{2,1,0:T(1,128)} %get-tuple-element.164), calls=%async_computation | async-start | bytes 16384 | tf_op jit(solution)/shard_map/all_to_all | solution.py:884

commit v6 on v5

--- a/solution.py
+++ b/solution.py
@@ -371,8 +371,6 @@
     xx_ref,
     extra_ref,
     weight_ref,
-    p_ref,
-    s_ref,
     edge_ref,
     plane_e,
     plane_o,
@@ -389,7 +387,6 @@
     sems,
 ):
     ny, planes, groups = sizes.ny, sizes.planes, sizes.groups
-    rows = planes * ny
     place = lax.axis_index("gx")
     even = place % 2 == 0
     x_o, _ = facing(sizes, even)
@@ -419,16 +416,12 @@
             to = pl.ds(y0 + i * ny, SUB)
             plane_o[to, :] = jnp.where(even, low[i], high[i])
             plane_e[to, :] = jnp.where(even, high[i], low[i])
-        p_ref[pl.ds(y0 + SUB, SUB), :] = rp
-        s_ref[pl.ds(y0 + SUB, SUB), :] = rs - xx * rp
-        for x in range(1, planes):
-            at = pl.ds(y0 + x * ny, SUB)
-            to = pl.ds(y0 + (x * ny + SUB), SUB)
-            rp = rp_ref[at, :]
-            p_ref[to, :] = rp
-            s_ref[to, :] = rs_ref[at, :] - xx_ref[at, :] * rp
-
-    clear_ends(rows, p_ref, s_ref)
+        rp_end = rp_ref[end, :]
+        send_o[at, :] = jnp.where(even, rp, rp_end)
+        send_o[pl.ds(y0 + ny, SUB), :] = jnp.where(
+            even, rs - xx * rp, rs_ref[end, :] - xx_ref[end, :] * rp_end
+        )
+
     sub = iota((SUB, LANES), 0)
     for g in range(groups):
         y = path_y(sizes, cell_ref, g)
@@ -436,6 +429,8 @@
         slab = pl.ds(y, planes, ny)
         ip = jnp.where(sub == 0, edge_ref[pl.ds(y, 1), :], ip_ref[slab, :])
         xx = jnp.where(sub == 0, edge_ref[pl.ds(y + 5 * ny, 1), :], xx_ref[slab, :])
+        rp = jnp.where(sub == 0, edge_ref[pl.ds(y + 2 * ny, 1), :], rp_ref[slab, :])
+        rows_ref[g : g + 1, :] = jnp.sum(weight_ref[at, :] * rp, axis=0, keepdims=True)
         wp = weight_ref[at, :] * ip
         wp_ref[at, :] = wp
         ws_ref[at, :] = wp * xx
@@ -472,9 +467,7 @@
     mu = rhs * inv
     mu_ref[...] = mu
 
-    finish_plane(sizes, x_o, p_ref, s_ref, None, None, send_o)
     add_wells_to_plane(sizes, cell_ref, mu_ref, wp_ref, ws_ref, x_o, send_o)
-    path_rows(sizes, cell_ref, weight_ref, p_ref, rows_ref)
     put_sums(sizes, even, before, rows_ref[...] + shared_ref[...] * row_of(mu, groups), sums_out, send_o)
 
 
@@ -537,8 +530,6 @@
     sizes,
     first,
     cell_ref,
-    p_in,
-    s_in,
     mu_ref,
     wp_ref,
     ws_ref,
@@ -567,9 +558,23 @@
     if first:
         plane_o, p_old, s_old, p_ref, s_ref, rows_ref, sums_out, send_e, near_ref = refs
         halo = None
+        clear_ends(rows, p_old, s_old)
+
+        @pl.loop(0, ny // SUB)
+        def _(r):
+            y0 = pl.multiple_of(r * SUB, SUB)
+            for x in range(planes):
+                at, to = pl.ds(y0 + x * ny, SUB), pl.ds(y0 + (x * ny + SUB), SUB)
+                if x == 0:
+                    rp, rs, xx = [edge_ref[pl.ds(y0 + i * ny, SUB), :] for i in (2, 3, 5)]
+                else:
+                    rp, rs, xx = rp_ref[at, :], rs_ref[at, :], xx_ref[at, :]
+                p_old[to, :] = rp
+                s_old[to, :] = rs - xx * rp
+
         near_weights(sizes, cell_ref, weight_ref, plane_e, plane_o, near_ref)
     else:
-        halo, p_old, s_old, p_ref, s_ref, rows_ref, sums_out, send_e = refs
+        halo, _, _, p_old, s_old, p_ref, s_ref, rows_ref, sums_out, send_e = refs
     finish_core_plane(sizes, cell_ref, p_old, s_old, mu_ref, wp_ref, ws_ref, halo, plane_e, send_e)
     before = table_ref[BEFORE * sizes.groups : (BEFORE + 1) * sizes.groups, :]
     put_sums(sizes, jnp.logical_not(even), before, sums_in[...], sums_out, send_e)
@@ -833,14 +838,13 @@
     fields = [vmem(padded), vmem(padded)]
     block = vmem(2 * ny + SUB)
     slabs = vmem(groups * SUB)
-    p, s, edge, plane_e, plane_o, wp, ws, shared, table, mu, sums, send_o = call(
+    edge, plane_e, plane_o, wp, ws, shared, table, mu, sums, send_o = call(
         functools.partial(start_kernel, sizes),
         [y, from_o, from_e, wells, lines(well_rhs), lines(well_slot), coefficients[0]]
         + coefficients[5:]
         + [extra, weight],
         [SMEM] + [VMEM] * 3 + [HBM] * 2 + [VMEM] * 9,
-        fields
-        + [vmem(6 * ny), vmem(4 * ny), vmem(4 * ny), slabs, slabs, vmem(groups), vmem(TABLE * groups)]
+        [vmem(6 * ny), vmem(4 * ny), vmem(4 * ny), slabs, slabs, vmem(groups), vmem(TABLE * groups)]
         + [vmem(groups), vmem(groups), block],
         [
             group_row,
@@ -858,12 +862,14 @@
         first = sweep == 1
         _, _, p, s, by_lane, sums, send_e, *rest = call_vmem(
             lambda sz, *refs: inner_kernel(sz, first, *refs),
-            [p, s, mu, wp, ws, weight, send_o, sums, table] + coefficients + [edge, plane_e, plane_o if first else from_e],
+            [mu, wp, ws, weight, send_o, sums, table]
+            + coefficients
+            + ([edge, plane_e, plane_o] if first else [edge, plane_e, from_e, p, s]),
             fields + fields + [vmem(groups), vmem(groups), block] + ([vmem(4 * groups)] if first else []),
             [],
             "inner",
             2,
-            {1: 0, 2: 1},
+            {} if first else {22: 0, 23: 1},
         )
         if first:
             near = rest[0]

time: 64.3 us -> 64.4 us (level)
  starting transfers between devices: 31.1 us -> 29.8 us
  Pallas kernels: 22.1 us -> 23.4 us
    ppermute x6, starting transfers between devices: 22 us -> 19.6 us  [to_core(): return lax.ppermute(block, 'gx', pairs_e)]
    pallas_call x19, Pallas kernels: 22.1 us -> 23.4 us  [call(): pl.pallas_call(kernel, in_specs=[spec(space) for space in spaces], out_sp...]
    all_to_all x1, starting transfers between devices: 5.08 us -> 6.23 us  [body(): grads = lax.all_to_all(sums, 'gx', 0, 0)]
  transfers between devices with their start and end apart: 13 -> 13, of which waited for: 6 -> 6; matrix products, arithmetic and copies ran while one was open for 0% -> 0% of each run, Pallas kernels for 28% -> 30%
where the time goes in v6:
time: 64.4 us; the launch traced here: 64 us
  starting transfers between devices  29.8 us (46%)
  Pallas kernels  23.4 us (36%)
  waiting for transfers between devices  9.51 us (15%)
  between operations  0.78 us (1%)
    pallas_call x19, Pallas kernels, call(): pl.pallas_call(kernel, in_specs=[spec(space) for space in spaces], out_sp...  23.4 us
    ppermute x6, starting transfers between devices, to_core(): return lax.ppermute(block, 'gx', pairs_e)  19.6 us
    all_to_all x1, starting transfers between devices, body(): grads = lax.all_to_all(sums, 'gx', 0, 0)  6.23 us
    all_to_all x1, waiting for transfers between devices, body(): grads = lax.all_to_all(sums, 'gx', 0, 0)  4.89 us
    ppermute x6, waiting for transfers between devices, to_core(): return lax.ppermute(block, 'gx', pairs_e)  4.6 us
    ppermute x6, starting transfers between devices, to_chip(): return lax.ppermute(block, 'gx', pairs_o)  4.01 us
  transfers between devices with their start and end apart: 13, of which 6 were waited for; matrix products, arithmetic and copies ran while one was open for 0% of the time, Pallas kernels for 30%

profile of v6, /device:TPU:0, one launch (start us, length us, event | category | flops | bytes accessed | tf_op | source)
XLA Modules:
  0.0 64.0 jit_solution(8550252928904170425)
XLA Ops:
  0.6 0.9 %first.1 = (f32[136,128]{1,0:T(8,128)S(1)}, f32[64,128]{1,0:T(8,128)S(1)}) custom-call(f32[1024,128]{1,0:T(8,128)} %bitcast.8, s32[2,128]{1,0:T(2,128)} %bitcast.12, f32[2,128]{1,0:T(2,128)} %bitcast.9), custom_call_target="tpu_custom_call" | custom-call | flops 4000000 | bytes 3000000 | tf_op jit(solution)/shard_map/first/pallas_call | solution.py:774
  1.5 0.7 %collective-permute-start = (f32[136,128]{1,0:T(8,128)S(1)}, f32[136,128]{1,0:T(8,128)S(1)}, u32[]{:S(2)}, u32[]{:S(2)}) collective-permute-start(f32[136,128]{1,0:T(8,128)S(1)} %get-tuple-element.83), channel_id=1, source_target_pairs={{1,2},{2,1},{3,4},{4,3},{5,6},{6,5},{7,8},{8,7},{9,10},{10,9},{11,... | collective-permute-start | bytes 208904 | tf_op jit(solution)/shard_map/ppermute | solution.py:801
  2.2 4.4 %collective-permute-start.1 = (f32[136,128]{1,0:T(8,128)S(1)}, f32[136,128]{1,0:T(8,128)S(1)}, u32[]{:S(2)}, u32[]{:S(2)}) collective-permute-start(f32[136,128]{1,0:T(8,128)S(1)} %get-tuple-element.83), channel_id=1, source_target_pairs={{0,1},{1,0},{2,3},{3,2},{4,5},{5,4},{6,7},{7,6},{8,9},{9,8},{10,11... | collective-permute-start | bytes 208904 | tf_op jit(solution)/shard_map/ppermute | solution.py:798
  6.6 3.4 %setup.1 = (f32[1024,128]{1,0:T(8,128)S(1)}, f32[1024,128]{1,0:T(8,128)S(1)}, f32[1024,128]{1,0:T(8,128)S(1)}, f32[1024,128]{1,0:T(8,128)S(1)}, f32[1024,128]{1,...) custom-call(s32[256]{0:T(256)} %cell_hbm.1, ...), custom_call_target="tpu_custom_call" | custom-call | flops 16000000 | bytes 12000000 | tf_op jit(solution)/shard_map/setup/pallas_call | solution.py:774
  10.0 0.0 collective-permute-done.from_o
  10.0 0.0 collective-permute-done.1.from_e
  10.0 1.4 %start.1 = (f32[768,128]{1,0:T(8,128)S(1)}, f32[512,128]{1,0:T(8,128)S(1)}, f32[512,128]{1,0:T(8,128)S(1)}, f32[256,128]{1,0:T(8,128)S(1)}, f32[256,128]{1,0:T(8...) custom-call(s32[32]{0:T(128)S(4)} %get-tuple-element.82.cell_ref.ref, ...), custom_call_target="tpu_custom_call" | custom-call | flops 8000000 | bytes 6000000 | tf_op jit(solution)/shard_map/start/pallas_call | solution.py:774
  11.4 0.7 %collective-permute-start.2 = (f32[264,128]{1,0:T(8,128)S(1)}, f32[264,128]{1,0:T(8,128)S(1)}, u32[]{:S(2)}, u32[]{:S(2)}) collective-permute-start(f32[264,128]{1,0:T(8,128)S(1)} %get-tuple-element.94.refs_5_), channel_id=1, source_target_pairs={{1,2},{2,1},{3,4},{4,3},{5,6},{6,5},{7,8},{8,7},{9,10},{10,9},{11,... | collective-permute-start | bytes 405512 | tf_op jit(solution)/shard_map/ppermute | solution.py:801
  12.1 3.9 %inner.5 = (f32[1040,128]{1,0:T(8,128)}, f32[1040,128]{1,0:T(8,128)}, f32[1040,128]{1,0:T(8,128)S(1)}, f32[1040,128]{1,0:T(8,128)S(1)}, f32[32,128]{1,0:T(8,128)...) custom-call(s32[32]{0:T(128)S(4)} %get-tuple-element.82.cell_ref.refs_0_, ...), custom_call_target="tpu_custom_call" | custom-call | flops 8000000 | bytes 6000000 | tf_op jit(solution)/shard_map/inner/pallas_call | solution.py:774
  16.0 2.9 %collective-permute-start.3 = (f32[264,128]{1,0:T(8,128)S(1)}, f32[264,128]{1,0:T(8,128)S(1)}, u32[]{:S(2)}, u32[]{:S(2)}) collective-permute-start(f32[264,128]{1,0:T(8,128)S(1)} %get-tuple-element.111), channel_id=1, source_target_pairs={{0,1},{1,0},{2,3},{3,2},{4,5},{5,4},{6,7},{7,6},{8,9},{9,8},{10,11... | collective-permute-start | bytes 405512 | tf_op jit(solution)/shard_map/ppermute | solution.py:798
  18.8 0.0 collective-permute-done.2.from_o.refs_2_
  18.8 0.1 facing.5
  18.9 0.9 %collective-permute-done.3.refs_3_.refs_21_ = f32[264,128]{1,0:T(8,128)S(1)} collective-permute-done((f32[264,128]{1,0:T(8,128)S(1)}, f32[264,128]{1,0:T(8,128)S(1)}, u32[]{:S(2)}, u32[]{:S(2)}) %collective-permute-start.3) | collective-permute-done | bytes 135200 | tf_op jit(solution)/shard_map/ppermute | solution.py:798
  19.8 0.3 outer.5
  20.1 0.7 %collective-permute-start.4 = (f32[264,128]{1,0:T(8,128)S(1)}, f32[264,128]{1,0:T(8,128)S(1)}, u32[]{:S(2)}, u32[]{:S(2)}) collective-permute-start(f32[264,128]{1,0:T(8,128)S(1)} %get-tuple-element.116.refs_5_), channel_id=1, source_target_pairs={{1,2},{2,1},{3,4},{4,3},{5,6},{6,5},{7,8},{8,7},{9,10},{10,9},{11,... | collective-permute-start | bytes 405512 | tf_op jit(solution)/shard_map/ppermute | solution.py:801
  20.8 2.6 %inner.6 = (f32[1040,128]{1,0:T(8,128)S(1)}, f32[1040,128]{1,0:T(8,128)S(1)}, f32[1040,128]{1,0:T(8,128)S(1)}, f32[1040,128]{1,0:T(8,128)S(1)}, f32[32,128]{1,0:...) custom-call(s32[32]{0:T(128)S(4)} %get-tuple-element.82.cell_ref.refs, ...), custom_call_target="tpu_custom_call", output_to_operand_aliasing={{0}: (22, {}), {1}: (23, {})} | custom-call | flops 8000000 | bytes 6000000 | tf_op jit(solution)/shard_map/inner/pallas_call | solution.py:774
  23.4 2.9 %collective-permute-start.5 = (f32[264,128]{1,0:T(8,128)S(1)}, f32[264,128]{1,0:T(8,128)S(1)}, u32[]{:S(2)}, u32[]{:S(2)}) collective-permute-start(f32[264,128]{1,0:T(8,128)S(1)} %get-tuple-element.122), channel_id=1, source_target_pairs={{0,1},{1,0},{2,3},{3,2},{4,5},{5,4},{6,7},{7,6},{8,9},{9,8},{10,11... | collective-permute-start | bytes 405512 | tf_op jit(solution)/shard_map/ppermute | solution.py:798
  26.3 0.0 collective-permute-done.4.from_o.refs_2_
  26.3 0.1 facing.6
  26.4 0.9 %collective-permute-done.5.refs_3_.refs_21_ = f32[264,128]{1,0:T(8,128)S(1)} collective-permute-done((f32[264,128]{1,0:T(8,128)S(1)}, f32[264,128]{1,0:T(8,128)S(1)}, u32[]{:S(2)}, u32[]{:S(2)}) %collective-permute-start.5) | collective-permute-done | bytes 135200 | tf_op jit(solution)/shard_map/ppermute | solution.py:798
  27.3 0.3 outer.6
  27.6 0.7 %collective-permute-start.6 = (f32[264,128]{1,0:T(8,128)S(1)}, f32[264,128]{1,0:T(8,128)S(1)}, u32[]{:S(2)}, u32[]{:S(2)}) collective-permute-start(f32[264,128]{1,0:T(8,128)S(1)} %get-tuple-element.126.refs_5_), channel_id=1, source_target_pairs={{1,2},{2,1},{3,4},{4,3},{5,6},{6,5},{7,8},{8,7},{9,10},{10,9},{11,... | collective-permute-start | bytes 405512 | tf_op jit(solution)/shard_map/ppermute | solution.py:801
  28.2 2.5 %inner.7 = (f32[1040,128]{1,0:T(8,128)S(1)}, f32[1040,128]{1,0:T(8,128)S(1)}, f32[1040,128]{1,0:T(8,128)S(1)}, f32[1040,128]{1,0:T(8,128)S(1)}, f32[32,128]{1,0:...) custom-call(s32[32]{0:T(128)S(4)} %get-tuple-element.82.cell_ref.refs, ...), custom_call_target="tpu_custom_call", output_to_operand_aliasing={{0}: (22, {}), {1}: (23, {})} | custom-call | flops 8000000 | bytes 6000000 | tf_op jit(solution)/shard_map/inner/pallas_call | solution.py:774
  30.8 2.9 %collective-permute-start.7 = (f32[264,128]{1,0:T(8,128)S(1)}, f32[264,128]{1,0:T(8,128)S(1)}, u32[]{:S(2)}, u32[]{:S(2)}) collective-permute-start(f32[264,128]{1,0:T(8,128)S(1)} %get-tuple-element.132), channel_id=1, source_target_pairs={{0,1},{1,0},{2,3},{3,2},{4,5},{5,4},{6,7},{7,6},{8,9},{9,8},{10,11... | collective-permute-start | bytes 405512 | tf_op jit(solution)/shard_map/ppermute | solution.py:798
  33.7 0.0 collective-permute-done.6.from_o.refs_2_
  33.7 0.1 facing.7
  33.8 0.9 %collective-permute-done.7.refs_3_.refs_21_ = f32[264,128]{1,0:T(8,128)S(1)} collective-permute-done((f32[264,128]{1,0:T(8,128)S(1)}, f32[264,128]{1,0:T(8,128)S(1)}, u32[]{:S(2)}, u32[]{:S(2)}) %collective-permute-start.7) | collective-permute-done | bytes 135200 | tf_op jit(solution)/shard_map/ppermute | solution.py:798
  34.7 0.3 outer.7
  35.0 0.7 %collective-permute-start.8 = (f32[264,128]{1,0:T(8,128)S(1)}, f32[264,128]{1,0:T(8,128)S(1)}, u32[]{:S(2)}, u32[]{:S(2)}) collective-permute-start(f32[264,128]{1,0:T(8,128)S(1)} %get-tuple-element.136.refs_5_), channel_id=1, source_target_pairs={{1,2},{2,1},{3,4},{4,3},{5,6},{6,5},{7,8},{8,7},{9,10},{10,9},{11,... | collective-permute-start | bytes 405512 | tf_op jit(solution)/shard_map/ppermute | solution.py:801
  35.6 2.5 %inner.8 = (f32[1040,128]{1,0:T(8,128)S(1)}, f32[1040,128]{1,0:T(8,128)S(1)}, f32[1040,128]{1,0:T(8,128)S(1)}, f32[1040,128]{1,0:T(8,128)S(1)}, f32[32,128]{1,0:...) custom-call(s32[32]{0:T(128)S(4)} %get-tuple-element.82.cell_ref.refs, ...), custom_call_target="tpu_custom_call", output_to_operand_aliasing={{0}: (22, {}), {1}: (23, {})} | custom-call | flops 8000000 | bytes 6000000 | tf_op jit(solution)/shard_map/inner/pallas_call | solution.py:774
  38.1 3.2 %collective-permute-start.9 = (f32[264,128]{1,0:T(8,128)S(1)}, f32[264,128]{1,0:T(8,128)S(1)}, u32[]{:S(2)}, u32[]{:S(2)}) collective-permute-start(f32[264,128]{1,0:T(8,128)S(1)} %get-tuple-element.142), channel_id=1, source_target_pairs={{0,1},{1,0},{2,3},{3,2},{4,5},{5,4},{6,7},{7,6},{8,9},{9,8},{10,11... | collective-permute-start | bytes 405512 | tf_op jit(solution)/shard_map/ppermute | solution.py:798
  41.3 0.0 collective-permute-done.8.from_o.refs_2_
  41.3 0.1 facing.8
  41.4 0.9 %collective-permute-done.9.refs_3_.refs_21_ = f32[264,128]{1,0:T(8,128)S(1)} collective-permute-done((f32[264,128]{1,0:T(8,128)S(1)}, f32[264,128]{1,0:T(8,128)S(1)}, u32[]{:S(2)}, u32[]{:S(2)}) %collective-permute-start.9) | collective-permute-done | bytes 135200 | tf_op jit(solution)/shard_map/ppermute | solution.py:798
  42.3 0.3 outer.8
  42.6 0.7 %collective-permute-start.10 = (f32[264,128]{1,0:T(8,128)S(1)}, f32[264,128]{1,0:T(8,128)S(1)}, u32[]{:S(2)}, u32[]{:S(2)}) collective-permute-start(f32[264,128]{1,0:T(8,128)S(1)} %get-tuple-element.147.refs_5_), channel_id=1, source_target_pairs={{1,2},{2,1},{3,4},{4,3},{5,6},{6,5},{7,8},{8,7},{9,10},{10,9},{11,... | collective-permute-start | bytes 405512 | tf_op jit(solution)/shard_map/ppermute | solution.py:801
  43.2 2.5 %inner.9 = (f32[1040,128]{1,0:T(8,128)S(1)}, f32[1040,128]{1,0:T(8,128)S(1)}, f32[1040,128]{1,0:T(8,128)S(1)}, f32[1040,128]{1,0:T(8,128)S(1)}, f32[32,128]{1,0:...) custom-call(s32[32]{0:T(128)S(4)} %get-tuple-element.82.cell_ref.refs, ...), custom_call_target="tpu_custom_call", output_to_operand_aliasing={{0}: (22, {}), {1}: (23, {})} | custom-call | flops 8000000 | bytes 6000000 | tf_op jit(solution)/shard_map/inner/pallas_call | solution.py:774
  45.8 3.2 %collective-permute-start.11 = (f32[264,128]{1,0:T(8,128)S(1)}, f32[264,128]{1,0:T(8,128)S(1)}, u32[]{:S(2)}, u32[]{:S(2)}) collective-permute-start(f32[264,128]{1,0:T(8,128)S(1)} %get-tuple-element.152), channel_id=1, source_target_pairs={{0,1},{1,0},{2,3},{3,2},{4,5},{5,4},{6,7},{7,6},{8,9},{9,8},{10,11... | collective-permute-start | bytes 405512 | tf_op jit(solution)/shard_map/ppermute | solution.py:798
  49.0 0.0 collective-permute-done.10.from_o.refs_2_
  49.0 0.1 facing.9
  49.1 0.9 %collective-permute-done.11.refs_3_.from_e = f32[264,128]{1,0:T(8,128)S(1)} collective-permute-done((f32[264,128]{1,0:T(8,128)S(1)}, f32[264,128]{1,0:T(8,128)S(1)}, u32[]{:S(2)}, u32[]{:S(2)}) %collective-permute-start.11) | collective-permute-done | bytes 135200 | tf_op jit(solution)/shard_map/ppermute | solution.py:798
  50.0 0.9 %outer.9 = (f32[264,128]{1,0:T(8,128)S(1)}, f32[32,128]{1,0:T(8,128)S(1)}, f32[16,1,128]{2,1,0:T(1,128)}) custom-call(s32[32]{0:T(128)S(4)} %get-tuple-element.82.cell_ref.refs_0_, f32[264,128]{1,0:T(8,128)S(1)} %get-tuple-element.151.refs_1_, f32[264,128]{1,0:T(8,128)S(1)} %collective-permute-done.10.from_o.refs_2_, ...), custom_call_target="tpu_custom_call", output_to_operand_aliasing={{0}: (1, {})} | custom-call | flops 4000000 | bytes 3000000 | tf_op jit(solution)/shard_map/outer/pallas_call | solution.py:774
  50.8 6.2 %all-to-all-start = ((f32[16,1,128]{2,1,0:T(1,128)}), f32[16,1,128]{2,1,0:T(1,128)S(1)}, u32[]{:S(2)}, u32[]{:S(2)}) async-start(f32[16,1,128]{2,1,0:T(1,128)} %get-tuple-element.160), calls=%async_computation | async-start | bytes 16384 | tf_op jit(solution)/shard_map/all_to_all | solution.py:890
  57.1 1.5 %final.1 = (f32[1040,128]{1,0:T(8,128)S(1)}, f32[1040,128]{1,0:T(8,128)S(1)}, f32[1024,128]{1,0:T(8,128)}, f32[1024,128]{1,0:T(8,128)}) custom-call(s32[32]{0:T(128)S(4)} %get-tuple-element.82.cell_ref.refs_0_, f32[1040,128]{1,0:T(8,128)S(1)} %get-tuple-element.149.p_ref.p_in, ...), custom_call_target="tpu_custom_call", output_to_operand_aliasing={{0}: (1, {}), {1}: (2, {})} | custom-call | flops 8000000 | bytes 6000000 | tf_op jit(solution)/shard_map/final/pallas_call | solution.py:774
  58.6 4.9 %all-to-all-done = f32[16,1,128]{2,1,0:T(1,128)S(1)} async-done(((f32[16,1,128]{2,1,0:T(1,128)}), f32[16,1,128]{2,1,0:T(1,128)S(1)}, u32[]{:S(2)}, u32[]{:S(2)}) %all-to-all-start) | async-done | bytes 8224 | tf_op jit(solution)/shard_map/all_to_all | solution.py:890
  63.5 0.5 reduce_sum.9
Async XLA Ops:
  1.5 8.5 %collective-permute-start = (f32[136,128]{1,0:T(8,128)S(1)}, f32[136,128]{1,0:T(8,128)S(1)}, u32[]{:S(2)}, u32[]{:S(2)}) collective-permute-start(f32[136,128]{1,0:T(8,128)S(1)} %get-tuple-element.83), channel_id=1, source_target_pairs={{1,2},{2,1},{3,4},{4,3},{5,6},{6,5},{7,8},{8,7},{9,10},{10,9},{11,... | collective-permute-start | bytes 208904 | tf_op jit(solution)/shard_map/ppermute | solution.py:801
  2.2 7.8 %collective-permute-start.1 = (f32[136,128]{1,0:T(8,128)S(1)}, f32[136,128]{1,0:T(8,128)S(1)}, u32[]{:S(2)}, u32[]{:S(2)}) collective-permute-start(f32[136,128]{1,0:T(8,128)S(1)} %get-tuple-element.83), channel_id=1, source_target_pairs={{0,1},{1,0},{2,3},{3,2},{4,5},{5,4},{6,7},{7,6},{8,9},{9,8},{10,11... | collective-permute-start | bytes 208904 | tf_op jit(solution)/shard_map/ppermute | solution.py:798
  11.4 7.4 %collective-permute-start.2 = (f32[264,128]{1,0:T(8,128)S(1)}, f32[264,128]{1,0:T(8,128)S(1)}, u32[]{:S(2)}, u32[]{:S(2)}) collective-permute-start(f32[264,128]{1,0:T(8,128)S(1)} %get-tuple-element.94.refs_5_), channel_id=1, source_target_pairs={{1,2},{2,1},{3,4},{4,3},{5,6},{6,5},{7,8},{8,7},{9,10},{10,9},{11,... | collective-permute-start | bytes 405512 | tf_op jit(solution)/shard_map/ppermute | solution.py:801
  16.0 3.9 %collective-permute-start.3 = (f32[264,128]{1,0:T(8,128)S(1)}, f32[264,128]{1,0:T(8,128)S(1)}, u32[]{:S(2)}, u32[]{:S(2)}) collective-permute-start(f32[264,128]{1,0:T(8,128)S(1)} %get-tuple-element.111), channel_id=1, source_target_pairs={{0,1},{1,0},{2,3},{3,2},{4,5},{5,4},{6,7},{7,6},{8,9},{9,8},{10,11... | collective-permute-start | bytes 405512 | tf_op jit(solution)/shard_map/ppermute | solution.py:798
  20.1 6.2 %collective-permute-start.4 = (f32[264,128]{1,0:T(8,128)S(1)}, f32[264,128]{1,0:T(8,128)S(1)}, u32[]{:S(2)}, u32[]{:S(2)}) collective-permute-start(f32[264,128]{1,0:T(8,128)S(1)} %get-tuple-element.116.refs_5_), channel_id=1, source_target_pairs={{1,2},{2,1},{3,4},{4,3},{5,6},{6,5},{7,8},{8,7},{9,10},{10,9},{11,... | collective-permute-start | bytes 405512 | tf_op jit(solution)/shard_map/ppermute | solution.py:801
  23.4 3.9 %collective-permute-start.5 = (f32[264,128]{1,0:T(8,128)S(1)}, f32[264,128]{1,0:T(8,128)S(1)}, u32[]{:S(2)}, u32[]{:S(2)}) collective-permute-start(f32[264,128]{1,0:T(8,128)S(1)} %get-tuple-element.122), channel_id=1, source_target_pairs={{0,1},{1,0},{2,3},{3,2},{4,5},{5,4},{6,7},{7,6},{8,9},{9,8},{10,11... | collective-permute-start | bytes 405512 | tf_op jit(solution)/shard_map/ppermute | solution.py:798
  27.6 6.1 %collective-permute-start.6 = (f32[264,128]{1,0:T(8,128)S(1)}, f32[264,128]{1,0:T(8,128)S(1)}, u32[]{:S(2)}, u32[]{:S(2)}) collective-permute-start(f32[264,128]{1,0:T(8,128)S(1)} %get-tuple-element.126.refs_5_), channel_id=1, source_target_pairs={{1,2},{2,1},{3,4},{4,3},{5,6},{6,5},{7,8},{8,7},{9,10},{10,9},{11,... | collective-permute-start | bytes 405512 | tf_op jit(solution)/shard_map/ppermute | solution.py:801
  30.8 3.9 %collective-permute-start.7 = (f32[264,128]{1,0:T(8,128)S(1)}, f32[264,128]{1,0:T(8,128)S(1)}, u32[]{:S(2)}, u32[]{:S(2)}) collective-permute-start(f32[264,128]{1,0:T(8,128)S(1)} %get-tuple-element.132), channel_id=1, source_target_pairs={{0,1},{1,0},{2,3},{3,2},{4,5},{5,4},{6,7},{7,6},{8,9},{9,8},{10,11... | collective-permute-start | bytes 405512 | tf_op jit(solution)/shard_map/ppermute | solution.py:798
  35.0 6.3 %collective-permute-start.8 = (f32[264,128]{1,0:T(8,128)S(1)}, f32[264,128]{1,0:T(8,128)S(1)}, u32[]{:S(2)}, u32[]{:S(2)}) collective-permute-start(f32[264,128]{1,0:T(8,128)S(1)} %get-tuple-element.136.refs_5_), channel_id=1, source_target_pairs={{1,2},{2,1},{3,4},{4,3},{5,6},{6,5},{7,8},{8,7},{9,10},{10,9},{11,... | collective-permute-start | bytes 405512 | tf_op jit(solution)/shard_map/ppermute | solution.py:801
  38.1 4.2 %collective-permute-start.9 = (f32[264,128]{1,0:T(8,128)S(1)}, f32[264,128]{1,0:T(8,128)S(1)}, u32[]{:S(2)}, u32[]{:S(2)}) collective-permute-start(f32[264,128]{1,0:T(8,128)S(1)} %get-tuple-element.142), channel_id=1, source_target_pairs={{0,1},{1,0},{2,3},{3,2},{4,5},{5,4},{6,7},{7,6},{8,9},{9,8},{10,11... | collective-permute-start | bytes 405512 | tf_op jit(solution)/shard_map/ppermute | solution.py:798
  42.6 6.4 %collective-permute-start.10 = (f32[264,128]{1,0:T(8,128)S(1)}, f32[264,128]{1,0:T(8,128)S(1)}, u32[]{:S(2)}, u32[]{:S(2)}) collective-permute-start(f32[264,128]{1,0:T(8,128)S(1)} %get-tuple-element.147.refs_5_), channel_id=1, source_target_pairs={{1,2},{2,1},{3,4},{4,3},{5,6},{6,5},{7,8},{8,7},{9,10},{10,9},{11,... | collective-permute-start | bytes 405512 | tf_op jit(solution)/shard_map/ppermute | solution.py:801
  45.8 4.2 %collective-permute-start.11 = (f32[264,128]{1,0:T(8,128)S(1)}, f32[264,128]{1,0:T(8,128)S(1)}, u32[]{:S(2)}, u32[]{:S(2)}) collective-permute-start(f32[264,128]{1,0:T(8,128)S(1)} %get-tuple-element.152), channel_id=1, source_target_pairs={{0,1},{1,0},{2,3},{3,2},{4,5},{5,4},{6,7},{7,6},{8,9},{9,8},{10,11... | collective-permute-start | bytes 405512 | tf_op jit(solution)/shard_map/ppermute | solution.py:798
  50.8 12.6 %all-to-all-start = ((f32[16,1,128]{2,1,0:T(1,128)}), f32[16,1,128]{2,1,0:T(1,128)S(1)}, u32[]{:S(2)}, u32[]{:S(2)}) async-start(f32[16,1,128]{2,1,0:T(1,128)} %get-tuple-element.160), calls=%async_computation | async-start | bytes 16384 | tf_op jit(solution)/shard_map/all_to_all | solution.py:890

commit v7 on v6

--- a/solution.py
+++ b/solution.py
@@ -104,6 +104,8 @@
     sizes,
     cell_hbm,
     index_hbm,
+    rhs_hbm,
+    slot_hbm,
     tx_hbm,
     ty_hbm,
     tz_hbm,
@@ -128,6 +130,9 @@
     extra_ref,
     weight_ref,
     y_ref,
+    p_ref,
+    s_ref,
+    lanes_ref,
     raw_tx,
     raw_ty,
     raw_tz,
@@ -141,6 +146,8 @@
     cwi_ref,
     cell_ref,
     index_ref,
+    rhs_ref,
+    slot_ref,
     sems,
     fetch_sems,
 ):
@@ -170,10 +177,8 @@
             )
         return found
 
-    fetches = [
-        pltpu.make_async_copy(src, dst, fetch_sems.at[i])
-        for i, (src, dst) in enumerate(((cell_hbm, cell_ref), (index_hbm, index_ref)))
-    ]
+    wanted = ((cell_hbm, cell_ref), (index_hbm, index_ref), (rhs_hbm, rhs_ref), (slot_hbm, slot_ref))
+    fetches = [pltpu.make_async_copy(src, dst, fetch_sems.at[i]) for i, (src, dst) in enumerate(wanted)]
     for fetch in fetches:
         fetch.start()
     for c in range(CHUNKS):
@@ -190,6 +195,11 @@
 
     for fetch in fetches:
         fetch.wait()
+    clear_ends(rows, p_ref, s_ref)
+    place = lax.axis_index("gx")
+    behind = jnp.maximum(place - 1, 0)
+    for i, (ref, whose) in enumerate(((rhs_ref, place), (rhs_ref, behind), (slot_ref, place), (slot_ref, behind))):
+        lanes_ref[i * groups : (i + 1) * groups, :] = own_lanes(ref, whose, groups)
     spot = iota((SUB, LANES), 0) * LANES + iota((SUB, LANES), 1)
     for g in range(groups):
         _, y, _ = split_cell(cell_ref[g * run], ny)
@@ -252,10 +262,15 @@
                     is_ = 1.0 / ds
                     ip_ref[at, :] = ip
                 cc_ref[at, :] = coupling * ip
-                rp_ref[at, :] = rhs_p * ip
-                rs_ref[at, :] = rhs_s * is_
+                rp, rs, xx = rhs_p * ip, rhs_s * is_, cross * is_
+                rp_ref[at, :] = rp
+                rs_ref[at, :] = rs
                 uu_ref[at, :] = upwind * is_
-                xx_ref[at, :] = cross * is_
+                xx_ref[at, :] = xx
+                if x > 0:
+                    to = pl.ds(y0 + (x * ny + SUB), SUB)
+                    p_ref[to, :] = rp
+                    s_ref[to, :] = rs - xx * rp
                 txl = tx
 
 
@@ -360,8 +375,6 @@
     from_o,
     from_e,
     wells_ref,
-    rhs_hbm,
-    slot_hbm,
     tx_ref,
     rp_ref,
     ip_ref,
@@ -371,6 +384,11 @@
     xx_ref,
     extra_ref,
     weight_ref,
+    lanes_ref,
+    p_in,
+    s_in,
+    p_ref,
+    s_ref,
     edge_ref,
     plane_e,
     plane_o,
@@ -382,20 +400,11 @@
     sums_out,
     send_o,
     rows_ref,
-    rhs_ref,
-    slot_ref,
-    sems,
 ):
     ny, planes, groups = sizes.ny, sizes.planes, sizes.groups
     place = lax.axis_index("gx")
     even = place % 2 == 0
     x_o, _ = facing(sizes, even)
-    fetches = [
-        pltpu.make_async_copy(rhs_hbm, rhs_ref, sems.at[0]),
-        pltpu.make_async_copy(slot_hbm, slot_ref, sems.at[1]),
-    ]
-    for fetch in fetches:
-        fetch.start()
 
     @pl.loop(0, ny // SUB)
     def _(r):
@@ -417,9 +426,12 @@
             plane_o[to, :] = jnp.where(even, low[i], high[i])
             plane_e[to, :] = jnp.where(even, high[i], low[i])
         rp_end = rp_ref[end, :]
+        s0 = rs - xx * rp
+        p_ref[pl.ds(y0 + SUB, SUB), :] = rp
+        s_ref[pl.ds(y0 + SUB, SUB), :] = s0
         send_o[at, :] = jnp.where(even, rp, rp_end)
         send_o[pl.ds(y0 + ny, SUB), :] = jnp.where(
-            even, rs - xx * rp, rs_ref[end, :] - xx_ref[end, :] * rp_end
+            even, s0, rs_ref[end, :] - xx_ref[end, :] * rp_end
         )
 
     sub = iota((SUB, LANES), 0)
@@ -444,10 +456,9 @@
     is_before = before > 0.5
     sum_own = mine * (1.0 - before) + column_of(high[1:2, :], groups)
     sum_before = mine * before + column_of(low[0:1, :], groups)
-    for fetch in fetches:
-        fetch.wait()
-    rhs_own = own_lanes(rhs_ref, place, groups)
-    rhs_before = own_lanes(rhs_ref, jnp.maximum(place - 1, 0), groups)
+    rhs_own, rhs_before, slot_own, slot_before = [
+        lanes_ref[i * groups : (i + 1) * groups, :] for i in range(4)
+    ]
     inv_own = 1.0 / (1.5 * sum_own + 0.5)
     inv_before = 1.0 / (1.5 * sum_before + 0.5)
     rhs = jnp.where(is_before, rhs_before, rhs_own)
@@ -459,8 +470,8 @@
         SUM_OWN: sum_own,
         RHS: rhs,
         INV: inv,
-        SLOT_OWN: own_lanes(slot_ref, place, groups),
-        SLOT_BEFORE: own_lanes(slot_ref, jnp.maximum(place - 1, 0), groups),
+        SLOT_OWN: slot_own,
+        SLOT_BEFORE: slot_before,
     }
     for i, entry in entries.items():
         table_ref[i * groups : (i + 1) * groups, :] = entry
@@ -556,22 +567,8 @@
     rows = planes * ny
     even = lax.axis_index("gx") % 2 == 0
     if first:
-        plane_o, p_old, s_old, p_ref, s_ref, rows_ref, sums_out, send_e, near_ref = refs
+        plane_o, _, _, p_old, s_old, p_ref, s_ref, rows_ref, sums_out, send_e, near_ref = refs
         halo = None
-        clear_ends(rows, p_old, s_old)
-
-        @pl.loop(0, ny // SUB)
-        def _(r):
-            y0 = pl.multiple_of(r * SUB, SUB)
-            for x in range(planes):
-                at, to = pl.ds(y0 + x * ny, SUB), pl.ds(y0 + (x * ny + SUB), SUB)
-                if x == 0:
-                    rp, rs, xx = [edge_ref[pl.ds(y0 + i * ny, SUB), :] for i in (2, 3, 5)]
-                else:
-                    rp, rs, xx = rp_ref[at, :], rs_ref[at, :], xx_ref[at, :]
-                p_old[to, :] = rp
-                s_old[to, :] = rs - xx * rp
-
         near_weights(sizes, cell_ref, weight_ref, plane_e, plane_o, near_ref)
     else:
         halo, _, _, p_old, s_old, p_ref, s_ref, rows_ref, sums_out, send_e = refs
@@ -815,9 +812,10 @@
     big = [trans_x, trans_y, trans_z, accel, coupling, upwind, storage, rhs_pressure, rhs_saturation, cross]
     made = call(
         functools.partial(setup_kernel, sizes),
-        [perf_cell, perf_index] + big,
-        [HBM] * (2 + len(big)),
-        [vmem(rows)] * 11 + [vmem(3 * ny), vmem(groups * SUB), SMEM((groups,), jnp.int32)],
+        [perf_cell, perf_index, lines(well_rhs), lines(well_slot)] + big,
+        [HBM] * (4 + len(big)),
+        [vmem(rows)] * 11 + [vmem(3 * ny), vmem(groups * SUB), SMEM((groups,), jnp.int32)]
+        + [vmem(padded), vmem(padded), vmem(4 * groups)],
         [
             VMEM((planes, ny, LANES), F32),
             VMEM((planes, ny + SUB, LANES), F32),
@@ -827,33 +825,30 @@
             VMEM((rows, LANES), F32),
             SMEM(perf_cell.shape, jnp.int32),
             SMEM(perf_index.shape, F32),
+            VMEM(lines(well_rhs).shape, F32),
+            VMEM(lines(well_slot).shape, jnp.int32),
             DMA((CHUNKS, 10)),
-            DMA((2,)),
+            DMA((4,)),
         ],
         "setup",
         4,
     )
-    coefficients, (extra, weight, y) = list(made[:11]), made[11:]
+    coefficients, (extra, weight, y, p, s, lanes) = list(made[:11]), made[11:]
     group_row = VMEM((groups, LANES), F32)
     fields = [vmem(padded), vmem(padded)]
     block = vmem(2 * ny + SUB)
     slabs = vmem(groups * SUB)
-    edge, plane_e, plane_o, wp, ws, shared, table, mu, sums, send_o = call(
+    p, s, edge, plane_e, plane_o, wp, ws, shared, table, mu, sums, send_o = call(
         functools.partial(start_kernel, sizes),
-        [y, from_o, from_e, wells, lines(well_rhs), lines(well_slot), coefficients[0]]
-        + coefficients[5:]
-        + [extra, weight],
-        [SMEM] + [VMEM] * 3 + [HBM] * 2 + [VMEM] * 9,
-        [vmem(6 * ny), vmem(4 * ny), vmem(4 * ny), slabs, slabs, vmem(groups), vmem(TABLE * groups)]
+        [y, from_o, from_e, wells, coefficients[0]] + coefficients[5:] + [extra, weight, lanes, p, s],
+        [SMEM] + [VMEM] * 15,
+        fields
+        + [vmem(6 * ny), vmem(4 * ny), vmem(4 * ny), slabs, slabs, vmem(groups), vmem(TABLE * groups)]
         + [vmem(groups), vmem(groups), block],
-        [
-            group_row,
-            VMEM(lines(well_rhs).shape, F32),
-            VMEM(lines(well_slot).shape, jnp.int32),
-            DMA((2,)),
-        ],
+        [group_row],
         "start",
         2,
+        {14: 0, 15: 1},
     )
     near = None
     for sweep in range(1, SWEEPS):
@@ -864,12 +859,12 @@
             lambda sz, *refs: inner_kernel(sz, first, *refs),
             [mu, wp, ws, weight, send_o, sums, table]
             + coefficients
-            + ([edge, plane_e, plane_o] if first else [edge, plane_e, from_e, p, s]),
+            + [edge, plane_e, plane_o if first else from_e, p, s],
             fields + fields + [vmem(groups), vmem(groups), block] + ([vmem(4 * groups)] if first else []),
             [],
             "inner",
             2,
-            {} if first else {22: 0, 23: 1},
+            {22: 0, 23: 1},
         )
         if first:
             near = rest[0]

time: 64.4 us -> 65.7 us (1.020)
  starting transfers between devices: 29.8 us -> 31.1 us
    ppermute x6, starting transfers between devices: 19.6 us -> 21.9 us  [to_core(): return lax.ppermute(block, 'gx', pairs_e)]
    all_to_all x1, starting transfers between devices: 6.23 us -> 5.17 us  [body(): grads = lax.all_to_all(sums, 'gx', 0, 0)]
where the time goes in v7:
time: 65.7 us; the launch traced here: 65.4 us
  starting transfers between devices  31.1 us (47%)
  Pallas kernels  23.5 us (36%)
  waiting for transfers between devices  9.52 us (14%)
  between operations  0.77 us (1%)
    pallas_call x19, Pallas kernels, call(): pl.pallas_call(kernel, in_specs=[spec(space) for space in spaces], out_sp...  23.5 us
    ppermute x6, starting transfers between devices, to_core(): return lax.ppermute(block, 'gx', pairs_e)  21.9 us
    all_to_all x1, starting transfers between devices, body(): grads = lax.all_to_all(sums, 'gx', 0, 0)  5.17 us
    all_to_all x1, waiting for transfers between devices, body(): grads = lax.all_to_all(sums, 'gx', 0, 0)  4.9 us
    ppermute x6, waiting for transfers between devices, to_core(): return lax.ppermute(block, 'gx', pairs_e)  4.6 us
    ppermute x6, starting transfers between devices, to_chip(): return lax.ppermute(block, 'gx', pairs_o)  4 us
  transfers between devices with their start and end apart: 13, of which 6 were waited for; matrix products, arithmetic and copies ran while one was open for 0% of the time, Pallas kernels for 30%

profile of v7, /device:TPU:0, one launch (start us, length us, event | category | flops | bytes accessed | tf_op | source)
XLA Modules:
  0.0 65.4 jit_solution(2267797590900020157)
XLA Ops:
  0.6 0.9 %first.1 = (f32[136,128]{1,0:T(8,128)S(1)}, f32[64,128]{1,0:T(8,128)S(1)}) custom-call(f32[1024,128]{1,0:T(8,128)} %bitcast.8, s32[2,128]{1,0:T(2,128)} %bitcast.12, f32[2,128]{1,0:T(2,128)} %bitcast.9), custom_call_target="tpu_custom_call" | custom-call | flops 4000000 | bytes 3000000 | tf_op jit(solution)/shard_map/first/pallas_call | solution.py:771
  1.5 0.7 %collective-permute-start = (f32[136,128]{1,0:T(8,128)S(1)}, f32[136,128]{1,0:T(8,128)S(1)}, u32[]{:S(2)}, u32[]{:S(2)}) collective-permute-start(f32[136,128]{1,0:T(8,128)S(1)} %get-tuple-element.88), channel_id=1, source_target_pairs={{1,2},{2,1},{3,4},{4,3},{5,6},{6,5},{7,8},{8,7},{9,10},{10,9},{11,... | collective-permute-start | bytes 208904 | tf_op jit(solution)/shard_map/ppermute | solution.py:798
  2.2 4.4 %collective-permute-start.1 = (f32[136,128]{1,0:T(8,128)S(1)}, f32[136,128]{1,0:T(8,128)S(1)}, u32[]{:S(2)}, u32[]{:S(2)}) collective-permute-start(f32[136,128]{1,0:T(8,128)S(1)} %get-tuple-element.88), channel_id=1, source_target_pairs={{0,1},{1,0},{2,3},{3,2},{4,5},{5,4},{6,7},{7,6},{8,9},{9,8},{10,11... | collective-permute-start | bytes 208904 | tf_op jit(solution)/shard_map/ppermute | solution.py:795
  6.6 4.9 %setup.1 = (f32[1024,128]{1,0:T(8,128)S(1)}, f32[1024,128]{1,0:T(8,128)S(1)}, f32[1024,128]{1,0:T(8,128)S(1)}, f32[1024,128]{1,0:T(8,128)S(1)}, f32[1024,128]{1,...) custom-call(s32[256]{0:T(256)} %cell_hbm.1, ...), custom_call_target="tpu_custom_call" | custom-call | flops 16000000 | bytes 12000000 | tf_op jit(solution)/shard_map/setup/pallas_call | solution.py:771
  11.5 0.0 collective-permute-done.from_o
  11.6 0.0 collective-permute-done.1.from_e
  11.6 1.2 %start.1 = (f32[1040,128]{1,0:T(8,128)S(1)}, f32[1040,128]{1,0:T(8,128)S(1)}, f32[768,128]{1,0:T(8,128)S(1)}, f32[512,128]{1,0:T(8,128)S(1)}, f32[512,128]{1,0:T...) custom-call(s32[32]{0:T(128)S(4)} %get-tuple-element.87.cell_ref.ref, ...), custom_call_target="tpu_custom_call", output_to_operand_aliasing={{0}: (14, {}), {1}: (15, {})} | custom-call | flops 8000000 | bytes 6000000 | tf_op jit(solution)/shard_map/start/pallas_call | solution.py:771
  12.8 0.7 %collective-permute-start.2 = (f32[264,128]{1,0:T(8,128)S(1)}, f32[264,128]{1,0:T(8,128)S(1)}, u32[]{:S(2)}, u32[]{:S(2)}) collective-permute-start(f32[264,128]{1,0:T(8,128)S(1)} %get-tuple-element.102.refs_5_), channel_id=1, source_target_pairs={{1,2},{2,1},{3,4},{4,3},{5,6},{6,5},{7,8},{8,7},{9,10},{10,9},{11,... | collective-permute-start | bytes 405512 | tf_op jit(solution)/shard_map/ppermute | solution.py:798
  13.4 2.6 %inner.5 = (f32[1040,128]{1,0:T(8,128)S(1)}, f32[1040,128]{1,0:T(8,128)S(1)}, f32[1040,128]{1,0:T(8,128)S(1)}, f32[1040,128]{1,0:T(8,128)S(1)}, f32[32,128]{1,0:...) custom-call(s32[32]{0:T(128)S(4)} %get-tuple-element.87.cell_ref.ref, ...), custom_call_target="tpu_custom_call", output_to_operand_aliasing={{0}: (22, {}), {1}: (23, {})} | custom-call | flops 8000000 | bytes 6000000 | tf_op jit(solution)/shard_map/inner/pallas_call | solution.py:771
  16.1 2.9 %collective-permute-start.3 = (f32[264,128]{1,0:T(8,128)S(1)}, f32[264,128]{1,0:T(8,128)S(1)}, u32[]{:S(2)}, u32[]{:S(2)}) collective-permute-start(f32[264,128]{1,0:T(8,128)S(1)} %get-tuple-element.121), channel_id=1, source_target_pairs={{0,1},{1,0},{2,3},{3,2},{4,5},{5,4},{6,7},{7,6},{8,9},{9,8},{10,11... | collective-permute-start | bytes 405512 | tf_op jit(solution)/shard_map/ppermute | solution.py:795
  19.0 0.0 collective-permute-done.2.from_o.refs_2_
  19.0 0.1 facing.5
  19.1 0.9 %collective-permute-done.3.refs_3_.refs_21_ = f32[264,128]{1,0:T(8,128)S(1)} collective-permute-done((f32[264,128]{1,0:T(8,128)S(1)}, f32[264,128]{1,0:T(8,128)S(1)}, u32[]{:S(2)}, u32[]{:S(2)}) %collective-permute-start.3) | collective-permute-done | bytes 135200 | tf_op jit(solution)/shard_map/ppermute | solution.py:795
  20.0 0.3 outer.5
  20.3 0.7 %collective-permute-start.4 = (f32[264,128]{1,0:T(8,128)S(1)}, f32[264,128]{1,0:T(8,128)S(1)}, u32[]{:S(2)}, u32[]{:S(2)}) collective-permute-start(f32[264,128]{1,0:T(8,128)S(1)} %get-tuple-element.126.refs_5_), channel_id=1, source_target_pairs={{1,2},{2,1},{3,4},{4,3},{5,6},{6,5},{7,8},{8,7},{9,10},{10,9},{11,... | collective-permute-start | bytes 405512 | tf_op jit(solution)/shard_map/ppermute | solution.py:798
  20.9 2.5 %inner.6 = (f32[1040,128]{1,0:T(8,128)S(1)}, f32[1040,128]{1,0:T(8,128)S(1)}, f32[1040,128]{1,0:T(8,128)S(1)}, f32[1040,128]{1,0:T(8,128)S(1)}, f32[32,128]{1,0:...) custom-call(s32[32]{0:T(128)S(4)} %get-tuple-element.87.cell_ref.refs, ...), custom_call_target="tpu_custom_call", output_to_operand_aliasing={{0}: (22, {}), {1}: (23, {})} | custom-call | flops 8000000 | bytes 6000000 | tf_op jit(solution)/shard_map/inner/pallas_call | solution.py:771
  23.5 3.6 %collective-permute-start.5 = (f32[264,128]{1,0:T(8,128)S(1)}, f32[264,128]{1,0:T(8,128)S(1)}, u32[]{:S(2)}, u32[]{:S(2)}) collective-permute-start(f32[264,128]{1,0:T(8,128)S(1)} %get-tuple-element.132), channel_id=1, source_target_pairs={{0,1},{1,0},{2,3},{3,2},{4,5},{5,4},{6,7},{7,6},{8,9},{9,8},{10,11... | collective-permute-start | bytes 405512 | tf_op jit(solution)/shard_map/ppermute | solution.py:795
  27.0 0.0 collective-permute-done.4.from_o.refs_2_
  27.0 0.1 facing.6
  27.1 0.9 %collective-permute-done.5.refs_3_.refs_21_ = f32[264,128]{1,0:T(8,128)S(1)} collective-permute-done((f32[264,128]{1,0:T(8,128)S(1)}, f32[264,128]{1,0:T(8,128)S(1)}, u32[]{:S(2)}, u32[]{:S(2)}) %collective-permute-start.5) | collective-permute-done | bytes 135200 | tf_op jit(solution)/shard_map/ppermute | solution.py:795
  28.0 0.3 outer.6
  28.3 0.7 %collective-permute-start.6 = (f32[264,128]{1,0:T(8,128)S(1)}, f32[264,128]{1,0:T(8,128)S(1)}, u32[]{:S(2)}, u32[]{:S(2)}) collective-permute-start(f32[264,128]{1,0:T(8,128)S(1)} %get-tuple-element.136.refs_5_), channel_id=1, source_target_pairs={{1,2},{2,1},{3,4},{4,3},{5,6},{6,5},{7,8},{8,7},{9,10},{10,9},{11,... | collective-permute-start | bytes 405512 | tf_op jit(solution)/shard_map/ppermute | solution.py:798
  29.0 2.5 %inner.7 = (f32[1040,128]{1,0:T(8,128)S(1)}, f32[1040,128]{1,0:T(8,128)S(1)}, f32[1040,128]{1,0:T(8,128)S(1)}, f32[1040,128]{1,0:T(8,128)S(1)}, f32[32,128]{1,0:...) custom-call(s32[32]{0:T(128)S(4)} %get-tuple-element.87.cell_ref.refs, ...), custom_call_target="tpu_custom_call", output_to_operand_aliasing={{0}: (22, {}), {1}: (23, {})} | custom-call | flops 8000000 | bytes 6000000 | tf_op jit(solution)/shard_map/inner/pallas_call | solution.py:771
  31.5 3.7 %collective-permute-start.7 = (f32[264,128]{1,0:T(8,128)S(1)}, f32[264,128]{1,0:T(8,128)S(1)}, u32[]{:S(2)}, u32[]{:S(2)}) collective-permute-start(f32[264,128]{1,0:T(8,128)S(1)} %get-tuple-element.142), channel_id=1, source_target_pairs={{0,1},{1,0},{2,3},{3,2},{4,5},{5,4},{6,7},{7,6},{8,9},{9,8},{10,11... | collective-permute-start | bytes 405512 | tf_op jit(solution)/shard_map/ppermute | solution.py:795
  35.2 0.0 collective-permute-done.6.from_o.refs_2_
  35.2 0.1 facing.7
  35.2 0.9 %collective-permute-done.7.refs_3_.refs_21_ = f32[264,128]{1,0:T(8,128)S(1)} collective-permute-done((f32[264,128]{1,0:T(8,128)S(1)}, f32[264,128]{1,0:T(8,128)S(1)}, u32[]{:S(2)}, u32[]{:S(2)}) %collective-permute-start.7) | collective-permute-done | bytes 135200 | tf_op jit(solution)/shard_map/ppermute | solution.py:795
  36.2 0.3 outer.7
  36.4 0.7 %collective-permute-start.8 = (f32[264,128]{1,0:T(8,128)S(1)}, f32[264,128]{1,0:T(8,128)S(1)}, u32[]{:S(2)}, u32[]{:S(2)}) collective-permute-start(f32[264,128]{1,0:T(8,128)S(1)} %get-tuple-element.146.refs_5_), channel_id=1, source_target_pairs={{1,2},{2,1},{3,4},{4,3},{5,6},{6,5},{7,8},{8,7},{9,10},{10,9},{11,... | collective-permute-start | bytes 405512 | tf_op jit(solution)/shard_map/ppermute | solution.py:798
  37.1 2.5 %inner.8 = (f32[1040,128]{1,0:T(8,128)S(1)}, f32[1040,128]{1,0:T(8,128)S(1)}, f32[1040,128]{1,0:T(8,128)S(1)}, f32[1040,128]{1,0:T(8,128)S(1)}, f32[32,128]{1,0:...) custom-call(s32[32]{0:T(128)S(4)} %get-tuple-element.87.cell_ref.refs, ...), custom_call_target="tpu_custom_call", output_to_operand_aliasing={{0}: (22, {}), {1}: (23, {})} | custom-call | flops 8000000 | bytes 6000000 | tf_op jit(solution)/shard_map/inner/pallas_call | solution.py:771
  39.6 3.7 %collective-permute-start.9 = (f32[264,128]{1,0:T(8,128)S(1)}, f32[264,128]{1,0:T(8,128)S(1)}, u32[]{:S(2)}, u32[]{:S(2)}) collective-permute-start(f32[264,128]{1,0:T(8,128)S(1)} %get-tuple-element.152), channel_id=1, source_target_pairs={{0,1},{1,0},{2,3},{3,2},{4,5},{5,4},{6,7},{7,6},{8,9},{9,8},{10,11... | collective-permute-start | bytes 405512 | tf_op jit(solution)/shard_map/ppermute | solution.py:795
  43.3 0.0 collective-permute-done.8.from_o.refs_2_
  43.3 0.1 facing.8
  43.4 0.9 %collective-permute-done.9.refs_3_.refs_21_ = f32[264,128]{1,0:T(8,128)S(1)} collective-permute-done((f32[264,128]{1,0:T(8,128)S(1)}, f32[264,128]{1,0:T(8,128)S(1)}, u32[]{:S(2)}, u32[]{:S(2)}) %collective-permute-start.9) | collective-permute-done | bytes 135200 | tf_op jit(solution)/shard_map/ppermute | solution.py:795
  44.3 0.3 outer.8
  44.6 0.7 %collective-permute-start.10 = (f32[264,128]{1,0:T(8,128)S(1)}, f32[264,128]{1,0:T(8,128)S(1)}, u32[]{:S(2)}, u32[]{:S(2)}) collective-permute-start(f32[264,128]{1,0:T(8,128)S(1)} %get-tuple-element.157.refs_5_), channel_id=1, source_target_pairs={{1,2},{2,1},{3,4},{4,3},{5,6},{6,5},{7,8},{8,7},{9,10},{10,9},{11,... | collective-permute-start | bytes 405512 | tf_op jit(solution)/shard_map/ppermute | solution.py:798
  45.3 2.5 %inner.9 = (f32[1040,128]{1,0:T(8,128)S(1)}, f32[1040,128]{1,0:T(8,128)S(1)}, f32[1040,128]{1,0:T(8,128)S(1)}, f32[1040,128]{1,0:T(8,128)S(1)}, f32[32,128]{1,0:...) custom-call(s32[32]{0:T(128)S(4)} %get-tuple-element.87.cell_ref.refs, ...), custom_call_target="tpu_custom_call", output_to_operand_aliasing={{0}: (22, {}), {1}: (23, {})} | custom-call | flops 8000000 | bytes 6000000 | tf_op jit(solution)/shard_map/inner/pallas_call | solution.py:771
  47.8 3.6 %collective-permute-start.11 = (f32[264,128]{1,0:T(8,128)S(1)}, f32[264,128]{1,0:T(8,128)S(1)}, u32[]{:S(2)}, u32[]{:S(2)}) collective-permute-start(f32[264,128]{1,0:T(8,128)S(1)} %get-tuple-element.162), channel_id=1, source_target_pairs={{0,1},{1,0},{2,3},{3,2},{4,5},{5,4},{6,7},{7,6},{8,9},{9,8},{10,11... | collective-permute-start | bytes 405512 | tf_op jit(solution)/shard_map/ppermute | solution.py:795
  51.4 0.0 collective-permute-done.10.from_o.refs_2_
  51.4 0.1 facing.9
  51.5 0.9 %collective-permute-done.11.refs_3_.from_e = f32[264,128]{1,0:T(8,128)S(1)} collective-permute-done((f32[264,128]{1,0:T(8,128)S(1)}, f32[264,128]{1,0:T(8,128)S(1)}, u32[]{:S(2)}, u32[]{:S(2)}) %collective-permute-start.11) | collective-permute-done | bytes 135200 | tf_op jit(solution)/shard_map/ppermute | solution.py:795
  52.4 0.9 %outer.9 = (f32[264,128]{1,0:T(8,128)S(1)}, f32[32,128]{1,0:T(8,128)S(1)}, f32[16,1,128]{2,1,0:T(1,128)}) custom-call(s32[32]{0:T(128)S(4)} %get-tuple-element.87.cell_ref.refs_0_, f32[264,128]{1,0:T(8,128)S(1)} %get-tuple-element.161.refs_1_, f32[264,128]{1,0:T(8,128)S(1)} %collective-permute-done.10.from_o.refs_2_, ...), custom_call_target="tpu_custom_call", output_to_operand_aliasing={{0}: (1, {})} | custom-call | flops 4000000 | bytes 3000000 | tf_op jit(solution)/shard_map/outer/pallas_call | solution.py:771
  53.2 5.2 %all-to-all-start = ((f32[16,1,128]{2,1,0:T(1,128)}), f32[16,1,128]{2,1,0:T(1,128)S(1)}, u32[]{:S(2)}, u32[]{:S(2)}) async-start(f32[16,1,128]{2,1,0:T(1,128)} %get-tuple-element.170), calls=%async_computation | async-start | bytes 16384 | tf_op jit(solution)/shard_map/all_to_all | solution.py:885
  58.4 1.5 %final.1 = (f32[1040,128]{1,0:T(8,128)S(1)}, f32[1040,128]{1,0:T(8,128)S(1)}, f32[1024,128]{1,0:T(8,128)}, f32[1024,128]{1,0:T(8,128)}) custom-call(s32[32]{0:T(128)S(4)} %get-tuple-element.87.cell_ref.refs_0_, f32[1040,128]{1,0:T(8,128)S(1)} %get-tuple-element.159.p_ref.p_in, ...), custom_call_target="tpu_custom_call", output_to_operand_aliasing={{0}: (1, {}), {1}: (2, {})} | custom-call | flops 8000000 | bytes 6000000 | tf_op jit(solution)/shard_map/final/pallas_call | solution.py:771
  59.9 4.9 %all-to-all-done = f32[16,1,128]{2,1,0:T(1,128)S(1)} async-done(((f32[16,1,128]{2,1,0:T(1,128)}), f32[16,1,128]{2,1,0:T(1,128)S(1)}, u32[]{:S(2)}, u32[]{:S(2)}) %all-to-all-start) | async-done | bytes 8224 | tf_op jit(solution)/shard_map/all_to_all | solution.py:885
  64.8 0.5 reduce_sum.9
Async XLA Ops:
  1.5 10.0 %collective-permute-start = (f32[136,128]{1,0:T(8,128)S(1)}, f32[136,128]{1,0:T(8,128)S(1)}, u32[]{:S(2)}, u32[]{:S(2)}) collective-permute-start(f32[136,128]{1,0:T(8,128)S(1)} %get-tuple-element.88), channel_id=1, source_target_pairs={{1,2},{2,1},{3,4},{4,3},{5,6},{6,5},{7,8},{8,7},{9,10},{10,9},{11,... | collective-permute-start | bytes 208904 | tf_op jit(solution)/shard_map/ppermute | solution.py:798
  2.2 9.3 %collective-permute-start.1 = (f32[136,128]{1,0:T(8,128)S(1)}, f32[136,128]{1,0:T(8,128)S(1)}, u32[]{:S(2)}, u32[]{:S(2)}) collective-permute-start(f32[136,128]{1,0:T(8,128)S(1)} %get-tuple-element.88), channel_id=1, source_target_pairs={{0,1},{1,0},{2,3},{3,2},{4,5},{5,4},{6,7},{7,6},{8,9},{9,8},{10,11... | collective-permute-start | bytes 208904 | tf_op jit(solution)/shard_map/ppermute | solution.py:795
  12.8 6.2 %collective-permute-start.2 = (f32[264,128]{1,0:T(8,128)S(1)}, f32[264,128]{1,0:T(8,128)S(1)}, u32[]{:S(2)}, u32[]{:S(2)}) collective-permute-start(f32[264,128]{1,0:T(8,128)S(1)} %get-tuple-element.102.refs_5_), channel_id=1, source_target_pairs={{1,2},{2,1},{3,4},{4,3},{5,6},{6,5},{7,8},{8,7},{9,10},{10,9},{11,... | collective-permute-start | bytes 405512 | tf_op jit(solution)/shard_map/ppermute | solution.py:798
  16.1 3.9 %collective-permute-start.3 = (f32[264,128]{1,0:T(8,128)S(1)}, f32[264,128]{1,0:T(8,128)S(1)}, u32[]{:S(2)}, u32[]{:S(2)}) collective-permute-start(f32[264,128]{1,0:T(8,128)S(1)} %get-tuple-element.121), channel_id=1, source_target_pairs={{0,1},{1,0},{2,3},{3,2},{4,5},{5,4},{6,7},{7,6},{8,9},{9,8},{10,11... | collective-permute-start | bytes 405512 | tf_op jit(solution)/shard_map/ppermute | solution.py:795
  20.3 6.8 %collective-permute-start.4 = (f32[264,128]{1,0:T(8,128)S(1)}, f32[264,128]{1,0:T(8,128)S(1)}, u32[]{:S(2)}, u32[]{:S(2)}) collective-permute-start(f32[264,128]{1,0:T(8,128)S(1)} %get-tuple-element.126.refs_5_), channel_id=1, source_target_pairs={{1,2},{2,1},{3,4},{4,3},{5,6},{6,5},{7,8},{8,7},{9,10},{10,9},{11,... | collective-permute-start | bytes 405512 | tf_op jit(solution)/shard_map/ppermute | solution.py:798
  23.5 4.6 %collective-permute-start.5 = (f32[264,128]{1,0:T(8,128)S(1)}, f32[264,128]{1,0:T(8,128)S(1)}, u32[]{:S(2)}, u32[]{:S(2)}) collective-permute-start(f32[264,128]{1,0:T(8,128)S(1)} %get-tuple-element.132), channel_id=1, source_target_pairs={{0,1},{1,0},{2,3},{3,2},{4,5},{5,4},{6,7},{7,6},{8,9},{9,8},{10,11... | collective-permute-start | bytes 405512 | tf_op jit(solution)/shard_map/ppermute | solution.py:795
  28.3 6.9 %collective-permute-start.6 = (f32[264,128]{1,0:T(8,128)S(1)}, f32[264,128]{1,0:T(8,128)S(1)}, u32[]{:S(2)}, u32[]{:S(2)}) collective-permute-start(f32[264,128]{1,0:T(8,128)S(1)} %get-tuple-element.136.refs_5_), channel_id=1, source_target_pairs={{1,2},{2,1},{3,4},{4,3},{5,6},{6,5},{7,8},{8,7},{9,10},{10,9},{11,... | collective-permute-start | bytes 405512 | tf_op jit(solution)/shard_map/ppermute | solution.py:798
  31.5 4.7 %collective-permute-start.7 = (f32[264,128]{1,0:T(8,128)S(1)}, f32[264,128]{1,0:T(8,128)S(1)}, u32[]{:S(2)}, u32[]{:S(2)}) collective-permute-start(f32[264,128]{1,0:T(8,128)S(1)} %get-tuple-element.142), channel_id=1, source_target_pairs={{0,1},{1,0},{2,3},{3,2},{4,5},{5,4},{6,7},{7,6},{8,9},{9,8},{10,11... | collective-permute-start | bytes 405512 | tf_op jit(solution)/shard_map/ppermute | solution.py:795
  36.4 6.9 %collective-permute-start.8 = (f32[264,128]{1,0:T(8,128)S(1)}, f32[264,128]{1,0:T(8,128)S(1)}, u32[]{:S(2)}, u32[]{:S(2)}) collective-permute-start(f32[264,128]{1,0:T(8,128)S(1)} %get-tuple-element.146.refs_5_), channel_id=1, source_target_pairs={{1,2},{2,1},{3,4},{4,3},{5,6},{6,5},{7,8},{8,7},{9,10},{10,9},{11,... | collective-permute-start | bytes 405512 | tf_op jit(solution)/shard_map/ppermute | solution.py:798
  39.6 4.7 %collective-permute-start.9 = (f32[264,128]{1,0:T(8,128)S(1)}, f32[264,128]{1,0:T(8,128)S(1)}, u32[]{:S(2)}, u32[]{:S(2)}) collective-permute-start(f32[264,128]{1,0:T(8,128)S(1)} %get-tuple-element.152), channel_id=1, source_target_pairs={{0,1},{1,0},{2,3},{3,2},{4,5},{5,4},{6,7},{7,6},{8,9},{9,8},{10,11... | collective-permute-start | bytes 405512 | tf_op jit(solution)/shard_map/ppermute | solution.py:795
  44.6 6.8 %collective-permute-start.10 = (f32[264,128]{1,0:T(8,128)S(1)}, f32[264,128]{1,0:T(8,128)S(1)}, u32[]{:S(2)}, u32[]{:S(2)}) collective-permute-start(f32[264,128]{1,0:T(8,128)S(1)} %get-tuple-element.157.refs_5_), channel_id=1, source_target_pairs={{1,2},{2,1},{3,4},{4,3},{5,6},{6,5},{7,8},{8,7},{9,10},{10,9},{11,... | collective-permute-start | bytes 405512 | tf_op jit(solution)/shard_map/ppermute | solution.py:798
  47.8 4.6 %collective-permute-start.11 = (f32[264,128]{1,0:T(8,128)S(1)}, f32[264,128]{1,0:T(8,128)S(1)}, u32[]{:S(2)}, u32[]{:S(2)}) collective-permute-start(f32[264,128]{1,0:T(8,128)S(1)} %get-tuple-element.162), channel_id=1, source_target_pairs={{0,1},{1,0},{2,3},{3,2},{4,5},{5,4},{6,7},{7,6},{8,9},{9,8},{10,11... | collective-permute-start | bytes 405512 | tf_op jit(solution)/shard_map/ppermute | solution.py:795
  53.2 11.6 %all-to-all-start = ((f32[16,1,128]{2,1,0:T(1,128)}), f32[16,1,128]{2,1,0:T(1,128)S(1)}, u32[]{:S(2)}, u32[]{:S(2)}) async-start(f32[16,1,128]{2,1,0:T(1,128)} %get-tuple-element.170), calls=%async_computation | async-start | bytes 16384 | tf_op jit(solution)/shard_map/all_to_all | solution.py:885

commit v8 on v6

--- a/solution.py
+++ b/solution.py
@@ -62,14 +62,18 @@
     )
 
 
-def first_kernel(sizes, tx_hbm, well_hbm, index_hbm, send_ref, wells_ref, well_ref, index_ref, sems):
+def first_kernel(
+    sizes, tx_hbm, well_hbm, index_hbm, rhs_hbm, slot_hbm, send_ref, wells_ref, well_ref, index_ref, rhs_ref, slot_ref, sems
+):
     ny, groups, run = sizes.ny, sizes.groups, sizes.run
     plane = pltpu.make_async_copy(
         tx_hbm.at[pl.ds((sizes.planes - 1) * ny, ny)], send_ref.at[pl.ds(0, ny)], sems.at[0]
     )
     get_well = pltpu.make_async_copy(well_hbm, well_ref, sems.at[1])
     get_index = pltpu.make_async_copy(index_hbm, index_ref, sems.at[2])
-    for copy in (get_well, get_index, plane):
+    get_rhs = pltpu.make_async_copy(rhs_hbm, rhs_ref, sems.at[3])
+    get_slot = pltpu.make_async_copy(slot_hbm, slot_ref, sems.at[4])
+    for copy in (get_well, get_index, plane, get_rhs, get_slot):
         copy.start()
     place = lax.axis_index("gx")
     shape = (groups, LANES)
@@ -88,6 +92,11 @@
     wells_ref[0:groups, :] = before
     wells_ref[groups : 2 * groups, :] = total
     send_ref[ny : ny + SUB, :] = well_block(total * (1.0 - before), total * before, groups)
+    get_rhs.wait()
+    get_slot.wait()
+    behind = jnp.maximum(place - 1, 0)
+    for i, (ref, whose) in enumerate(((rhs_ref, place), (rhs_ref, behind), (slot_ref, place), (slot_ref, behind))):
+        wells_ref[(i + 2) * groups : (i + 3) * groups, :] = own_lanes(ref, whose, groups)
     plane.wait()
 
 
@@ -360,8 +369,6 @@
     from_o,
     from_e,
     wells_ref,
-    rhs_hbm,
-    slot_hbm,
     tx_ref,
     rp_ref,
     ip_ref,
@@ -382,20 +389,11 @@
     sums_out,
     send_o,
     rows_ref,
-    rhs_ref,
-    slot_ref,
-    sems,
 ):
     ny, planes, groups = sizes.ny, sizes.planes, sizes.groups
     place = lax.axis_index("gx")
     even = place % 2 == 0
     x_o, _ = facing(sizes, even)
-    fetches = [
-        pltpu.make_async_copy(rhs_hbm, rhs_ref, sems.at[0]),
-        pltpu.make_async_copy(slot_hbm, slot_ref, sems.at[1]),
-    ]
-    for fetch in fetches:
-        fetch.start()
 
     @pl.loop(0, ny // SUB)
     def _(r):
@@ -444,10 +442,9 @@
     is_before = before > 0.5
     sum_own = mine * (1.0 - before) + column_of(high[1:2, :], groups)
     sum_before = mine * before + column_of(low[0:1, :], groups)
-    for fetch in fetches:
-        fetch.wait()
-    rhs_own = own_lanes(rhs_ref, place, groups)
-    rhs_before = own_lanes(rhs_ref, jnp.maximum(place - 1, 0), groups)
+    rhs_own, rhs_before, slot_own, slot_before = [
+        wells_ref[i * groups : (i + 1) * groups, :] for i in range(2, 6)
+    ]
     inv_own = 1.0 / (1.5 * sum_own + 0.5)
     inv_before = 1.0 / (1.5 * sum_before + 0.5)
     rhs = jnp.where(is_before, rhs_before, rhs_own)
@@ -459,8 +456,8 @@
         SUM_OWN: sum_own,
         RHS: rhs,
         INV: inv,
-        SLOT_OWN: own_lanes(slot_ref, place, groups),
-        SLOT_BEFORE: own_lanes(slot_ref, jnp.maximum(place - 1, 0), groups),
+        SLOT_OWN: slot_own,
+        SLOT_BEFORE: slot_before,
     }
     for i, entry in entries.items():
         table_ref[i * groups : (i + 1) * groups, :] = entry
@@ -803,10 +800,16 @@
     index = lines(perf_index)
     send, wells = call(
         functools.partial(first_kernel, sizes),
-        [flat(trans_x), lines(perf_well), index],
-        [HBM, HBM, HBM],
-        [vmem(ny + SUB), vmem(2 * groups)],
-        [VMEM(index.shape, jnp.int32), VMEM(index.shape, F32), DMA((3,))],
+        [flat(trans_x), lines(perf_well), index, lines(well_rhs), lines(well_slot)],
+        [HBM] * 5,
+        [vmem(ny + SUB), vmem(6 * groups)],
+        [
+            VMEM(index.shape, jnp.int32),
+            VMEM(index.shape, F32),
+            VMEM(lines(well_rhs).shape, F32),
+            VMEM(lines(well_slot).shape, jnp.int32),
+            DMA((5,)),
+        ],
         "first",
         1,
     )
@@ -840,18 +843,11 @@
     slabs = vmem(groups * SUB)
     edge, plane_e, plane_o, wp, ws, shared, table, mu, sums, send_o = call(
         functools.partial(start_kernel, sizes),
-        [y, from_o, from_e, wells, lines(well_rhs), lines(well_slot), coefficients[0]]
-        + coefficients[5:]
-        + [extra, weight],
-        [SMEM] + [VMEM] * 3 + [HBM] * 2 + [VMEM] * 9,
+        [y, from_o, from_e, wells, coefficients[0]] + coefficients[5:] + [extra, weight],
+        [SMEM] + [VMEM] * 12,
         [vmem(6 * ny), vmem(4 * ny), vmem(4 * ny), slabs, slabs, vmem(groups), vmem(TABLE * groups)]
         + [vmem(groups), vmem(groups), block],
-        [
-            group_row,
-            VMEM(lines(well_rhs).shape, F32),
-            VMEM(lines(well_slot).shape, jnp.int32),
-            DMA((2,)),
-        ],
+        [group_row],
         "start",
         2,
     )

time: 64.4 us -> 64.2 us (level)
  no operation moved by 1% of the time
where the time goes in v8:
time: 64.2 us; the launch traced here: 63.9 us
  starting transfers between devices  29.8 us (46%)
  Pallas kernels  23.3 us (36%)
  waiting for transfers between devices  9.51 us (15%)
  between operations  0.77 us (1%)
    pallas_call x19, Pallas kernels, call(): pl.pallas_call(kernel, in_specs=[spec(space) for space in spaces], out_sp...  23.3 us
    ppermute x6, starting transfers between devices, to_core(): return lax.ppermute(block, 'gx', pairs_e)  19.5 us
    all_to_all x1, starting transfers between devices, body(): grads = lax.all_to_all(sums, 'gx', 0, 0)  6.23 us
    all_to_all x1, waiting for transfers between devices, body(): grads = lax.all_to_all(sums, 'gx', 0, 0)  4.9 us
    ppermute x6, waiting for transfers between devices, to_core(): return lax.ppermute(block, 'gx', pairs_e)  4.6 us
    ppermute x6, starting transfers between devices, to_chip(): return lax.ppermute(block, 'gx', pairs_o)  4 us
  transfers between devices with their start and end apart: 13, of which 6 were waited for; matrix products, arithmetic and copies ran while one was open for 0% of the time, Pallas kernels for 30%

profile of v8, /device:TPU:0, one launch (start us, length us, event | category | flops | bytes accessed | tf_op | source)
XLA Modules:
  0.0 63.9 jit_solution(8317084318524653718)
XLA Ops:
  0.6 0.9 %first.1 = (f32[136,128]{1,0:T(8,128)S(1)}, f32[192,128]{1,0:T(8,128)S(1)}) custom-call(f32[1024,128]{1,0:T(8,128)} %bitcast.8, s32[2,128]{1,0:T(2,128)} %bitcast.12, f32[2,128]{1,0:T(2,128)} %bitcast.9, f32[4,128]{1,0:T(4,128)} %bitcast.10, s32[4,128]{1,0:T(4,128)} %bitcast.11), custom_call_target="tpu_custom_call" | custom-call | flops 4000000 | bytes 3000000 | tf_op jit(solution)/shard_map/first/pallas_call | solution.py:771
  1.6 0.7 %collective-permute-start = (f32[136,128]{1,0:T(8,128)S(1)}, f32[136,128]{1,0:T(8,128)S(1)}, u32[]{:S(2)}, u32[]{:S(2)}) collective-permute-start(f32[136,128]{1,0:T(8,128)S(1)} %get-tuple-element.83), channel_id=1, source_target_pairs={{1,2},{2,1},{3,4},{4,3},{5,6},{6,5},{7,8},{8,7},{9,10},{10,9},{11,... | collective-permute-start | bytes 208904 | tf_op jit(solution)/shard_map/ppermute | solution.py:798
  2.2 4.4 %collective-permute-start.1 = (f32[136,128]{1,0:T(8,128)S(1)}, f32[136,128]{1,0:T(8,128)S(1)}, u32[]{:S(2)}, u32[]{:S(2)}) collective-permute-start(f32[136,128]{1,0:T(8,128)S(1)} %get-tuple-element.83), channel_id=1, source_target_pairs={{0,1},{1,0},{2,3},{3,2},{4,5},{5,4},{6,7},{7,6},{8,9},{9,8},{10,11... | collective-permute-start | bytes 208904 | tf_op jit(solution)/shard_map/ppermute | solution.py:795
  6.6 3.4 %setup.1 = (f32[1024,128]{1,0:T(8,128)S(1)}, f32[1024,128]{1,0:T(8,128)S(1)}, f32[1024,128]{1,0:T(8,128)S(1)}, f32[1024,128]{1,0:T(8,128)S(1)}, f32[1024,128]{1,...) custom-call(s32[256]{0:T(256)} %cell_hbm.1, ...), custom_call_target="tpu_custom_call" | custom-call | flops 16000000 | bytes 12000000 | tf_op jit(solution)/shard_map/setup/pallas_call | solution.py:771
  10.0 0.0 collective-permute-done.from_o
  10.0 0.0 collective-permute-done.1.from_e
  10.0 1.2 %start.1 = (f32[768,128]{1,0:T(8,128)S(1)}, f32[512,128]{1,0:T(8,128)S(1)}, f32[512,128]{1,0:T(8,128)S(1)}, f32[256,128]{1,0:T(8,128)S(1)}, f32[256,128]{1,0:T(8...) custom-call(s32[32]{0:T(128)S(4)} %get-tuple-element.82.cell_ref.ref, ...), custom_call_target="tpu_custom_call" | custom-call | flops 8000000 | bytes 6000000 | tf_op jit(solution)/shard_map/start/pallas_call | solution.py:771
  11.2 0.7 %collective-permute-start.2 = (f32[264,128]{1,0:T(8,128)S(1)}, f32[264,128]{1,0:T(8,128)S(1)}, u32[]{:S(2)}, u32[]{:S(2)}) collective-permute-start(f32[264,128]{1,0:T(8,128)S(1)} %get-tuple-element.94.refs_5_), channel_id=1, source_target_pairs={{1,2},{2,1},{3,4},{4,3},{5,6},{6,5},{7,8},{8,7},{9,10},{10,9},{11,... | collective-permute-start | bytes 405512 | tf_op jit(solution)/shard_map/ppermute | solution.py:798
  11.9 3.9 %inner.5 = (f32[1040,128]{1,0:T(8,128)}, f32[1040,128]{1,0:T(8,128)}, f32[1040,128]{1,0:T(8,128)S(1)}, f32[1040,128]{1,0:T(8,128)S(1)}, f32[32,128]{1,0:T(8,128)...) custom-call(s32[32]{0:T(128)S(4)} %get-tuple-element.82.cell_ref.refs_0_, ...), custom_call_target="tpu_custom_call" | custom-call | flops 8000000 | bytes 6000000 | tf_op jit(solution)/shard_map/inner/pallas_call | solution.py:771
  15.8 2.9 %collective-permute-start.3 = (f32[264,128]{1,0:T(8,128)S(1)}, f32[264,128]{1,0:T(8,128)S(1)}, u32[]{:S(2)}, u32[]{:S(2)}) collective-permute-start(f32[264,128]{1,0:T(8,128)S(1)} %get-tuple-element.111), channel_id=1, source_target_pairs={{0,1},{1,0},{2,3},{3,2},{4,5},{5,4},{6,7},{7,6},{8,9},{9,8},{10,11... | collective-permute-start | bytes 405512 | tf_op jit(solution)/shard_map/ppermute | solution.py:795
  18.7 0.0 collective-permute-done.2.from_o.refs_2_
  18.7 0.1 facing.5
  18.7 0.9 %collective-permute-done.3.refs_3_.refs_21_ = f32[264,128]{1,0:T(8,128)S(1)} collective-permute-done((f32[264,128]{1,0:T(8,128)S(1)}, f32[264,128]{1,0:T(8,128)S(1)}, u32[]{:S(2)}, u32[]{:S(2)}) %collective-permute-start.3) | collective-permute-done | bytes 135200 | tf_op jit(solution)/shard_map/ppermute | solution.py:795
  19.6 0.3 outer.5
  19.9 0.7 %collective-permute-start.4 = (f32[264,128]{1,0:T(8,128)S(1)}, f32[264,128]{1,0:T(8,128)S(1)}, u32[]{:S(2)}, u32[]{:S(2)}) collective-permute-start(f32[264,128]{1,0:T(8,128)S(1)} %get-tuple-element.116.refs_5_), channel_id=1, source_target_pairs={{1,2},{2,1},{3,4},{4,3},{5,6},{6,5},{7,8},{8,7},{9,10},{10,9},{11,... | collective-permute-start | bytes 405512 | tf_op jit(solution)/shard_map/ppermute | solution.py:798
  20.6 2.6 %inner.6 = (f32[1040,128]{1,0:T(8,128)S(1)}, f32[1040,128]{1,0:T(8,128)S(1)}, f32[1040,128]{1,0:T(8,128)S(1)}, f32[1040,128]{1,0:T(8,128)S(1)}, f32[32,128]{1,0:...) custom-call(s32[32]{0:T(128)S(4)} %get-tuple-element.82.cell_ref.refs, ...), custom_call_target="tpu_custom_call", output_to_operand_aliasing={{0}: (22, {}), {1}: (23, {})} | custom-call | flops 8000000 | bytes 6000000 | tf_op jit(solution)/shard_map/inner/pallas_call | solution.py:771
  23.2 2.9 %collective-permute-start.5 = (f32[264,128]{1,0:T(8,128)S(1)}, f32[264,128]{1,0:T(8,128)S(1)}, u32[]{:S(2)}, u32[]{:S(2)}) collective-permute-start(f32[264,128]{1,0:T(8,128)S(1)} %get-tuple-element.122), channel_id=1, source_target_pairs={{0,1},{1,0},{2,3},{3,2},{4,5},{5,4},{6,7},{7,6},{8,9},{9,8},{10,11... | collective-permute-start | bytes 405512 | tf_op jit(solution)/shard_map/ppermute | solution.py:795
  26.1 0.0 collective-permute-done.4.from_o.refs_2_
  26.1 0.1 facing.6
  26.2 0.9 %collective-permute-done.5.refs_3_.refs_21_ = f32[264,128]{1,0:T(8,128)S(1)} collective-permute-done((f32[264,128]{1,0:T(8,128)S(1)}, f32[264,128]{1,0:T(8,128)S(1)}, u32[]{:S(2)}, u32[]{:S(2)}) %collective-permute-start.5) | collective-permute-done | bytes 135200 | tf_op jit(solution)/shard_map/ppermute | solution.py:795
  27.1 0.3 outer.6
  27.4 0.7 %collective-permute-start.6 = (f32[264,128]{1,0:T(8,128)S(1)}, f32[264,128]{1,0:T(8,128)S(1)}, u32[]{:S(2)}, u32[]{:S(2)}) collective-permute-start(f32[264,128]{1,0:T(8,128)S(1)} %get-tuple-element.126.refs_5_), channel_id=1, source_target_pairs={{1,2},{2,1},{3,4},{4,3},{5,6},{6,5},{7,8},{8,7},{9,10},{10,9},{11,... | collective-permute-start | bytes 405512 | tf_op jit(solution)/shard_map/ppermute | solution.py:798
  28.0 2.5 %inner.7 = (f32[1040,128]{1,0:T(8,128)S(1)}, f32[1040,128]{1,0:T(8,128)S(1)}, f32[1040,128]{1,0:T(8,128)S(1)}, f32[1040,128]{1,0:T(8,128)S(1)}, f32[32,128]{1,0:...) custom-call(s32[32]{0:T(128)S(4)} %get-tuple-element.82.cell_ref.refs, ...), custom_call_target="tpu_custom_call", output_to_operand_aliasing={{0}: (22, {}), {1}: (23, {})} | custom-call | flops 8000000 | bytes 6000000 | tf_op jit(solution)/shard_map/inner/pallas_call | solution.py:771
  30.6 2.9 %collective-permute-start.7 = (f32[264,128]{1,0:T(8,128)S(1)}, f32[264,128]{1,0:T(8,128)S(1)}, u32[]{:S(2)}, u32[]{:S(2)}) collective-permute-start(f32[264,128]{1,0:T(8,128)S(1)} %get-tuple-element.132), channel_id=1, source_target_pairs={{0,1},{1,0},{2,3},{3,2},{4,5},{5,4},{6,7},{7,6},{8,9},{9,8},{10,11... | collective-permute-start | bytes 405512 | tf_op jit(solution)/shard_map/ppermute | solution.py:795
  33.5 0.0 collective-permute-done.6.from_o.refs_2_
  33.5 0.1 facing.7
  33.6 0.9 %collective-permute-done.7.refs_3_.refs_21_ = f32[264,128]{1,0:T(8,128)S(1)} collective-permute-done((f32[264,128]{1,0:T(8,128)S(1)}, f32[264,128]{1,0:T(8,128)S(1)}, u32[]{:S(2)}, u32[]{:S(2)}) %collective-permute-start.7) | collective-permute-done | bytes 135200 | tf_op jit(solution)/shard_map/ppermute | solution.py:795
  34.5 0.3 outer.7
  34.8 0.7 %collective-permute-start.8 = (f32[264,128]{1,0:T(8,128)S(1)}, f32[264,128]{1,0:T(8,128)S(1)}, u32[]{:S(2)}, u32[]{:S(2)}) collective-permute-start(f32[264,128]{1,0:T(8,128)S(1)} %get-tuple-element.136.refs_5_), channel_id=1, source_target_pairs={{1,2},{2,1},{3,4},{4,3},{5,6},{6,5},{7,8},{8,7},{9,10},{10,9},{11,... | collective-permute-start | bytes 405512 | tf_op jit(solution)/shard_map/ppermute | solution.py:798
  35.4 2.5 %inner.8 = (f32[1040,128]{1,0:T(8,128)S(1)}, f32[1040,128]{1,0:T(8,128)S(1)}, f32[1040,128]{1,0:T(8,128)S(1)}, f32[1040,128]{1,0:T(8,128)S(1)}, f32[32,128]{1,0:...) custom-call(s32[32]{0:T(128)S(4)} %get-tuple-element.82.cell_ref.refs, ...), custom_call_target="tpu_custom_call", output_to_operand_aliasing={{0}: (22, {}), {1}: (23, {})} | custom-call | flops 8000000 | bytes 6000000 | tf_op jit(solution)/shard_map/inner/pallas_call | solution.py:771
  38.0 3.2 %collective-permute-start.9 = (f32[264,128]{1,0:T(8,128)S(1)}, f32[264,128]{1,0:T(8,128)S(1)}, u32[]{:S(2)}, u32[]{:S(2)}) collective-permute-start(f32[264,128]{1,0:T(8,128)S(1)} %get-tuple-element.142), channel_id=1, source_target_pairs={{0,1},{1,0},{2,3},{3,2},{4,5},{5,4},{6,7},{7,6},{8,9},{9,8},{10,11... | collective-permute-start | bytes 405512 | tf_op jit(solution)/shard_map/ppermute | solution.py:795
  41.1 0.0 collective-permute-done.8.from_o.refs_2_
  41.1 0.1 facing.8
  41.2 0.9 %collective-permute-done.9.refs_3_.refs_21_ = f32[264,128]{1,0:T(8,128)S(1)} collective-permute-done((f32[264,128]{1,0:T(8,128)S(1)}, f32[264,128]{1,0:T(8,128)S(1)}, u32[]{:S(2)}, u32[]{:S(2)}) %collective-permute-start.9) | collective-permute-done | bytes 135200 | tf_op jit(solution)/shard_map/ppermute | solution.py:795
  42.1 0.3 outer.8
  42.4 0.7 %collective-permute-start.10 = (f32[264,128]{1,0:T(8,128)S(1)}, f32[264,128]{1,0:T(8,128)S(1)}, u32[]{:S(2)}, u32[]{:S(2)}) collective-permute-start(f32[264,128]{1,0:T(8,128)S(1)} %get-tuple-element.147.refs_5_), channel_id=1, source_target_pairs={{1,2},{2,1},{3,4},{4,3},{5,6},{6,5},{7,8},{8,7},{9,10},{10,9},{11,... | collective-permute-start | bytes 405512 | tf_op jit(solution)/shard_map/ppermute | solution.py:798
  43.1 2.5 %inner.9 = (f32[1040,128]{1,0:T(8,128)S(1)}, f32[1040,128]{1,0:T(8,128)S(1)}, f32[1040,128]{1,0:T(8,128)S(1)}, f32[1040,128]{1,0:T(8,128)S(1)}, f32[32,128]{1,0:...) custom-call(s32[32]{0:T(128)S(4)} %get-tuple-element.82.cell_ref.refs, ...), custom_call_target="tpu_custom_call", output_to_operand_aliasing={{0}: (22, {}), {1}: (23, {})} | custom-call | flops 8000000 | bytes 6000000 | tf_op jit(solution)/shard_map/inner/pallas_call | solution.py:771
  45.6 3.2 %collective-permute-start.11 = (f32[264,128]{1,0:T(8,128)S(1)}, f32[264,128]{1,0:T(8,128)S(1)}, u32[]{:S(2)}, u32[]{:S(2)}) collective-permute-start(f32[264,128]{1,0:T(8,128)S(1)} %get-tuple-element.152), channel_id=1, source_target_pairs={{0,1},{1,0},{2,3},{3,2},{4,5},{5,4},{6,7},{7,6},{8,9},{9,8},{10,11... | collective-permute-start | bytes 405512 | tf_op jit(solution)/shard_map/ppermute | solution.py:795
  48.8 0.0 collective-permute-done.10.from_o.refs_2_
  48.8 0.1 facing.9
  48.9 0.9 %collective-permute-done.11.refs_3_.from_e = f32[264,128]{1,0:T(8,128)S(1)} collective-permute-done((f32[264,128]{1,0:T(8,128)S(1)}, f32[264,128]{1,0:T(8,128)S(1)}, u32[]{:S(2)}, u32[]{:S(2)}) %collective-permute-start.11) | collective-permute-done | bytes 135200 | tf_op jit(solution)/shard_map/ppermute | solution.py:795
  49.8 0.9 %outer.9 = (f32[264,128]{1,0:T(8,128)S(1)}, f32[32,128]{1,0:T(8,128)S(1)}, f32[16,1,128]{2,1,0:T(1,128)}) custom-call(s32[32]{0:T(128)S(4)} %get-tuple-element.82.cell_ref.refs_0_, f32[264,128]{1,0:T(8,128)S(1)} %get-tuple-element.151.refs_1_, f32[264,128]{1,0:T(8,128)S(1)} %collective-permute-done.10.from_o.refs_2_, ...), custom_call_target="tpu_custom_call", output_to_operand_aliasing={{0}: (1, {})} | custom-call | flops 4000000 | bytes 3000000 | tf_op jit(solution)/shard_map/outer/pallas_call | solution.py:771
  50.7 6.2 %all-to-all-start = ((f32[16,1,128]{2,1,0:T(1,128)}), f32[16,1,128]{2,1,0:T(1,128)S(1)}, u32[]{:S(2)}, u32[]{:S(2)}) async-start(f32[16,1,128]{2,1,0:T(1,128)} %get-tuple-element.160), calls=%async_computation | async-start | bytes 16384 | tf_op jit(solution)/shard_map/all_to_all | solution.py:886
  56.9 1.5 %final.1 = (f32[1040,128]{1,0:T(8,128)S(1)}, f32[1040,128]{1,0:T(8,128)S(1)}, f32[1024,128]{1,0:T(8,128)}, f32[1024,128]{1,0:T(8,128)}) custom-call(s32[32]{0:T(128)S(4)} %get-tuple-element.82.cell_ref.refs_0_, f32[1040,128]{1,0:T(8,128)S(1)} %get-tuple-element.149.p_ref.p_in, ...), custom_call_target="tpu_custom_call", output_to_operand_aliasing={{0}: (1, {}), {1}: (2, {})} | custom-call | flops 8000000 | bytes 6000000 | tf_op jit(solution)/shard_map/final/pallas_call | solution.py:771
  58.4 4.9 %all-to-all-done = f32[16,1,128]{2,1,0:T(1,128)S(1)} async-done(((f32[16,1,128]{2,1,0:T(1,128)}), f32[16,1,128]{2,1,0:T(1,128)S(1)}, u32[]{:S(2)}, u32[]{:S(2)}) %all-to-all-start) | async-done | bytes 8224 | tf_op jit(solution)/shard_map/all_to_all | solution.py:886
  63.3 0.5 reduce_sum.9
Async XLA Ops:
  1.6 8.5 %collective-permute-start = (f32[136,128]{1,0:T(8,128)S(1)}, f32[136,128]{1,0:T(8,128)S(1)}, u32[]{:S(2)}, u32[]{:S(2)}) collective-permute-start(f32[136,128]{1,0:T(8,128)S(1)} %get-tuple-element.83), channel_id=1, source_target_pairs={{1,2},{2,1},{3,4},{4,3},{5,6},{6,5},{7,8},{8,7},{9,10},{10,9},{11,... | collective-permute-start | bytes 208904 | tf_op jit(solution)/shard_map/ppermute | solution.py:798
  2.2 7.8 %collective-permute-start.1 = (f32[136,128]{1,0:T(8,128)S(1)}, f32[136,128]{1,0:T(8,128)S(1)}, u32[]{:S(2)}, u32[]{:S(2)}) collective-permute-start(f32[136,128]{1,0:T(8,128)S(1)} %get-tuple-element.83), channel_id=1, source_target_pairs={{0,1},{1,0},{2,3},{3,2},{4,5},{5,4},{6,7},{7,6},{8,9},{9,8},{10,11... | collective-permute-start | bytes 208904 | tf_op jit(solution)/shard_map/ppermute | solution.py:795
  11.2 7.4 %collective-permute-start.2 = (f32[264,128]{1,0:T(8,128)S(1)}, f32[264,128]{1,0:T(8,128)S(1)}, u32[]{:S(2)}, u32[]{:S(2)}) collective-permute-start(f32[264,128]{1,0:T(8,128)S(1)} %get-tuple-element.94.refs_5_), channel_id=1, source_target_pairs={{1,2},{2,1},{3,4},{4,3},{5,6},{6,5},{7,8},{8,7},{9,10},{10,9},{11,... | collective-permute-start | bytes 405512 | tf_op jit(solution)/shard_map/ppermute | solution.py:798
  15.8 3.9 %collective-permute-start.3 = (f32[264,128]{1,0:T(8,128)S(1)}, f32[264,128]{1,0:T(8,128)S(1)}, u32[]{:S(2)}, u32[]{:S(2)}) collective-permute-start(f32[264,128]{1,0:T(8,128)S(1)} %get-tuple-element.111), channel_id=1, source_target_pairs={{0,1},{1,0},{2,3},{3,2},{4,5},{5,4},{6,7},{7,6},{8,9},{9,8},{10,11... | collective-permute-start | bytes 405512 | tf_op jit(solution)/shard_map/ppermute | solution.py:795
  19.9 6.2 %collective-permute-start.4 = (f32[264,128]{1,0:T(8,128)S(1)}, f32[264,128]{1,0:T(8,128)S(1)}, u32[]{:S(2)}, u32[]{:S(2)}) collective-permute-start(f32[264,128]{1,0:T(8,128)S(1)} %get-tuple-element.116.refs_5_), channel_id=1, source_target_pairs={{1,2},{2,1},{3,4},{4,3},{5,6},{6,5},{7,8},{8,7},{9,10},{10,9},{11,... | collective-permute-start | bytes 405512 | tf_op jit(solution)/shard_map/ppermute | solution.py:798
  23.2 3.9 %collective-permute-start.5 = (f32[264,128]{1,0:T(8,128)S(1)}, f32[264,128]{1,0:T(8,128)S(1)}, u32[]{:S(2)}, u32[]{:S(2)}) collective-permute-start(f32[264,128]{1,0:T(8,128)S(1)} %get-tuple-element.122), channel_id=1, source_target_pairs={{0,1},{1,0},{2,3},{3,2},{4,5},{5,4},{6,7},{7,6},{8,9},{9,8},{10,11... | collective-permute-start | bytes 405512 | tf_op jit(solution)/shard_map/ppermute | solution.py:795
  27.4 6.1 %collective-permute-start.6 = (f32[264,128]{1,0:T(8,128)S(1)}, f32[264,128]{1,0:T(8,128)S(1)}, u32[]{:S(2)}, u32[]{:S(2)}) collective-permute-start(f32[264,128]{1,0:T(8,128)S(1)} %get-tuple-element.126.refs_5_), channel_id=1, source_target_pairs={{1,2},{2,1},{3,4},{4,3},{5,6},{6,5},{7,8},{8,7},{9,10},{10,9},{11,... | collective-permute-start | bytes 405512 | tf_op jit(solution)/shard_map/ppermute | solution.py:798
  30.6 3.9 %collective-permute-start.7 = (f32[264,128]{1,0:T(8,128)S(1)}, f32[264,128]{1,0:T(8,128)S(1)}, u32[]{:S(2)}, u32[]{:S(2)}) collective-permute-start(f32[264,128]{1,0:T(8,128)S(1)} %get-tuple-element.132), channel_id=1, source_target_pairs={{0,1},{1,0},{2,3},{3,2},{4,5},{5,4},{6,7},{7,6},{8,9},{9,8},{10,11... | collective-permute-start | bytes 405512 | tf_op jit(solution)/shard_map/ppermute | solution.py:795
  34.8 6.4 %collective-permute-start.8 = (f32[264,128]{1,0:T(8,128)S(1)}, f32[264,128]{1,0:T(8,128)S(1)}, u32[]{:S(2)}, u32[]{:S(2)}) collective-permute-start(f32[264,128]{1,0:T(8,128)S(1)} %get-tuple-element.136.refs_5_), channel_id=1, source_target_pairs={{1,2},{2,1},{3,4},{4,3},{5,6},{6,5},{7,8},{8,7},{9,10},{10,9},{11,... | collective-permute-start | bytes 405512 | tf_op jit(solution)/shard_map/ppermute | solution.py:798
  38.0 4.2 %collective-permute-start.9 = (f32[264,128]{1,0:T(8,128)S(1)}, f32[264,128]{1,0:T(8,128)S(1)}, u32[]{:S(2)}, u32[]{:S(2)}) collective-permute-start(f32[264,128]{1,0:T(8,128)S(1)} %get-tuple-element.142), channel_id=1, source_target_pairs={{0,1},{1,0},{2,3},{3,2},{4,5},{5,4},{6,7},{7,6},{8,9},{9,8},{10,11... | collective-permute-start | bytes 405512 | tf_op jit(solution)/shard_map/ppermute | solution.py:795
  42.4 6.4 %collective-permute-start.10 = (f32[264,128]{1,0:T(8,128)S(1)}, f32[264,128]{1,0:T(8,128)S(1)}, u32[]{:S(2)}, u32[]{:S(2)}) collective-permute-start(f32[264,128]{1,0:T(8,128)S(1)} %get-tuple-element.147.refs_5_), channel_id=1, source_target_pairs={{1,2},{2,1},{3,4},{4,3},{5,6},{6,5},{7,8},{8,7},{9,10},{10,9},{11,... | collective-permute-start | bytes 405512 | tf_op jit(solution)/shard_map/ppermute | solution.py:798
  45.6 4.2 %collective-permute-start.11 = (f32[264,128]{1,0:T(8,128)S(1)}, f32[264,128]{1,0:T(8,128)S(1)}, u32[]{:S(2)}, u32[]{:S(2)}) collective-permute-start(f32[264,128]{1,0:T(8,128)S(1)} %get-tuple-element.152), channel_id=1, source_target_pairs={{0,1},{1,0},{2,3},{3,2},{4,5},{5,4},{6,7},{7,6},{8,9},{9,8},{10,11... | collective-permute-start | bytes 405512 | tf_op jit(solution)/shard_map/ppermute | solution.py:795
  50.7 12.6 %all-to-all-start = ((f32[16,1,128]{2,1,0:T(1,128)}), f32[16,1,128]{2,1,0:T(1,128)S(1)}, u32[]{:S(2)}, u32[]{:S(2)}) async-start(f32[16,1,128]{2,1,0:T(1,128)} %get-tuple-element.160), calls=%async_computation | async-start | bytes 16384 | tf_op jit(solution)/shard_map/all_to_all | solution.py:886

commit v9 on v8

--- a/solution.py
+++ b/solution.py
@@ -11,7 +11,7 @@
 SUB = 8
 LANES = 128
 F32 = jnp.float32
-CHUNKS = 4
+CHUNKS = 2
 
 
 def vmem(rows):

time: 64.2 us -> 64.3 us (level)
  no operation moved by 1% of the time
where the time goes in v9:
time: 64.3 us; the launch traced here: 63.9 us
  starting transfers between devices  29.7 us (46%)
  Pallas kernels  23.4 us (36%)
  waiting for transfers between devices  9.5 us (15%)
  between operations  0.76 us (1%)
    pallas_call x19, Pallas kernels, call(): pl.pallas_call(kernel, in_specs=[spec(space) for space in spaces], out_sp...  23.4 us
    ppermute x6, starting transfers between devices, to_core(): return lax.ppermute(block, 'gx', pairs_e)  19.5 us
    all_to_all x1, starting transfers between devices, body(): grads = lax.all_to_all(sums, 'gx', 0, 0)  6.24 us
    all_to_all x1, waiting for transfers between devices, body(): grads = lax.all_to_all(sums, 'gx', 0, 0)  4.89 us
    ppermute x6, waiting for transfers between devices, to_core(): return lax.ppermute(block, 'gx', pairs_e)  4.6 us
    ppermute x6, starting transfers between devices, to_chip(): return lax.ppermute(block, 'gx', pairs_o)  4 us
  transfers between devices with their start and end apart: 13, of which 6 were waited for; matrix products, arithmetic and copies ran while one was open for 0% of the time, Pallas kernels for 30%

profile of v9, /device:TPU:0, one launch (start us, length us, event | category | flops | bytes accessed | tf_op | source)
XLA Modules:
  0.0 63.9 jit_solution(17964983225398653521)
XLA Ops:
  0.6 0.9 %first.1 = (f32[136,128]{1,0:T(8,128)S(1)}, f32[192,128]{1,0:T(8,128)S(1)}) custom-call(f32[1024,128]{1,0:T(8,128)} %bitcast.8, s32[2,128]{1,0:T(2,128)} %bitcast.12, f32[2,128]{1,0:T(2,128)} %bitcast.9, f32[4,128]{1,0:T(4,128)} %bitcast.10, s32[4,128]{1,0:T(4,128)} %bitcast.11), custom_call_target="tpu_custom_call" | custom-call | flops 4000000 | bytes 3000000 | tf_op jit(solution)/shard_map/first/pallas_call | solution.py:771
  1.6 0.7 %collective-permute-start = (f32[136,128]{1,0:T(8,128)S(1)}, f32[136,128]{1,0:T(8,128)S(1)}, u32[]{:S(2)}, u32[]{:S(2)}) collective-permute-start(f32[136,128]{1,0:T(8,128)S(1)} %get-tuple-element.83), channel_id=1, source_target_pairs={{1,2},{2,1},{3,4},{4,3},{5,6},{6,5},{7,8},{8,7},{9,10},{10,9},{11,... | collective-permute-start | bytes 208904 | tf_op jit(solution)/shard_map/ppermute | solution.py:798
  2.2 4.4 %collective-permute-start.1 = (f32[136,128]{1,0:T(8,128)S(1)}, f32[136,128]{1,0:T(8,128)S(1)}, u32[]{:S(2)}, u32[]{:S(2)}) collective-permute-start(f32[136,128]{1,0:T(8,128)S(1)} %get-tuple-element.83), channel_id=1, source_target_pairs={{0,1},{1,0},{2,3},{3,2},{4,5},{5,4},{6,7},{7,6},{8,9},{9,8},{10,11... | collective-permute-start | bytes 208904 | tf_op jit(solution)/shard_map/ppermute | solution.py:795
  6.6 3.4 %setup.1 = (f32[1024,128]{1,0:T(8,128)S(1)}, f32[1024,128]{1,0:T(8,128)S(1)}, f32[1024,128]{1,0:T(8,128)S(1)}, f32[1024,128]{1,0:T(8,128)S(1)}, f32[1024,128]{1,...) custom-call(s32[256]{0:T(256)} %cell_hbm.1, ...), custom_call_target="tpu_custom_call" | custom-call | flops 16000000 | bytes 12000000 | tf_op jit(solution)/shard_map/setup/pallas_call | solution.py:771
  10.1 0.0 collective-permute-done.from_o
  10.1 0.0 collective-permute-done.1.from_e
  10.1 1.2 %start.1 = (f32[768,128]{1,0:T(8,128)S(1)}, f32[512,128]{1,0:T(8,128)S(1)}, f32[512,128]{1,0:T(8,128)S(1)}, f32[256,128]{1,0:T(8,128)S(1)}, f32[256,128]{1,0:T(8...) custom-call(s32[32]{0:T(128)S(4)} %get-tuple-element.82.cell_ref.ref, ...), custom_call_target="tpu_custom_call" | custom-call | flops 8000000 | bytes 6000000 | tf_op jit(solution)/shard_map/start/pallas_call | solution.py:771
  11.3 0.7 %collective-permute-start.2 = (f32[264,128]{1,0:T(8,128)S(1)}, f32[264,128]{1,0:T(8,128)S(1)}, u32[]{:S(2)}, u32[]{:S(2)}) collective-permute-start(f32[264,128]{1,0:T(8,128)S(1)} %get-tuple-element.94.refs_5_), channel_id=1, source_target_pairs={{1,2},{2,1},{3,4},{4,3},{5,6},{6,5},{7,8},{8,7},{9,10},{10,9},{11,... | collective-permute-start | bytes 405512 | tf_op jit(solution)/shard_map/ppermute | solution.py:798
  11.9 3.9 %inner.5 = (f32[1040,128]{1,0:T(8,128)}, f32[1040,128]{1,0:T(8,128)}, f32[1040,128]{1,0:T(8,128)S(1)}, f32[1040,128]{1,0:T(8,128)S(1)}, f32[32,128]{1,0:T(8,128)...) custom-call(s32[32]{0:T(128)S(4)} %get-tuple-element.82.cell_ref.refs_0_, ...), custom_call_target="tpu_custom_call" | custom-call | flops 8000000 | bytes 6000000 | tf_op jit(solution)/shard_map/inner/pallas_call | solution.py:771
  15.8 2.9 %collective-permute-start.3 = (f32[264,128]{1,0:T(8,128)S(1)}, f32[264,128]{1,0:T(8,128)S(1)}, u32[]{:S(2)}, u32[]{:S(2)}) collective-permute-start(f32[264,128]{1,0:T(8,128)S(1)} %get-tuple-element.111), channel_id=1, source_target_pairs={{0,1},{1,0},{2,3},{3,2},{4,5},{5,4},{6,7},{7,6},{8,9},{9,8},{10,11... | collective-permute-start | bytes 405512 | tf_op jit(solution)/shard_map/ppermute | solution.py:795
  18.7 0.0 collective-permute-done.2.from_o.refs_2_
  18.7 0.1 facing.5
  18.8 0.9 %collective-permute-done.3.refs_3_.refs_21_ = f32[264,128]{1,0:T(8,128)S(1)} collective-permute-done((f32[264,128]{1,0:T(8,128)S(1)}, f32[264,128]{1,0:T(8,128)S(1)}, u32[]{:S(2)}, u32[]{:S(2)}) %collective-permute-start.3) | collective-permute-done | bytes 135200 | tf_op jit(solution)/shard_map/ppermute | solution.py:795
  19.7 0.3 outer.5
  19.9 0.7 %collective-permute-start.4 = (f32[264,128]{1,0:T(8,128)S(1)}, f32[264,128]{1,0:T(8,128)S(1)}, u32[]{:S(2)}, u32[]{:S(2)}) collective-permute-start(f32[264,128]{1,0:T(8,128)S(1)} %get-tuple-element.116.refs_5_), channel_id=1, source_target_pairs={{1,2},{2,1},{3,4},{4,3},{5,6},{6,5},{7,8},{8,7},{9,10},{10,9},{11,... | collective-permute-start | bytes 405512 | tf_op jit(solution)/shard_map/ppermute | solution.py:798
  20.6 2.6 %inner.6 = (f32[1040,128]{1,0:T(8,128)S(1)}, f32[1040,128]{1,0:T(8,128)S(1)}, f32[1040,128]{1,0:T(8,128)S(1)}, f32[1040,128]{1,0:T(8,128)S(1)}, f32[32,128]{1,0:...) custom-call(s32[32]{0:T(128)S(4)} %get-tuple-element.82.cell_ref.refs, ...), custom_call_target="tpu_custom_call", output_to_operand_aliasing={{0}: (22, {}), {1}: (23, {})} | custom-call | flops 8000000 | bytes 6000000 | tf_op jit(solution)/shard_map/inner/pallas_call | solution.py:771
  23.2 2.9 %collective-permute-start.5 = (f32[264,128]{1,0:T(8,128)S(1)}, f32[264,128]{1,0:T(8,128)S(1)}, u32[]{:S(2)}, u32[]{:S(2)}) collective-permute-start(f32[264,128]{1,0:T(8,128)S(1)} %get-tuple-element.122), channel_id=1, source_target_pairs={{0,1},{1,0},{2,3},{3,2},{4,5},{5,4},{6,7},{7,6},{8,9},{9,8},{10,11... | collective-permute-start | bytes 405512 | tf_op jit(solution)/shard_map/ppermute | solution.py:795
  26.2 0.0 collective-permute-done.4.from_o.refs_2_
  26.2 0.1 facing.6
  26.2 0.9 %collective-permute-done.5.refs_3_.refs_21_ = f32[264,128]{1,0:T(8,128)S(1)} collective-permute-done((f32[264,128]{1,0:T(8,128)S(1)}, f32[264,128]{1,0:T(8,128)S(1)}, u32[]{:S(2)}, u32[]{:S(2)}) %collective-permute-start.5) | collective-permute-done | bytes 135200 | tf_op jit(solution)/shard_map/ppermute | solution.py:795
  27.2 0.3 outer.6
  27.4 0.7 %collective-permute-start.6 = (f32[264,128]{1,0:T(8,128)S(1)}, f32[264,128]{1,0:T(8,128)S(1)}, u32[]{:S(2)}, u32[]{:S(2)}) collective-permute-start(f32[264,128]{1,0:T(8,128)S(1)} %get-tuple-element.126.refs_5_), channel_id=1, source_target_pairs={{1,2},{2,1},{3,4},{4,3},{5,6},{6,5},{7,8},{8,7},{9,10},{10,9},{11,... | collective-permute-start | bytes 405512 | tf_op jit(solution)/shard_map/ppermute | solution.py:798
  28.1 2.5 %inner.7 = (f32[1040,128]{1,0:T(8,128)S(1)}, f32[1040,128]{1,0:T(8,128)S(1)}, f32[1040,128]{1,0:T(8,128)S(1)}, f32[1040,128]{1,0:T(8,128)S(1)}, f32[32,128]{1,0:...) custom-call(s32[32]{0:T(128)S(4)} %get-tuple-element.82.cell_ref.refs, ...), custom_call_target="tpu_custom_call", output_to_operand_aliasing={{0}: (22, {}), {1}: (23, {})} | custom-call | flops 8000000 | bytes 6000000 | tf_op jit(solution)/shard_map/inner/pallas_call | solution.py:771
  30.6 2.9 %collective-permute-start.7 = (f32[264,128]{1,0:T(8,128)S(1)}, f32[264,128]{1,0:T(8,128)S(1)}, u32[]{:S(2)}, u32[]{:S(2)}) collective-permute-start(f32[264,128]{1,0:T(8,128)S(1)} %get-tuple-element.132), channel_id=1, source_target_pairs={{0,1},{1,0},{2,3},{3,2},{4,5},{5,4},{6,7},{7,6},{8,9},{9,8},{10,11... | collective-permute-start | bytes 405512 | tf_op jit(solution)/shard_map/ppermute | solution.py:795
  33.6 0.0 collective-permute-done.6.from_o.refs_2_
  33.6 0.1 facing.7
  33.6 0.9 %collective-permute-done.7.refs_3_.refs_21_ = f32[264,128]{1,0:T(8,128)S(1)} collective-permute-done((f32[264,128]{1,0:T(8,128)S(1)}, f32[264,128]{1,0:T(8,128)S(1)}, u32[]{:S(2)}, u32[]{:S(2)}) %collective-permute-start.7) | collective-permute-done | bytes 135200 | tf_op jit(solution)/shard_map/ppermute | solution.py:795
  34.6 0.3 outer.7
  34.8 0.7 %collective-permute-start.8 = (f32[264,128]{1,0:T(8,128)S(1)}, f32[264,128]{1,0:T(8,128)S(1)}, u32[]{:S(2)}, u32[]{:S(2)}) collective-permute-start(f32[264,128]{1,0:T(8,128)S(1)} %get-tuple-element.136.refs_5_), channel_id=1, source_target_pairs={{1,2},{2,1},{3,4},{4,3},{5,6},{6,5},{7,8},{8,7},{9,10},{10,9},{11,... | collective-permute-start | bytes 405512 | tf_op jit(solution)/shard_map/ppermute | solution.py:798
  35.5 2.5 %inner.8 = (f32[1040,128]{1,0:T(8,128)S(1)}, f32[1040,128]{1,0:T(8,128)S(1)}, f32[1040,128]{1,0:T(8,128)S(1)}, f32[1040,128]{1,0:T(8,128)S(1)}, f32[32,128]{1,0:...) custom-call(s32[32]{0:T(128)S(4)} %get-tuple-element.82.cell_ref.refs, ...), custom_call_target="tpu_custom_call", output_to_operand_aliasing={{0}: (22, {}), {1}: (23, {})} | custom-call | flops 8000000 | bytes 6000000 | tf_op jit(solution)/shard_map/inner/pallas_call | solution.py:771
  38.0 3.2 %collective-permute-start.9 = (f32[264,128]{1,0:T(8,128)S(1)}, f32[264,128]{1,0:T(8,128)S(1)}, u32[]{:S(2)}, u32[]{:S(2)}) collective-permute-start(f32[264,128]{1,0:T(8,128)S(1)} %get-tuple-element.142), channel_id=1, source_target_pairs={{0,1},{1,0},{2,3},{3,2},{4,5},{5,4},{6,7},{7,6},{8,9},{9,8},{10,11... | collective-permute-start | bytes 405512 | tf_op jit(solution)/shard_map/ppermute | solution.py:795
  41.2 0.0 collective-permute-done.8.from_o.refs_2_
  41.2 0.1 facing.8
  41.2 0.9 %collective-permute-done.9.refs_3_.refs_21_ = f32[264,128]{1,0:T(8,128)S(1)} collective-permute-done((f32[264,128]{1,0:T(8,128)S(1)}, f32[264,128]{1,0:T(8,128)S(1)}, u32[]{:S(2)}, u32[]{:S(2)}) %collective-permute-start.9) | collective-permute-done | bytes 135200 | tf_op jit(solution)/shard_map/ppermute | solution.py:795
  42.2 0.3 outer.8
  42.4 0.7 %collective-permute-start.10 = (f32[264,128]{1,0:T(8,128)S(1)}, f32[264,128]{1,0:T(8,128)S(1)}, u32[]{:S(2)}, u32[]{:S(2)}) collective-permute-start(f32[264,128]{1,0:T(8,128)S(1)} %get-tuple-element.147.refs_5_), channel_id=1, source_target_pairs={{1,2},{2,1},{3,4},{4,3},{5,6},{6,5},{7,8},{8,7},{9,10},{10,9},{11,... | collective-permute-start | bytes 405512 | tf_op jit(solution)/shard_map/ppermute | solution.py:798
  43.1 2.5 %inner.9 = (f32[1040,128]{1,0:T(8,128)S(1)}, f32[1040,128]{1,0:T(8,128)S(1)}, f32[1040,128]{1,0:T(8,128)S(1)}, f32[1040,128]{1,0:T(8,128)S(1)}, f32[32,128]{1,0:...) custom-call(s32[32]{0:T(128)S(4)} %get-tuple-element.82.cell_ref.refs, ...), custom_call_target="tpu_custom_call", output_to_operand_aliasing={{0}: (22, {}), {1}: (23, {})} | custom-call | flops 8000000 | bytes 6000000 | tf_op jit(solution)/shard_map/inner/pallas_call | solution.py:771
  45.6 3.2 %collective-permute-start.11 = (f32[264,128]{1,0:T(8,128)S(1)}, f32[264,128]{1,0:T(8,128)S(1)}, u32[]{:S(2)}, u32[]{:S(2)}) collective-permute-start(f32[264,128]{1,0:T(8,128)S(1)} %get-tuple-element.152), channel_id=1, source_target_pairs={{0,1},{1,0},{2,3},{3,2},{4,5},{5,4},{6,7},{7,6},{8,9},{9,8},{10,11... | collective-permute-start | bytes 405512 | tf_op jit(solution)/shard_map/ppermute | solution.py:795
  48.9 0.0 collective-permute-done.10.from_o.refs_2_
  48.9 0.1 facing.9
  48.9 0.9 %collective-permute-done.11.refs_3_.from_e = f32[264,128]{1,0:T(8,128)S(1)} collective-permute-done((f32[264,128]{1,0:T(8,128)S(1)}, f32[264,128]{1,0:T(8,128)S(1)}, u32[]{:S(2)}, u32[]{:S(2)}) %collective-permute-start.11) | collective-permute-done | bytes 135200 | tf_op jit(solution)/shard_map/ppermute | solution.py:795
  49.8 0.9 %outer.9 = (f32[264,128]{1,0:T(8,128)S(1)}, f32[32,128]{1,0:T(8,128)S(1)}, f32[16,1,128]{2,1,0:T(1,128)}) custom-call(s32[32]{0:T(128)S(4)} %get-tuple-element.82.cell_ref.refs_0_, f32[264,128]{1,0:T(8,128)S(1)} %get-tuple-element.151.refs_1_, f32[264,128]{1,0:T(8,128)S(1)} %collective-permute-done.10.from_o.refs_2_, ...), custom_call_target="tpu_custom_call", output_to_operand_aliasing={{0}: (1, {})} | custom-call | flops 4000000 | bytes 3000000 | tf_op jit(solution)/shard_map/outer/pallas_call | solution.py:771
  50.7 6.2 %all-to-all-start = ((f32[16,1,128]{2,1,0:T(1,128)}), f32[16,1,128]{2,1,0:T(1,128)S(1)}, u32[]{:S(2)}, u32[]{:S(2)}) async-start(f32[16,1,128]{2,1,0:T(1,128)} %get-tuple-element.160), calls=%async_computation | async-start | bytes 16384 | tf_op jit(solution)/shard_map/all_to_all | solution.py:886
  56.9 1.5 %final.1 = (f32[1040,128]{1,0:T(8,128)S(1)}, f32[1040,128]{1,0:T(8,128)S(1)}, f32[1024,128]{1,0:T(8,128)}, f32[1024,128]{1,0:T(8,128)}) custom-call(s32[32]{0:T(128)S(4)} %get-tuple-element.82.cell_ref.refs_0_, f32[1040,128]{1,0:T(8,128)S(1)} %get-tuple-element.149.p_ref.p_in, ...), custom_call_target="tpu_custom_call", output_to_operand_aliasing={{0}: (1, {}), {1}: (2, {})} | custom-call | flops 8000000 | bytes 6000000 | tf_op jit(solution)/shard_map/final/pallas_call | solution.py:771
  58.5 4.9 %all-to-all-done = f32[16,1,128]{2,1,0:T(1,128)S(1)} async-done(((f32[16,1,128]{2,1,0:T(1,128)}), f32[16,1,128]{2,1,0:T(1,128)S(1)}, u32[]{:S(2)}, u32[]{:S(2)}) %all-to-all-start) | async-done | bytes 8224 | tf_op jit(solution)/shard_map/all_to_all | solution.py:886
  63.4 0.5 reduce_sum.9
Async XLA Ops:
  1.6 8.5 %collective-permute-start = (f32[136,128]{1,0:T(8,128)S(1)}, f32[136,128]{1,0:T(8,128)S(1)}, u32[]{:S(2)}, u32[]{:S(2)}) collective-permute-start(f32[136,128]{1,0:T(8,128)S(1)} %get-tuple-element.83), channel_id=1, source_target_pairs={{1,2},{2,1},{3,4},{4,3},{5,6},{6,5},{7,8},{8,7},{9,10},{10,9},{11,... | collective-permute-start | bytes 208904 | tf_op jit(solution)/shard_map/ppermute | solution.py:798
  2.2 7.8 %collective-permute-start.1 = (f32[136,128]{1,0:T(8,128)S(1)}, f32[136,128]{1,0:T(8,128)S(1)}, u32[]{:S(2)}, u32[]{:S(2)}) collective-permute-start(f32[136,128]{1,0:T(8,128)S(1)} %get-tuple-element.83), channel_id=1, source_target_pairs={{0,1},{1,0},{2,3},{3,2},{4,5},{5,4},{6,7},{7,6},{8,9},{9,8},{10,11... | collective-permute-start | bytes 208904 | tf_op jit(solution)/shard_map/ppermute | solution.py:795
  11.3 7.4 %collective-permute-start.2 = (f32[264,128]{1,0:T(8,128)S(1)}, f32[264,128]{1,0:T(8,128)S(1)}, u32[]{:S(2)}, u32[]{:S(2)}) collective-permute-start(f32[264,128]{1,0:T(8,128)S(1)} %get-tuple-element.94.refs_5_), channel_id=1, source_target_pairs={{1,2},{2,1},{3,4},{4,3},{5,6},{6,5},{7,8},{8,7},{9,10},{10,9},{11,... | collective-permute-start | bytes 405512 | tf_op jit(solution)/shard_map/ppermute | solution.py:798
  15.8 3.9 %collective-permute-start.3 = (f32[264,128]{1,0:T(8,128)S(1)}, f32[264,128]{1,0:T(8,128)S(1)}, u32[]{:S(2)}, u32[]{:S(2)}) collective-permute-start(f32[264,128]{1,0:T(8,128)S(1)} %get-tuple-element.111), channel_id=1, source_target_pairs={{0,1},{1,0},{2,3},{3,2},{4,5},{5,4},{6,7},{7,6},{8,9},{9,8},{10,11... | collective-permute-start | bytes 405512 | tf_op jit(solution)/shard_map/ppermute | solution.py:795
  19.9 6.2 %collective-permute-start.4 = (f32[264,128]{1,0:T(8,128)S(1)}, f32[264,128]{1,0:T(8,128)S(1)}, u32[]{:S(2)}, u32[]{:S(2)}) collective-permute-start(f32[264,128]{1,0:T(8,128)S(1)} %get-tuple-element.116.refs_5_), channel_id=1, source_target_pairs={{1,2},{2,1},{3,4},{4,3},{5,6},{6,5},{7,8},{8,7},{9,10},{10,9},{11,... | collective-permute-start | bytes 405512 | tf_op jit(solution)/shard_map/ppermute | solution.py:798
  23.2 3.9 %collective-permute-start.5 = (f32[264,128]{1,0:T(8,128)S(1)}, f32[264,128]{1,0:T(8,128)S(1)}, u32[]{:S(2)}, u32[]{:S(2)}) collective-permute-start(f32[264,128]{1,0:T(8,128)S(1)} %get-tuple-element.122), channel_id=1, source_target_pairs={{0,1},{1,0},{2,3},{3,2},{4,5},{5,4},{6,7},{7,6},{8,9},{9,8},{10,11... | collective-permute-start | bytes 405512 | tf_op jit(solution)/shard_map/ppermute | solution.py:795
  27.4 6.1 %collective-permute-start.6 = (f32[264,128]{1,0:T(8,128)S(1)}, f32[264,128]{1,0:T(8,128)S(1)}, u32[]{:S(2)}, u32[]{:S(2)}) collective-permute-start(f32[264,128]{1,0:T(8,128)S(1)} %get-tuple-element.126.refs_5_), channel_id=1, source_target_pairs={{1,2},{2,1},{3,4},{4,3},{5,6},{6,5},{7,8},{8,7},{9,10},{10,9},{11,... | collective-permute-start | bytes 405512 | tf_op jit(solution)/shard_map/ppermute | solution.py:798
  30.6 3.9 %collective-permute-start.7 = (f32[264,128]{1,0:T(8,128)S(1)}, f32[264,128]{1,0:T(8,128)S(1)}, u32[]{:S(2)}, u32[]{:S(2)}) collective-permute-start(f32[264,128]{1,0:T(8,128)S(1)} %get-tuple-element.132), channel_id=1, source_target_pairs={{0,1},{1,0},{2,3},{3,2},{4,5},{5,4},{6,7},{7,6},{8,9},{9,8},{10,11... | collective-permute-start | bytes 405512 | tf_op jit(solution)/shard_map/ppermute | solution.py:795
  34.8 6.4 %collective-permute-start.8 = (f32[264,128]{1,0:T(8,128)S(1)}, f32[264,128]{1,0:T(8,128)S(1)}, u32[]{:S(2)}, u32[]{:S(2)}) collective-permute-start(f32[264,128]{1,0:T(8,128)S(1)} %get-tuple-element.136.refs_5_), channel_id=1, source_target_pairs={{1,2},{2,1},{3,4},{4,3},{5,6},{6,5},{7,8},{8,7},{9,10},{10,9},{11,... | collective-permute-start | bytes 405512 | tf_op jit(solution)/shard_map/ppermute | solution.py:798
  38.0 4.2 %collective-permute-start.9 = (f32[264,128]{1,0:T(8,128)S(1)}, f32[264,128]{1,0:T(8,128)S(1)}, u32[]{:S(2)}, u32[]{:S(2)}) collective-permute-start(f32[264,128]{1,0:T(8,128)S(1)} %get-tuple-element.142), channel_id=1, source_target_pairs={{0,1},{1,0},{2,3},{3,2},{4,5},{5,4},{6,7},{7,6},{8,9},{9,8},{10,11... | collective-permute-start | bytes 405512 | tf_op jit(solution)/shard_map/ppermute | solution.py:795
  42.4 6.4 %collective-permute-start.10 = (f32[264,128]{1,0:T(8,128)S(1)}, f32[264,128]{1,0:T(8,128)S(1)}, u32[]{:S(2)}, u32[]{:S(2)}) collective-permute-start(f32[264,128]{1,0:T(8,128)S(1)} %get-tuple-element.147.refs_5_), channel_id=1, source_target_pairs={{1,2},{2,1},{3,4},{4,3},{5,6},{6,5},{7,8},{8,7},{9,10},{10,9},{11,... | collective-permute-start | bytes 405512 | tf_op jit(solution)/shard_map/ppermute | solution.py:798
  45.6 4.2 %collective-permute-start.11 = (f32[264,128]{1,0:T(8,128)S(1)}, f32[264,128]{1,0:T(8,128)S(1)}, u32[]{:S(2)}, u32[]{:S(2)}) collective-permute-start(f32[264,128]{1,0:T(8,128)S(1)} %get-tuple-element.152), channel_id=1, source_target_pairs={{0,1},{1,0},{2,3},{3,2},{4,5},{5,4},{6,7},{7,6},{8,9},{9,8},{10,11... | collective-permute-start | bytes 405512 | tf_op jit(solution)/shard_map/ppermute | solution.py:795
  50.7 12.7 %all-to-all-start = ((f32[16,1,128]{2,1,0:T(1,128)}), f32[16,1,128]{2,1,0:T(1,128)S(1)}, u32[]{:S(2)}, u32[]{:S(2)}) async-start(f32[16,1,128]{2,1,0:T(1,128)} %get-tuple-element.160), calls=%async_computation | async-start | bytes 16384 | tf_op jit(solution)/shard_map/all_to_all | solution.py:886
